TPU v7x, 32 devices: a whole 2x2x4 slice. The times are simulated.
32 devices in a mesh: member: 2 (over y), lat: 16 (over z, x, core).
Axes of the slice: x: 2, y: 2, z: 4, core: 2. Of those that a mesh axis runs over, the one named last changes fastest.
Arguments:
- grid_latent: bfloat16 [32768, 512], P(('member', 'lat')), parts along dimension 0, may hold values from -6 to 6
- mesh_latent: bfloat16 [10240, 512], P(('member', 'lat')), parts along dimension 0, may hold values from -6 to 6
- grid_cotangent: bfloat16 [32768, 512], P(('member', 'lat')), parts along dimension 0, may hold values from -6 to 6
- enc_sender: int32 [65536], P(('member', 'lat')), parts along dimension 0, may hold values from 0 to 1023
- enc_receiver: int32 [65536], P(('member', 'lat')), parts along dimension 0, may hold values from 0 to 63
- enc_feat: float32 [4, 65536], P(None, ('member', 'lat')), parts along dimension 1, may hold values from -6 to 6
- enc_count: int32 [32], P(('member', 'lat')), parts along dimension 0, may hold values from 1 to 2048, 16384 in all
- dec_sender: int32 [3, 32768], P(None, ('member', 'lat')), parts along dimension 1, may hold values from 0 to 63
- dec_feat: float32 [3, 4, 32768], P(None, None, ('member', 'lat')), parts along dimension 2, may hold values from -6 to 6
- serve_rows: int32 [32, 16, 4], P(('member', 'lat')), parts along dimension 0, may hold values from 0 to 319
- enc_proj: bfloat16 [512, 512], replicated, may hold values from -0.25 to 0.25
- node_proj: bfloat16 [512, 512], replicated, may hold values from -0.25 to 0.25
- dec_proj: bfloat16 [512, 512], replicated, may hold values from -0.25 to 0.25
- enc_feat_w: float32 [512, 4], replicated, may hold values from -3 to 3
- dec_feat_w: float32 [512, 4], replicated, may hold values from -3 to 3
Outputs:
- grid_grad: bfloat16 [32768, 512], P(('member', 'lat')), parts along dimension 0
- mesh_grad: bfloat16 [10240, 512], P(('member', 'lat')), parts along dimension 0
- enc_proj_grad: float32 [1024, 512], P(('member', 'lat')), parts along dimension 0
- node_proj_grad: float32 [1024, 512], P(('member', 'lat')), parts along dimension 0
- dec_proj_grad: float32 [1024, 512], P(('member', 'lat')), parts along dimension 0
- enc_feat_w_grad: float32 [1024, 4], P(('member', 'lat')), parts along dimension 0
- dec_feat_w_grad: float32 [1024, 4], P(('member', 'lat')), parts along dimension 0
There are 2 independent parts, one for each index of `member`. A program takes and returns all parts, laid end to end along the dimension named above; an argument that names none is the same for every part. Nothing has to cross between parts.
Inputs may be any that keep to these rules, and one draw needn't show every extreme that they name: Each band's live edges are its first enc_count entries; some band has all 2048 live. `enc_sender`: band-local grid rows. `enc_receiver`: slots of the sending band. `dec_sender`: slots of the band holding the grid point. `serve_rows`: local mesh rows of the owner; a node may fill several slots.
All inputs are finite; a program needn't handle non-finite values. No bound on the sum of `enc_count` on one device may be relied on, other than what follows from the above.
Results may differ from a plain program's by a relative error of at most 0.012.
Values may be sent and summed in bfloat16 or wider, within the bound.
No kernel may reach another device: no remote copies, remote signals or barrier semaphores. Data moves between devices by JAX's collectives and lax.ppermute only.
A program may use at most 64 MiB of HBM per device.

v0:
```python
import math

import jax
import jax.numpy as jnp
from jax import lax
from jax.sharding import PartitionSpec as P


def silu_grad(value):
    sig = jax.nn.sigmoid(value)
    return sig * (1.0 + value * (1.0 - sig))


def per_device(
    grid_latent,
    mesh_latent,
    grid_cotangent,
    enc_sender,
    enc_receiver,
    enc_feat,
    enc_count,
    dec_sender,
    dec_feat,
    serve_rows,
    enc_proj,
    node_proj,
    dec_proj,
    enc_feat_w,
    dec_feat_w,
):
    highest = lax.Precision.HIGHEST
    owners_count = lax.axis_size("lat")
    serve_flat = serve_rows.reshape(-1)
    slot_total = serve_flat.shape[0]
    per_owner = slot_total // owners_count
    mesh_rows = mesh_latent.shape[0]
    grid_rows = grid_latent.shape[0]
    width = grid_latent.shape[1]
    edge_slots = enc_sender.shape[0]
    edge_block = math.gcd(edge_slots, 512)
    grid_block = math.gcd(grid_rows, 512)
    live_count = enc_count[0]
    slot_ids = lax.iota(jnp.int32, slot_total)[:, None]
    row_ids = lax.iota(jnp.int32, grid_rows)[:, None]

    def to_window(rows):
        outgoing = jnp.take(rows, serve_flat, axis=0).reshape(owners_count, per_owner, width)
        arrived = lax.all_to_all(outgoing, "lat", split_axis=0, concat_axis=0, tiled=True)
        return arrived.reshape(slot_total, width)

    def to_owners(partial_value):
        arrived = lax.all_to_all(
            partial_value.reshape(owners_count, per_owner, width),
            "lat",
            split_axis=0,
            concat_axis=0,
            tiled=True,
        )
        return jax.ops.segment_sum(
            arrived.reshape(slot_total, width), serve_flat, num_segments=mesh_rows
        )

    px = jnp.dot(grid_latent, enc_proj, preferred_element_type=jnp.float32).astype(jnp.bfloat16)

    def enc_block(start):
        senders = lax.dynamic_slice_in_dim(enc_sender, start, edge_block)
        receivers = lax.dynamic_slice_in_dim(enc_receiver, start, edge_block)
        feats = lax.dynamic_slice_in_dim(enc_feat, start, edge_block, 1)
        pre = jnp.take(px, senders, axis=0).astype(jnp.float32) + jnp.einsum(
            "fb,lf->bl", feats, enc_feat_w, precision=highest
        )
        live = (lax.iota(jnp.int32, edge_block) + start < live_count)[:, None]
        onehot = (receivers[None, :] == slot_ids).astype(jnp.bfloat16)
        return (pre, live, onehot, senders, feats)

    block_steps = edge_slots // edge_block

    def enc_forward(index, partial_value):
        pre, live, onehot, senders, feats = enc_block(index * edge_block)
        message = jnp.where(live, jax.nn.silu(pre), 0.0).astype(jnp.bfloat16)
        return partial_value + jnp.dot(onehot, message, preferred_element_type=jnp.float32)

    enc_partial = lax.fori_loop(
        0, block_steps, enc_forward, jnp.zeros((slot_total, width), jnp.float32)
    )
    agg = to_owners(enc_partial)
    act = jax.nn.silu(agg).astype(jnp.bfloat16)
    hmesh = (
        mesh_latent.astype(jnp.float32)
        + jnp.dot(act, node_proj, preferred_element_type=jnp.float32)
    ).astype(jnp.bfloat16)
    proj_window = to_window(
        jnp.dot(hmesh, dec_proj, preferred_element_type=jnp.float32).astype(jnp.bfloat16)
    )

    def dec_backward(index, carry):
        dproj, dfw = carry
        start = index * grid_block
        cot = lax.dynamic_slice_in_dim(grid_cotangent, start, grid_block).astype(jnp.float32)
        for k in range(3):
            senders = lax.dynamic_slice_in_dim(dec_sender[k], start, grid_block)
            feats = lax.dynamic_slice_in_dim(dec_feat[k], start, grid_block, 1)
            pre = jnp.take(proj_window, senders, axis=0).astype(jnp.float32) + jnp.einsum(
                "fg,lf->gl", feats, dec_feat_w, precision=highest
            )
            grad_half = (cot * silu_grad(pre)).astype(jnp.bfloat16)
            slot_hot = (senders[None, :] == slot_ids).astype(jnp.bfloat16)
            dproj = dproj + jnp.dot(slot_hot, grad_half, preferred_element_type=jnp.float32)
            dfw = dfw + jnp.einsum(
                "gl,fg->lf", grad_half.astype(jnp.float32), feats, precision=highest
            )
        return (dproj, dfw)

    start_carry = (
        jnp.zeros((slot_total, width), jnp.float32),
        jnp.zeros((width, dec_feat_w.shape[1]), jnp.float32),
    )
    dproj_window, dec_fw_part = lax.fori_loop(0, grid_rows // grid_block, dec_backward, start_carry)
    dec_weight = dec_proj.astype(jnp.float32)
    dproj = to_owners(dproj_window)
    dhmesh = jnp.dot(dproj, dec_weight.T, precision=highest)
    dec_proj_part = jnp.dot(hmesh.astype(jnp.float32).T, dproj, precision=highest)
    mesh_grad = dhmesh.astype(jnp.bfloat16)
    node_proj_part = jnp.dot(act.T, mesh_grad, preferred_element_type=jnp.float32)
    dagg = (
        jnp.dot(mesh_grad, node_proj.T, preferred_element_type=jnp.float32) * silu_grad(agg)
    ).astype(jnp.bfloat16)
    dagg_window = to_window(dagg)

    def enc_backward(index, carry):
        dpx, dew = carry
        pre, live, onehot, senders, feats = enc_block(index * edge_block)
        upstream = jnp.einsum("wb,wl->bl", onehot, dagg_window, preferred_element_type=jnp.float32)
        grad_half = jnp.where(live, upstream * silu_grad(pre), 0.0).astype(jnp.bfloat16)
        row_hot = (senders[None, :] == row_ids).astype(jnp.bfloat16)
        dpx = dpx + jnp.dot(row_hot, grad_half, preferred_element_type=jnp.float32)
        dew = dew + jnp.einsum("bl,fb->lf", grad_half.astype(jnp.float32), feats, precision=highest)
        return (dpx, dew)

    start_back = (
        jnp.zeros((grid_rows, width), jnp.float32),
        jnp.zeros((width, enc_feat_w.shape[1]), jnp.float32),
    )
    dpx_sum, enc_fw_part = lax.fori_loop(0, block_steps, enc_backward, start_back)
    dpx = dpx_sum.astype(jnp.bfloat16)
    enc_proj_part = jnp.dot(grid_latent.T, dpx, preferred_element_type=jnp.float32)
    grid_grad = (
        grid_cotangent.astype(jnp.float32)
        + jnp.dot(dpx, enc_proj.T, preferred_element_type=jnp.float32)
    ).astype(jnp.bfloat16)
    enc_proj_grad, node_proj_grad, dec_proj_grad, enc_feat_w_grad, dec_feat_w_grad = (
        lax.psum_scatter(enc_proj_part, "lat", scatter_dimension=0, tiled=True),
        lax.psum_scatter(node_proj_part, "lat", scatter_dimension=0, tiled=True),
        lax.psum_scatter(dec_proj_part, "lat", scatter_dimension=0, tiled=True),
        lax.psum_scatter(enc_fw_part, "lat", scatter_dimension=0, tiled=True),
        lax.psum_scatter(dec_fw_part, "lat", scatter_dimension=0, tiled=True),
    )
    return (
        grid_grad,
        mesh_grad,
        enc_proj_grad,
        node_proj_grad,
        dec_proj_grad,
        enc_feat_w_grad,
        dec_feat_w_grad,
    )


def solution(mesh):
    placed = (
        P(("member", "lat"), None),
        P(("member", "lat"), None),
        P(("member", "lat"), None),
        P(("member", "lat")),
        P(("member", "lat")),
        P(None, ("member", "lat")),
        P(("member", "lat")),
        P(None, ("member", "lat")),
        P(None, None, ("member", "lat")),
        P(("member", "lat"), None, None),
        P(),
        P(),
        P(),
        P(),
        P(),
    )
    return jax.shard_map(
        per_device,
        mesh=mesh,
        in_specs=placed,
        out_specs=(
            P(("member", "lat"), None),
            P(("member", "lat"), None),
            P(("member", "lat"), None),
            P(("member", "lat"), None),
            P(("member", "lat"), None),
            P(("member", "lat"), None),
            P(("member", "lat"), None),
        ),
        check_vma=False,
    )
```

profile of v0, /device:TPU:0, one launch (start us, length us, event | category | flops | bytes accessed | tf_op | source)
XLA Modules:
  0.0 422.8 jit_solution(5324247441549845793)
XLA Ops:
  8.4 1.7 convolution_convert_fusion
  10.2 17.5 %while.47 = (s32[]{:T(128)}, f32[64,512]{1,0:T(8,128)S(1)}, s32[2048]{0:T(1024)S(1)}, s32[]{:T(128)}, s32[2048]{0:T(1024)S(1)}, /*index=5*/bf16[1024,512]{1,0:T(...) while((s32[]{:T(128)}, f32[64,512]{1,0:T(8,128)S(1)}, ...), condition=%wide.region_1.3_spmd.clone, body=%wide.region_0.2_spmd.clone.sunk | while | flops 48600072 | bytes 2920649 | solution.py:83
  11.0 2.0 gather_fusion
  15.4 2.0 gather_fusion
  19.8 2.0 gather_fusion
  24.2 2.0 gather_fusion
  28.4 7.4 %all-to-all-start = ((f32[16,4,512]{2,1,0:T(4,128)}), f32[16,4,512]{2,1,0:T(4,128)S(1)}, u32[]{:S(2)}, u32[]{:S(2)}) async-start(f32[16,4,512]{2,1,0:T(4,128)} %reshape.90), calls=%async_computation | async-start | bytes 262144 | tf_op jit(solution)/shard_map/all_to_all | solution.py:52
  36.1 7.7 %all-to-all-done = f32[16,4,512]{2,1,0:T(4,128)S(1)} async-done(((f32[16,4,512]{2,1,0:T(4,128)}), f32[16,4,512]{2,1,0:T(4,128)S(1)}, u32[]{:S(2)}, u32[]{:S(2)}) %all-to-all-start) | async-done | bytes 131104 | tf_op jit(solution)/shard_map/all_to_all | solution.py:52
  45.8 1.5 fusion.44
  49.8 3.5 all-to-all-start.1
  53.3 6.8 %all-to-all-done.1 = bf16[16,4,512]{2,1,0:T(4,128)(2,1)S(1)} async-done(((bf16[16,4,512]{2,1,0:T(4,128)(2,1)}), bf16[16,4,512]{2,1,0:T(4,128)(2,1)S(1)}, u32[]{:S(2)}, u32[]{:S(2)}) %all-to-all-start.1) | async-done | bytes 65568 | tf_op jit(solution)/shard_map/all_to_all | solution.py:48
  60.2 33.9 %while.49 = (s32[]{:T(128)}, f32[64,512]{1,0:T(8,128)S(1)}, f32[512,4]{0,1:T(4,128)S(1)}, s32[3,1024]{1,0:T(4,128)S(1)}, bf16[1024,512]{1,0:T(8,128)(2,1)}, /*in...) while((s32[]{:T(128)}, f32[64,512]{1,0:T(8,128)S(1)}, ...), condition=%wide.region_4.8_spmd.clone.clone, body=%wide.region_3.7_spmd.clone.clone.sunk | while | flops 186638848 | bytes 12142822 | solution.py:118
  60.4 2.0 gather_fusion.3
  62.4 2.5 fusion.143
  64.9 2.6 gather_fusion.4
  67.5 2.7 fusion.144
  70.2 2.6 gather_fusion.2
  72.9 2.7 fusion.142
  77.3 2.0 gather_fusion.3
  79.3 2.5 fusion.143
  81.9 2.6 gather_fusion.4
  84.5 2.7 fusion.144
  87.2 2.6 gather_fusion.2
  89.8 2.7 fusion.142
  94.2 10.7 %all_to_all.20 = f32[16,4,512]{2,1,0:T(4,128)S(1)} all-to-all(f32[16,4,512]{2,1,0:T(4,128)S(1)} %reshape.95), channel_id=1, replica_groups=mesh['member'=2,'lat'=16] {'lat'}, dimensions={0} | all-to-all | bytes 262144 | tf_op jit(solution)/shard_map/all_to_all | solution.py:52
  106.2 1.8 convolution_convert_fusion.1
  108.6 1.7 fusion.45
  111.9 3.5 all-to-all-start.3
  116.4 5.9 %all-to-all-done.3 = bf16[16,4,512]{2,1,0:T(4,128)(2,1)S(1)} async-done(((bf16[16,4,512]{2,1,0:T(4,128)(2,1)}), bf16[16,4,512]{2,1,0:T(4,128)(2,1)S(1)}, u32[]{:S(2)}, u32[]{:S(2)}) %all-to-all-start.3) | async-done | bytes 65568 | tf_op jit(solution)/shard_map/all_to_all | solution.py:48
  122.3 31.5 %while.48 = (s32[]{:T(128)}, f32[1024,512]{1,0:T(8,128)}, f32[512,4]{0,1:T(4,128)S(1)}, s32[2048]{0:T(1024)S(1)}, s32[]{:T(128)}, /*index=5*/s32[2048]{0:T(1024)...) while((s32[]{:T(128)}, f32[1024,512]{1,0:T(8,128)}, ...), condition=%wide.region_7.11_spmd.clone, body=%wide.region_6.10_spmd.clone.sunk | while | flops 600615424 | bytes 26347796 | solution.py:144
  123.2 2.0 gather_fusion.1
  128.9 1.3 copy-done.2
  131.0 2.0 gather_fusion.1
  136.8 1.3 copy-done.2
  138.9 2.0 gather_fusion.1
  146.8 2.0 gather_fusion.1
  152.5 1.3 copy-done.2
  154.8 3.0 fusion.55
  157.9 1.5 fusion.52
  159.5 2.3 convolution_bitcast_fusion
  163.2 13.2 %reduce-scatter.20.cloned.1.call-done = f32[32,4]{1,0:T(8,128)} async-done(((f32[512,4]{1,0:T(8,128)}), f32[32,4]{1,0:T(8,128)}) %reduce-scatter.20.cloned.1.call-update) | async-done | bytes 528
  176.4 1.4 copy.33
  177.8 3.4 add_convert_fusion
  181.2 53.2 %reduce-scatter.18.cloned.1.call-done = f32[32,4]{1,0:T(8,128)} async-done(((f32[512,4]{1,0:T(8,128)}), f32[32,4]{1,0:T(8,128)}) %reduce-scatter.18.cloned.1.call-update) | async-done | bytes 528
  234.3 1.4 copy.31
  235.7 59.2 %reduce-scatter.14.cloned.1.call-done = f32[32,512]{1,0:T(8,128)} async-done(((f32[512,512]{1,0:T(8,128)}), f32[32,512]{1,0:T(8,128)}) %reduce-scatter.14.cloned.1.call-update) | async-done | bytes 65552 | tf_op jit(solution)/shard_map/reduce_scatter | solution.py:154
  294.9 60.9 %reduce-scatter.12.cloned.1.call-done = f32[32,512]{1,0:T(8,128)} async-done(((f32[512,512]{1,0:T(8,128)}), f32[32,512]{1,0:T(8,128)}) %reduce-scatter.12.cloned.1.call-update) | async-done | bytes 65552 | tf_op jit(solution)/shard_map/reduce_scatter | solution.py:153
  355.8 60.4 %reduce-scatter.16.cloned.1.call-done = f32[32,512]{1,0:T(8,128)} async-done(((f32[512,512]{1,0:T(8,128)}), f32[32,512]{1,0:T(8,128)}) %reduce-scatter.16.cloned.1.call-update) | async-done | bytes 65552
  (185 shorter events, 45.8 us)
Async XLA Ops:
  7.2 1.2 copy-start
  7.2 3.0 copy-start.13
  7.2 3.0 copy-start.12
  7.2 3.0 copy-start.15
  7.2 3.0 copy-start.14
  10.2 25.6 %copy-start.19 = (s32[1,16,4]{1,2,0:T(4,128)S(1)}, s32[1,16,4]{1,2,0:T(4,128)}, u32[]{:S(2)}) copy-start(s32[1,16,4]{1,2,0:T(4,128)} %param.36) | copy-start | bytes 772
  10.2 35.6 %copy-start.21 = (bf16[320,512]{1,0:T(8,128)(2,1)S(1)}, bf16[320,512]{1,0:T(8,128)(2,1)}, u32[]{:S(2)}) copy-start(bf16[320,512]{1,0:T(8,128)(2,1)} %param.28) | copy-start | bytes 983044
  28.4 15.3 %all-to-all-start = ((f32[16,4,512]{2,1,0:T(4,128)}), f32[16,4,512]{2,1,0:T(4,128)S(1)}, u32[]{:S(2)}, u32[]{:S(2)}) async-start(f32[16,4,512]{2,1,0:T(4,128)} %reshape.90), calls=%async_computation | async-start | bytes 262144 | tf_op jit(solution)/shard_map/all_to_all | solution.py:52
  36.0 11.2 %copy-start.20 = (s32[64]{0:T(128)}, s32[64]{0:T(128)S(1)}, u32[]{:S(2)}) copy-start(s32[64]{0:T(128)S(1)} %reshape.165) | copy-start | bytes 772
  36.0 12.3 %copy-start.16 = (s32[1024]{0:T(1024)}, s32[1024]{0:T(1024)S(1)}, u32[]{:S(2)}) copy-start(s32[1024]{0:T(1024)S(1)} %pad_clamp_fusion.5) | copy-start | bytes 12292
  36.1 13.0 %copy-start.17 = (pred[64]{0:T(512)(128)(4,1)}, pred[64]{0:T(512)(128)(4,1)S(1)}, u32[]{:S(2)}) copy-start(pred[64]{0:T(512)(128)(4,1)S(1)} %compare_and_fusion.5) | copy-start | bytes 196
  44.9 0.8 copy-start.7
  45.8 2.2 copy-start.3
  47.2 0.7 copy-start.4
  48.0 12.2 %copy-start.5 = (f32[3,4,1024]{2,1,0:T(4,128)S(1)}, f32[3,4,1024]{2,1,0:T(4,128)}, u32[]{:S(2)}) copy-start(f32[3,4,1024]{2,1,0:T(4,128)} %param.35) | copy-start | bytes 147460
  48.0 12.2 %copy-start.11 = (s32[3,1024]{1,0:T(4,128)S(1)}, s32[3,1024]{1,0:T(4,128)}, u32[]{:S(2)}) copy-start(s32[3,1024]{1,0:T(4,128)} %param.34) | copy-start | bytes 36868
  49.8 10.4 %all-to-all-start.1 = ((bf16[16,4,512]{2,1,0:T(4,128)(2,1)}), bf16[16,4,512]{2,1,0:T(4,128)(2,1)S(1)}, u32[]{:S(2)}, u32[]{:S(2)}) async-start(bf16[16,4,512]{2,1,0:T(4,128)(2,1)} %reshape.93), calls=%async_computation.1 | async-start | bytes 131072 | tf_op jit(solution)/shard_map/all_to_all | solution.py:48
  70.2 2.7 copy-start.22
  87.2 2.7 copy-start.22
  107.9 0.7 copy-start.9
  108.6 2.5 copy-start.18
  111.9 10.4 %all-to-all-start.3 = ((bf16[16,4,512]{2,1,0:T(4,128)(2,1)}), bf16[16,4,512]{2,1,0:T(4,128)(2,1)S(1)}, u32[]{:S(2)}, u32[]{:S(2)}) async-start(bf16[16,4,512]{2,1,0:T(4,128)(2,1)} %reshape.97), calls=%async_computation.3 | async-start | bytes 131072 | tf_op jit(solution)/shard_map/all_to_all | solution.py:48
  115.4 61.0 %reduce-scatter.20.cloned.1.call-start = ((), (), s32[]{:S(2)}) async-start(), calls=%async_computation.13 | async-start | bytes 278528
  116.4 117.9 %reduce-scatter.18.cloned.1.call-start = ((), (), s32[]{:S(2)}) async-start(), calls=%async_computation.12 | async-start | bytes 278528
  126.2 1.6 copy-start.1
  128.9 1.3 copy-start.2
  134.1 1.6 copy-start.1
  136.8 1.3 copy-start.2
  142.0 1.6 copy-start.1
  144.6 1.3 copy-start.2
  149.9 1.6 copy-start.1
  152.5 1.3 copy-start.2
  153.9 4.1 copy-start.8
  153.9 4.1 copy-start.10
  154.7 140.2 %reduce-scatter.14.cloned.1.call-start = ((), (), s32[]{:S(2)}) async-start(), calls=%async_computation.10 | async-start | bytes 1114112 | tf_op jit(solution)/shard_map/reduce_scatter | solution.py:154
  157.9 198.0 %reduce-scatter.12.cloned.1.call-start = ((), (), s32[]{:S(2)}) async-start(), calls=%async_computation.9 | async-start | bytes 1114112 | tf_op jit(solution)/shard_map/reduce_scatter | solution.py:153
  159.5 256.8 %reduce-scatter.16.cloned.1.call-start = ((), (), s32[]{:S(2)}) async-start(), calls=%async_computation.11 | async-start | bytes 1114112
  161.9 15.9 %copy-start.6 = (bf16[1024,512]{1,0:T(8,128)(2,1)S(1)}, bf16[1024,512]{1,0:T(8,128)(2,1)}, u32[]{:S(2)}) copy-start(bf16[1024,512]{1,0:T(8,128)(2,1)} %get-tuple-element.1052) | copy-start | bytes 3145732
Sparse Core Ops, SparseCore 0:
  119.8 56.5 reduce-scatter.19
  179.9 54.3 reduce-scatter.17
  238.5 56.3 reduce-scatter.13
  299.4 56.3 reduce-scatter.11
  359.9 56.3 reduce-scatter.15
where the time goes:
time: 424 us; the launch traced here: 423 us
  waiting for transfers between devices  267 us (63%)
  matrix products  54.5 us (13%)
  local copies, waits for them, and re-layouts  52.2 us (12%)
  starting transfers between devices  14.6 us (3%)
  between operations  14.2 us (3%)
  blocking collectives  10.7 us (3%)
  other arithmetic  8.54 us (2%)
    unnamed x8, waiting for transfers between devices  127 us
    reduce_scatter x1, waiting for transfers between devices, per_device(): lax.psum_scatter(node_proj_part, 'lat', scatter_dimension=0, tiled=True)  60.9 us
    reduce_scatter x1, waiting for transfers between devices, per_device(): lax.psum_scatter(dec_proj_part, 'lat', scatter_dimension=0, tiled=True)  59.2 us
    gather x8, local copies, waits for them, and re-layouts, enc_block(): jnp.take(px, senders, axis=0).astype(jnp.float32)  15.8 us
    dot_general x6, matrix products, dec_backward(): jnp.einsum('fg,lf->gl', feats, dec_feat_w, precision=highest)  15.7 us
    gather x6, local copies, waits for them, and re-layouts, dec_backward(): jnp.take(proj_window, senders, axis=0).astype(jnp.float32)  14.5 us
    all_to_all x2, waiting for transfers between devices, to_window(): lax.all_to_all(outgoing, 'lat', split_axis=0, concat_axis=0, tiled=True)  12.7 us
    all_to_all x1, blocking collectives, to_owners(): lax.all_to_all(partial_value.reshape(owners_count, per_owner, width), 'la...  10.7 us
  transfers between devices with their start and end apart: 8, of which 8 were waited for; matrix products, arithmetic and copies ran while one was open for 9% of the time, Pallas kernels for 0%

commit v1 on v0

--- a/solution.py
+++ b/solution.py
@@ -3,7 +3,18 @@
 import jax
 import jax.numpy as jnp
 from jax import lax
+from jax.experimental import pallas as pl
+from jax.experimental.pallas import tpu as pltpu
 from jax.sharding import PartitionSpec as P
+
+BF = jnp.bfloat16
+F32 = jnp.float32
+HI = lax.Precision.HIGHEST
+MIB = 1 << 20
+TAIL = 16
+NN = (((1,), (0,)), ((), ()))
+NT = (((1,), (1,)), ((), ()))
+TN = (((0,), (0,)), ((), ()))
 
 
 def silu_grad(value):
@@ -11,7 +22,7 @@
     return sig * (1.0 + value * (1.0 - sig))
 
 
-def per_device(
+def owner_plan(
     grid_latent,
     mesh_latent,
     grid_cotangent,
@@ -166,6 +177,434 @@
     )
 
 
+def mm(a, b, dims=NN, precision=None):
+    return lax.dot_general(a, b, dims, precision=precision, preferred_element_type=F32)
+
+
+def iota(shape, dim):
+    return lax.broadcasted_iota(jnp.int32, shape, dim)
+
+
+def sigmoid(value):
+    return 0.5 * jnp.tanh(0.5 * value) + 0.5
+
+
+def hot(mask):
+    return jnp.where(mask, 1.0, 0.0).astype(BF)
+
+
+def split3(value):
+    high = value.astype(BF).astype(F32)
+    rest = value - high
+    middle = rest.astype(BF).astype(F32)
+    return high, middle, rest - middle
+
+
+def stack_terms(value, order):
+    feats = value.shape[0]
+    rows = -(-6 * feats // 16) * 16
+    pick = (iota((rows, feats), 0) % feats == iota((rows, feats), 1)).astype(F32)
+    spread = mm(pick, value, precision=HI)
+    parts = split3(spread)
+    group = iota(spread.shape, 0) // feats
+    out = jnp.zeros_like(spread)
+    for index, which in enumerate(order):
+        out = jnp.where(group == index, parts[which], out)
+    return out.astype(BF)
+
+
+FEAT_ORDER = (0, 0, 1, 1, 2, 0)
+WEIGHT_ORDER = (0, 1, 0, 1, 0, 2)
+
+
+def weight_rows(weight):
+    feats = weight.shape[1]
+    eye = (iota((8, feats), 0) == iota((8, feats), 1)).astype(F32)
+    return stack_terms(mm(eye, weight, NT, HI)[:feats], WEIGHT_ORDER)
+
+
+def feature_grad(terms, feats):
+    pick = iota((8, terms.shape[0]), 1)
+    row = iota((8, terms.shape[0]), 0)
+    want = (pick % feats == row) & (row < feats)
+    want = want & ((pick // feats == 0) | (pick // feats == 2) | (pick // feats == 4))
+    return mm(want.astype(F32), terms, precision=HI)
+
+
+def encoder_kernel(count, latent, weight, send, receive, feat, feat_w, extra, message, slope, px):
+    edges = send.shape[1]
+    grid_rows = latent.shape[0]
+    slots = message.shape[1] - TAIL
+    block = math.gcd(edges, 512)
+    px[...] = mm(latent[...], weight[...]).astype(BF)
+    w_rows = weight_rows(feat_w[...])
+    total = jnp.zeros((slots, latent.shape[1]), F32)
+    for start in range(0, edges, block):
+        part = slice(start, start + block)
+        ids = jnp.broadcast_to(send[:, part].astype(F32), (128, block)).T
+        picks = [
+            hot(ids == (iota((block, 128), 1) + base).astype(F32))
+            for base in range(0, grid_rows, 128)
+        ]
+        pre = mm(jnp.concatenate(picks, 1), px[...])
+        pre = pre + mm(stack_terms(feat[:, part], FEAT_ORDER), w_rows, TN)
+        sig = sigmoid(pre)
+        silu = pre * sig
+        slope[part, :] = (sig + silu * (1.0 - sig)).astype(BF)
+        live = iota((1, block), 1) + start < count[0]
+        slot = jnp.where(live, receive[:, part], -1)
+        to_slot = hot(iota((slots, block), 0) == slot)
+        total = total + mm(to_slot, silu.astype(BF))
+    half = total.astype(BF)
+    for chip in range(message.shape[0]):
+        message[chip, :slots, :] = half
+        message[chip, slots:, :] = extra[chip]
+
+
+def gathered_rows(piece, chips, rows, core, cap, shape, dim):
+    index = iota(shape, dim)
+    chip = lax.div(index, rows)
+    slot = index - chip * rows
+    band = 2 * chip + jnp.where(piece == 0, core, 1 - core)
+    return band, slot, lax.div(slot, cap)
+
+
+def slot_matches(first, second, me, cap, mesh_rows):
+    chips, rows = first.shape[0], first.shape[1]
+    span = chips * rows
+    slots = rows - TAIL
+    owners = 2 * chips
+    core = lax.rem(me, 2)
+    flat = [ref[...].reshape(span, -1) for ref in (first, second)]
+    table = jnp.zeros((owners, 256), F32)
+    for piece in range(2):
+        shape = (owners, span)
+        at = (iota(shape, 0) - piece * chips) * rows + slots + 2 * cap
+        table = table + mm(hot(iota(shape, 1) == at), flat[piece][:, :256])
+    digits = jnp.concatenate([table[:, :128], table[:, 128:]], 0).astype(BF)
+    half = iota((slots, 2 * owners), 1)
+    holder = half % owners
+    holder = 2 * (holder % chips) + jnp.where(holder < chips, core, 1 - core)
+    wanted = holder == lax.div(iota((slots, 2 * owners), 0), cap)
+    mine = 256.0 * mm(hot(wanted & (half < owners)), digits) + mm(hot(wanted & (half >= owners)), digits)
+    lane = cap * me + iota((slots, 128), 0) % cap
+    own_key = jnp.sum(jnp.where(iota((slots, 128), 1) == lane, mine, 0.0), 1, keepdims=True)
+    own_key = own_key + (lax.div(iota((slots, 1), 0), cap) * mesh_rows).astype(F32)
+    keys, same, served = [], [], []
+    for piece in range(2):
+        band, slot, owner = gathered_rows(piece, chips, rows, core, cap, (1, span), 1)
+        spread = mm(digits, hot(iota((128, span), 0) == cap * band + slot % cap))
+        value = 256.0 * spread[:owners] + spread[owners:]
+        holder = iota((owners, 1), 0)
+        holder = 2 * (holder % chips) + jnp.where(holder < chips, core, 1 - core)
+        value = jnp.sum(jnp.where(holder == owner, value, 0.0), 0, keepdims=True)
+        key = jnp.where(slot < slots, value + (owner * mesh_rows).astype(F32), -1.0)
+        keys.append(key)
+        same.append(hot(key == own_key))
+        window = iota((slots, 1), 0)
+        row = slots + cap * core + window % cap
+        served.append(hot((band == lax.div(window, cap)) & (slot == row)))
+    return flat, keys, same, served
+
+
+def decoder_body(proj, send, feat, feat_w, cotangent):
+    slots = proj.shape[0]
+    grid_rows = cotangent.shape[0]
+    block = math.gcd(grid_rows, 512)
+    table = jnp.concatenate([proj, weight_rows(feat_w[...])], 0)
+    total = jnp.zeros((table.shape[0], proj.shape[1]), F32)
+    for start in range(0, grid_rows, block):
+        part = slice(start, start + block)
+        cot = cotangent[part, :].astype(F32)
+        for k in range(3):
+            to_slot = hot(iota((slots, block), 0) == send[k : k + 1, part])
+            pick = jnp.concatenate([to_slot, stack_terms(feat[k, :, part], FEAT_ORDER)], 0)
+            pre = mm(pick, table, TN)
+            sig = sigmoid(pre)
+            slope = sig + pre * sig * (1.0 - sig)
+            total = total + mm(pick, (cot * slope).astype(BF))
+    return total
+
+
+def decoder_kernel(
+    cap, mesh_rows, place, first, second, node_w, dec_w, send, feat, feat_w, cotangent, extra,
+    message, keys_out, same_out, slope_out,
+):
+    slots = first.shape[1] - TAIL
+    flat, keys, same, served = slot_matches(first, second, place[0], cap, mesh_rows)
+    both = jnp.zeros((2 * slots, first.shape[2]), F32)
+    for piece in range(2):
+        keys_out[piece : piece + 1, :] = keys[piece]
+        same_out[piece] = same[piece]
+        both = both + mm(jnp.concatenate([same[piece], served[piece]], 0), flat[piece])
+    agg, latent = both[:slots], both[slots:]
+    sig = sigmoid(agg)
+    silu = agg * sig
+    slope_out[...] = sig + silu * (1.0 - sig)
+    hmesh = (latent + mm(silu.astype(BF), node_w[...])).astype(BF)
+    proj = mm(hmesh, dec_w[...]).astype(BF)
+    total = decoder_body(proj, send, feat, feat_w, cotangent)
+    feats = feat_w.shape[1]
+    half = total[:slots].astype(BF)
+    grad = feature_grad(total[slots:], feats).astype(BF)
+    for chip in range(message.shape[0]):
+        message[chip, :slots, :] = half
+        message[chip, slots:, :] = jnp.concatenate([grad, extra[chip]], 0)
+
+
+def backward_kernel(
+    place, count, first, second, same, agg_slope, node_w, dec_w, send, receive, feat, slope, latent,
+    dpx_out, keep, give, hots, grads, part,
+):
+    slots = same.shape[1]
+    edges = send.shape[1]
+    grid_rows, width = latent.shape
+    feats = feat.shape[0]
+    core = lax.rem(place[0], 2)
+    dproj = mm(same[0], first[...].reshape(-1, width)) + mm(same[1], second[...].reshape(-1, width))
+    high = dproj.astype(BF)
+    low = (dproj - high.astype(F32)).astype(BF)
+    dhmesh = mm(jnp.concatenate([high, low], 0), dec_w[...], NT)
+    mesh_grad = (dhmesh[:slots] + dhmesh[slots:]).astype(BF)
+    dagg = (mm(mesh_grad, node_w[...], NT) * agg_slope[...]).astype(BF)
+    block = math.gcd(edges, 512)
+    for start in range(0, edges, block):
+        cut = slice(start, start + block)
+        live = iota((1, block), 1) + start < count[0]
+        slot = jnp.where(live, receive[:, cut], -1)
+        upstream = mm(hot(iota((slots, block), 0) == slot), dagg, TN)
+        grads[cut, :] = (upstream * slope[cut, :].astype(F32)).astype(BF)
+        hots[:grid_rows, cut] = hot(iota((grid_rows, block), 0) == send[:, cut])
+        hots[grid_rows:, cut] = stack_terms(feat[:, cut], FEAT_ORDER)
+    step = math.gcd(grid_rows, 256)
+    for start in range(0, grid_rows, step):
+        cut = slice(start, start + step)
+        dpx_out[cut, :] = mm(hots[cut, :], grads[...]).astype(BF)
+    terms = mm(hots[grid_rows:, :], grads[...])
+    pick = iota((128, terms.shape[0]), 1)
+    row = iota((128, terms.shape[0]), 0)
+    want = (pick % feats == row) & (row < feats)
+    group = lax.div(pick, feats)
+    want = want & ((group == 0) | (group == 2) | (group == 4))
+    part[:, width:] = mm(want.astype(F32), terms, precision=HI).T
+    part[:, :width] = mm(latent[...], dpx_out[...], TN)
+    chips, rows = keep.shape[0], keep.shape[1]
+    for chip in range(chips):
+        keep[chip] = part[pl.ds((2 * chip + core) * rows, rows), :]
+        give[chip] = part[pl.ds((2 * chip + 1 - core) * rows, rows), :].astype(BF)
+
+
+def weight_kernel(
+    cap, mesh_rows, feats, place, first, second, first_back, second_back, keys, node_w, dec_w,
+    mesh_out, dec_out, node_out, feat_out,
+):
+    chips, rows, width = first.shape
+    slots = rows - TAIL
+    span = chips * rows
+    owners = 2 * chips
+    me = place[0]
+    core = lax.rem(me, 2)
+    block = width // owners
+    forward = jnp.concatenate([first[...].reshape(span, width), second[...].reshape(span, width)], 0)
+    back = jnp.concatenate([first_back[...].reshape(span, width), second_back[...].reshape(span, width)], 0)
+    key = jnp.concatenate([keys[0:1, :], keys[1:2, :]], 1)
+    down = jnp.broadcast_to(key, (128, 2 * span)).T
+    down = jnp.where(down < 0.0, -2.0, down)
+    same = jnp.concatenate([hot(down == key[:, base : base + 128]) for base in range(0, 2 * span, 128)], 1)
+    agg = mm(same, forward)
+    act = (agg * sigmoid(agg)).astype(BF)
+    shape = (width, 128)
+    mine = hot((iota(shape, 0) == block * me + iota(shape, 1)) & (iota(shape, 1) < block))
+    node_cols = mm(node_w[...], mine).astype(BF)
+    both = mm(act, jnp.concatenate([node_cols, mine], 1))
+    pieces = [gathered_rows(piece, chips, rows, core, cap, (span, 1), 0) for piece in range(2)]
+    band, slot, owner = [jnp.concatenate([a, b], 0) for a, b in zip(*pieces)]
+    number = cap * band + slot % cap
+    source = jnp.where(lax.rem(owner, 2) == core, 0, chips) + lax.div(owner, 2)
+    at = jnp.where(slot < slots, source * TAIL + TAIL - 2 * cap + lax.div(number, chips), -1)
+    tails = jnp.concatenate(
+        [ref[chip, slots:, :] for ref in (first_back, second_back) for chip in range(chips)], 0
+    )
+    shape = (2 * span, tails.shape[0])
+    wide = mm(hot(iota(shape, 1) == at), tails)
+    shape = (2 * span, width)
+    wide = jnp.where(lax.div(iota(shape, 1), 2 * block) == lax.rem(number, chips), wide, 0.0).astype(BF)
+    shape = (width, 128)
+    fold = hot((iota(shape, 0) % (2 * block) == block * core + iota(shape, 1)) & (iota(shape, 1) < block))
+    hmesh = (both[:, :128] + mm(wide, fold)).astype(BF)
+    left = jnp.concatenate([hmesh, both[:, 128:].astype(BF)], 1)
+    sums = mm(left, back, TN)
+    dec_out[...] = sums[:block]
+    lead = sums[128 : 128 + block]
+    high = lead.astype(BF)
+    low = (lead - high.astype(F32)).astype(BF)
+    node_out[...] = mm(high, dec_w[...], NT) + mm(low, dec_w[...], NT)
+    shape = (8, 2 * span)
+    index = lax.rem(iota(shape, 1), rows)
+    feat_out[...] = mm(hot((index == slots + iota(shape, 0)) & (iota(shape, 0) < feats)), back)
+    mesh = mesh_out.shape[0]
+    shape = (mesh, 2 * span)
+    own = (me * mesh_rows + iota(shape, 0)).astype(F32)
+    dproj = mm(hot(own == key), back)
+    high = dproj.astype(BF)
+    low = (dproj - high.astype(F32)).astype(BF)
+    mesh_out[...] = (mm(high, dec_w[...], NT) + mm(low, dec_w[...], NT)).astype(BF)
+
+
+SMEM = pl.BlockSpec(memory_space=pltpu.SMEM)
+VMEM = pl.BlockSpec(memory_space=pltpu.VMEM)
+
+
+def kernel_call(body, name, scalars, arrays, outs, scratch, flops, limit):
+    shapes = [jax.ShapeDtypeStruct(shape, dtype) for shape, dtype in outs]
+    moved = sum(a.size * a.dtype.itemsize for a in arrays) + sum(s.size * s.dtype.itemsize for s in shapes)
+    return pl.pallas_call(
+        body,
+        name=name,
+        out_shape=shapes,
+        in_specs=[SMEM] * len(scalars) + [VMEM] * len(arrays),
+        out_specs=[VMEM] * len(shapes),
+        scratch_shapes=scratch,
+        compiler_params=pltpu.CompilerParams(vmem_limit_bytes=limit * MIB),
+        cost_estimate=pl.CostEstimate(flops=flops, bytes_accessed=moved, transcendentals=0),
+    )(*scalars, *arrays)
+
+
+def gather_plan(
+    grid_latent,
+    mesh_latent,
+    grid_cotangent,
+    enc_sender,
+    enc_receiver,
+    enc_feat,
+    enc_count,
+    dec_sender,
+    dec_feat,
+    serve_rows,
+    enc_proj,
+    node_proj,
+    dec_proj,
+    enc_feat_w,
+    dec_feat_w,
+):
+    owners = lax.axis_size("lat")
+    chips = owners // 2
+    cap = serve_rows.shape[2]
+    slots = owners * cap
+    mesh_rows, width = mesh_latent.shape
+    grid_rows = grid_latent.shape[0]
+    edges = enc_sender.shape[0]
+    feats = enc_feat.shape[0]
+    block = width // owners
+    rows = slots + TAIL
+    span = chips * rows
+    groups = [[core + 2 * chip for chip in range(chips)] for core in range(2)]
+    swap = [(index, index ^ 1) for index in range(owners)]
+    place = lax.axis_index("lat").astype(jnp.int32).reshape(1)
+
+    def gather(message):
+        first = lax.all_to_all(message, "lat", 0, 0, tiled=True, axis_index_groups=groups)
+        return first, lax.ppermute(first, "lat", swap)
+
+    served_ids = serve_rows.reshape(1, slots)
+    served = jnp.take(mesh_latent, served_ids[0], axis=0)
+    id_row = jnp.zeros((1, width), jnp.int32)
+    id_row = lax.dynamic_update_slice(id_row, served_ids // 256, (0, 0))
+    id_row = lax.dynamic_update_slice(id_row, served_ids % 256, (0, 128))
+    own_rows = served.reshape(chips, 2 * cap, width)
+    id_rows = jnp.broadcast_to(id_row.astype(BF)[None], (chips, 1, width))
+    extra = jnp.concatenate([own_rows, id_rows, jnp.zeros((chips, TAIL - 2 * cap - 1, width), BF)], 1)
+    columns = served.reshape(slots, chips, 2 * block).transpose(1, 0, 2).reshape(chips, 2 * cap, width)
+
+    send = enc_sender.reshape(1, edges)
+    receive = enc_receiver.reshape(1, edges)
+    message, slope = kernel_call(
+        encoder_kernel,
+        "encoder",
+        [enc_count],
+        [grid_latent, enc_proj, send, receive, enc_feat, enc_feat_w, extra],
+        [((chips, rows, width), BF), ((edges, width), BF)],
+        [pltpu.VMEM((grid_rows, width), BF)],
+        2 * edges * grid_rows * width,
+        32,
+    )
+    first, second = gather(message)
+    message, keys, same, agg_slope = kernel_call(
+        lambda *refs: decoder_kernel(cap, mesh_rows, *refs),
+        "decoder",
+        [place],
+        [first, second, node_proj, dec_proj, dec_sender, dec_feat, dec_feat_w, grid_cotangent, columns],
+        [((chips, rows, width), BF), ((2, span), F32), ((2, slots, span), BF), ((slots, width), F32)],
+        [],
+        24 * grid_rows * 128 * width,
+        32,
+    )
+    first_back, second_back = gather(message)
+    wide = width + 128
+    term_rows = -(-6 * feats // 16) * 16
+    dpx, keep, give = kernel_call(
+        backward_kernel,
+        "backward",
+        [place, enc_count],
+        [first_back, second_back, same, agg_slope, node_proj, dec_proj, send, receive, enc_feat, slope, grid_latent],
+        [((grid_rows, width), BF), ((chips, block, wide), F32), ((chips, block, wide), BF)],
+        [
+            pltpu.VMEM((grid_rows + term_rows, edges), BF),
+            pltpu.VMEM((edges, width), BF),
+            pltpu.VMEM((width, wide), F32),
+        ],
+        2 * edges * grid_rows * width,
+        32,
+    )
+    pair = (keep + lax.ppermute(give, "lat", swap).astype(F32)).astype(BF)
+    arrived = lax.all_to_all(pair, "lat", 0, 0, tiled=True, axis_index_groups=groups)
+    mesh_grad, dec_proj_grad, node_proj_grad, dec_feat_sum = kernel_call(
+        lambda *refs: weight_kernel(cap, mesh_rows, feats, *refs),
+        "weights",
+        [place],
+        [first, second, first_back, second_back, keys, node_proj, dec_proj],
+        [((mesh_rows, width), BF), ((block, width), F32), ((block, width), F32), ((8, width), F32)],
+        [],
+        2 * (2 * span) * (2 * span) * width,
+        32,
+    )
+    grid_grad = (
+        grid_cotangent.astype(F32) + lax.dot_general(dpx, enc_proj, NT, preferred_element_type=F32)
+    ).astype(BF)
+    total = jnp.sum(arrived.astype(F32), axis=0)
+    dec_feat_w_grad = lax.dynamic_slice(dec_feat_sum, (0, place[0] * block), (feats, block)).T
+    return (
+        grid_grad,
+        mesh_grad,
+        total[:, :width],
+        node_proj_grad,
+        dec_proj_grad,
+        total[:, width : width + feats],
+        dec_feat_w_grad,
+    )
+
+
+def gather_fits(args):
+    mesh_latent, serve_rows = args[1], args[9]
+    owners, cap = serve_rows.shape[1], serve_rows.shape[2]
+    width = mesh_latent.shape[1]
+    return (
+        owners * cap <= 128
+        and owners % 8 == 0
+        and cap == 4
+        and width % (128 * owners // 8) == 0
+        and mesh_latent.shape[0] <= 65536
+        and mesh_latent.shape[0] * owners < 1 << 24
+        and args[0].shape[0] % 128 == 0
+        and args[3].shape[0] % 128 == 0
+        and args[5].shape[0] == 4
+    )
+
+
+def per_device(*args):
+    return gather_plan(*args) if gather_fits(args) else owner_plan(*args)
+
+
 def solution(mesh):
     placed = (
         P(("member", "lat"), None),

time: 424 us -> 104 us (0.25)
  waiting for transfers between devices: 267 us -> 5.39 us
  matrix products: 54.5 us -> 1.71 us
  blocking collectives: 10.7 us -> 45.8 us
  local copies, waits for them, and re-layouts: 52.2 us -> 18.6 us
  Pallas kernels: 0 us -> 24.7 us
  between operations: 14.2 us -> 1.57 us
  starting transfers between devices: 14.6 us -> 3.57 us
  other arithmetic: 8.54 us -> 2.12 us
    unnamed x8 -> x0, waiting for transfers between devices: 127 us -> none
    reduce_scatter x2 -> x0, waiting for transfers between devices: 120 us -> none  [the longest x1 60.9 us: per_device(): lax.psum_scatter(node_proj_part, 'lat', scatter_dimension=0, tiled=True)]
    dot_general x51 -> x1, matrix products: 54.5 us -> 1.71 us  [gather_plan(): lax.dot_general(dpx, enc_proj, NT, preferred_element_type=F32)]
    all_to_all x1 -> x2, blocking collectives: 10.7 us -> 45.8 us  [gather(): lax.all_to_all(message, 'lat', 0, 0, tiled=True, axis_index_groups=groups)]
    gather x16 -> x2, local copies, waits for them, and re-layouts: 31.8 us -> 0.83 us  [gather_plan(): served = jnp.take(mesh_latent, served_ids[0], axis=0)]
    pallas_call x0 -> x4, Pallas kernels: none -> 24.7 us  [kernel_call(): pl.pallas_call(body, name=name, out_shape=shapes, in_specs=[SMEM] * len(s...]
    all_to_all x3 -> x1, waiting for transfers between devices: 20.4 us -> 0.01 us  [gather_plan(): lax.all_to_all(pair, 'lat', 0, 0, tiled=True, axis_index_groups=groups)]
    all_to_all x3 -> x1, starting transfers between devices: 14.4 us -> 3.43 us  [gather_plan(): lax.all_to_all(pair, 'lat', 0, 0, tiled=True, axis_index_groups=groups)]
  transfers between devices with their start and end apart: 8 -> 4, of which waited for: 8 -> 3; matrix products, arithmetic and copies ran while one was open for 9% -> 3% of each run, Pallas kernels for 0% -> 6%
where the time goes in v1:
time: 104 us
  blocking collectives  45.8 us (44%)
  Pallas kernels  24.7 us (24%)
  local copies, waits for them, and re-layouts  18.6 us (18%)
  waiting for transfers between devices  5.39 us (5%)
  starting transfers between devices  3.57 us (3%)
  other arithmetic  2.12 us (2%)
  matrix products  1.71 us (2%)
  between operations  1.57 us (2%)
    all_to_all x2, blocking collectives, gather(): lax.all_to_all(message, 'lat', 0, 0, tiled=True, axis_index_groups=groups)  45.8 us
    pallas_call x4, Pallas kernels, kernel_call(): pl.pallas_call(body, name=name, out_shape=shapes, in_specs=[SMEM] * len(s...  24.7 us
    unnamed x60, local copies, waits for them, and re-layouts  15.8 us
    ppermute x2, waiting for transfers between devices, gather(): return (first, lax.ppermute(first, 'lat', swap))  3.55 us
    all_to_all x1, starting transfers between devices, gather_plan(): lax.all_to_all(pair, 'lat', 0, 0, tiled=True, axis_index_groups=groups)  3.43 us
  transfers between devices with their start and end apart: 4, of which 3 were waited for; matrix products, arithmetic and copies ran while one was open for 3% of the time, Pallas kernels for 6%

profile of v1, /device:TPU:0, one launch (start us, length us, event | category | flops | bytes accessed | tf_op | source)
XLA Modules:
  0.0 103.6 jit_solution(8154922753759689902)
XLA Ops:
  0.6 0.0 copy-start
  0.6 0.8 copy.38
  1.5 0.1 reshape.222
  1.5 0.1 squeeze_reshape.8
  1.6 0.1 squeeze_reshape.7
  2.4 0.2 dynamic_update_slice.7
  2.6 0.8 copy.41.feat_w
  3.5 0.1 pad.3.clone
  3.5 0.7 gather_fusion
  4.3 0.1 bitcast_select_fusion
  4.4 0.1 maximum_maximum_fusion.extra
  4.4 0.0 copy-start.1
  4.5 1.2 %copy-done.1 = bf16[1024,512]{1,0:T(8,128)(2,1)S(1)} copy-done((bf16[1024,512]{1,0:T(8,128)(2,1)S(1)}, bf16[1024,512]{1,0:T(8,128)(2,1)}, u32[]{:S(2)}) %copy-start.1) | copy-done | bytes 1048600
  5.7 1.0 %copy-done.13 = bf16[512,512]{1,0:T(8,128)(2,1)S(1)} copy-done((bf16[512,512]{1,0:T(8,128)(2,1)S(1)}, bf16[512,512]{1,0:T(8,128)(2,1)}, u32[]{:S(2)}) %copy-start.13) | copy-done | bytes 524312
  6.7 0.8 copy-done.16
  7.5 0.7 copy-done.19
  8.2 0.7 copy-done.21
  8.9 6.0 %encoder.1 = (bf16[8,80,512]{2,1,0:T(8,128)(2,1)S(1)}, bf16[2048,512]{1,0:T(8,128)(2,1)S(1)}) custom-call(s32[1]{0:T(128)S(6)} %copy.50.count, bf16[1024,512]{1,0:T(8,128)(2,1)S(1)} %copy-done.1, bf16[512,512]{1,0:T(8,128)(2,1)S(1)} %copy-done.13, s32[1,2048]{1,0:T(1,128)S(1)} %bitcast.13, s32[1,2048]{1,0:T(1,128)S(1)} %bitcast.15, ...), custom_call_target="tpu_custom_call" | custom-call | flops 2147483648 | bytes 4513792 | tf_op jit(solution)/shard_map/encoder/pallas_call | solution.py:461
  14.9 1.4 %copy-done.25 = bf16[2048,512]{1,0:T(8,128)(2,1)} copy-done((bf16[2048,512]{1,0:T(8,128)(2,1)}, bf16[2048,512]{1,0:T(8,128)(2,1)S(1)}, u32[]{:S(2)}) %copy-start.25) | copy-done | bytes 2097176
  16.2 24.9 %all_to_all.15.refs_1_ = bf16[8,80,512]{2,1,0:T(8,128)(2,1)S(1)} all-to-all(bf16[8,80,512]{2,1,0:T(8,128)(2,1)S(1)} %get-tuple-element.20), channel_id=1, replica_groups={{0,2,4,6,8,10,12,14},{1,3,5,7,9,11,13,15},{16,18,20,22,24,26,28,30},{17..., dimensions={0} | all-to-all | bytes 1310720 | tf_op jit(solution)/shard_map/all_to_all | solution.py:506
  41.1 0.1 squeeze_reshape.9
  41.2 0.1 gather.10
  41.3 0.1 fusion
  41.4 0.1 reshape.223.refs_9_
  41.6 0.1 copy.44.refs_7_
  41.7 1.5 %collective-permute-done.refs_2_ = bf16[8,80,512]{2,1,0:T(8,128)(2,1)S(1)} collective-permute-done((bf16[8,80,512]{2,1,0:T(8,128)(2,1)S(1)}, bf16[8,80,512]{2,1,0:T(8,128)(2,1)S(1)}, u32[]{:S(2)}, u32[]{:S(2)}) %collective-permute-start) | collective-permute-done | bytes 655392 | tf_op jit(solution)/shard_map/ppermute | solution.py:507
  43.2 0.0 copy-start.8
  43.2 1.3 %copy-done.8 = bf16[512,512]{1,0:T(8,128)(2,1)S(1)} copy-done((bf16[512,512]{1,0:T(8,128)(2,1)S(1)}, bf16[512,512]{1,0:T(8,128)(2,1)}, u32[]{:S(2)}) %copy-start.8) | copy-done | bytes 524312
  44.5 1.0 %copy-done.11 = bf16[512,512]{1,0:T(8,128)(2,1)S(1)} copy-done((bf16[512,512]{1,0:T(8,128)(2,1)S(1)}, bf16[512,512]{1,0:T(8,128)(2,1)}, u32[]{:S(2)}) %copy-start.11) | copy-done | bytes 524312
  45.5 0.0 copy-start.22
  45.6 6.0 %decoder.1 = (bf16[8,80,512]{2,1,0:T(8,128)(2,1)S(1)}, f32[2,640]{1,0:T(2,128)S(1)}, bf16[2,64,640]{2,1,0:T(8,128)(2,1)S(1)}, f32[64,512]{1,0:T(8,128)S(1)}) custom-call(s32[1]{0:T(128)} %bitcast.refs_0_.place, bf16[8,80,512]{2,1,0:T(8,128)(2,1)S(1)} %all_to_all.15.refs_1_, bf16[8,80,512]{2,1,0:T(8,128)(2,1)S(1)} %collective-permute-done.refs_2_, ...), custom_call_target="tpu_custom_call" | custom-call | flops 1610612736 | bytes 4498432 | tf_op jit(solution)/shard_map/decoder/pallas_call | solution.py:461
  51.6 21.0 %all_to_all.16.first.refs_3_ = bf16[8,80,512]{2,1,0:T(8,128)(2,1)S(1)} all-to-all(bf16[8,80,512]{2,1,0:T(8,128)(2,1)S(1)} %get-tuple-element.21), channel_id=1, replica_groups={{0,2,4,6,8,10,12,14},{1,3,5,7,9,11,13,15},{16,18,20,22,24,26,28,30},{17..., dimensions={0} | all-to-all | bytes 1310720 | tf_op jit(solution)/shard_map/all_to_all | solution.py:506
  72.6 2.1 %collective-permute-done.1.second.refs_4_ = bf16[8,80,512]{2,1,0:T(8,128)(2,1)S(1)} collective-permute-done((bf16[8,80,512]{2,1,0:T(8,128)(2,1)S(1)}, bf16[8,80,512]{2,1,0:T(8,128)(2,1)S(1)}, u32[]{:S(2)}, u32[]{:S(2)}) %collective-permute-start.1) | collective-permute-done | bytes 655392 | tf_op jit(solution)/shard_map/ppermute | solution.py:507
  74.7 6.0 %backward.1 = (bf16[1024,512]{1,0:T(8,128)(2,1)S(1)}, f32[8,32,640]{2,1,0:T(8,128)S(1)}, bf16[8,32,640]{2,1,0:T(8,128)(2,1)}) custom-call(s32[1]{0:T(128)} %bitcast.refs_0_.place, s32[1]{0:T(128)S(6)} %copy.50.count, bf16[8,80,512]{2,1,0:T(8,128)(2,1)S(1)} %all_to_all.16.first.refs_3_, bf16[8,80,512]{2,1,0:T(8,128)(2,1)S(1)} %collective-permute-done.1.second.refs_4_, ...), custom_call_target="tpu_custom_call" | custom-call | flops 2147483648 | bytes 7880704 | tf_op jit(solution)/shard_map/backward/pallas_call | solution.py:461
  80.7 1.0 copy-done.23
  81.7 0.1 collective-permute-start.2
  81.8 1.8 %collective-permute-done.2 = bf16[8,32,640]{2,1,0:T(8,128)(2,1)} collective-permute-done((bf16[8,32,640]{2,1,0:T(8,128)(2,1)}, bf16[8,32,640]{2,1,0:T(8,128)(2,1)}, u32[]{:S(2)}, u32[]{:S(2)}) %collective-permute-start.2) | collective-permute-done | bytes 327712 | tf_op jit(solution)/shard_map/ppermute | solution.py:559
  83.6 1.8 %add_convert_fusion.1 = bf16[8,32,640]{2,1,0:T(8,128)(2,1)} fusion(f32[8,32,640]{2,1,0:T(8,128)S(1)} %get-tuple-element.28, bf16[8,32,640]{2,1,0:T(8,128)(2,1)} %collective-permute-done.2), kind=kLoop, calls=%fused_computation.3 | loop fusion | flops 491520 | bytes 1310720 | tf_op jit(solution)/shard_map/convert_element_type | solution.py:559
  85.4 3.4 %all-to-all-start.2 = ((bf16[8,32,640]{2,1,0:T(8,128)(2,1)}), bf16[8,32,640]{2,1,0:T(8,128)(2,1)S(1)}, u32[]{:S(2)}, u32[]{:S(2)}) async-start(bf16[8,32,640]{2,1,0:T(8,128)(2,1)} %add_convert_fusion.1), calls=%async_computation.2 | async-start | bytes 655360 | tf_op jit(solution)/shard_map/all_to_all | solution.py:560
  88.9 1.1 %copy-done.5 = bf16[8,80,512]{2,1,0:T(8,128)(2,1)S(1)} copy-done((bf16[8,80,512]{2,1,0:T(8,128)(2,1)S(1)}, bf16[8,80,512]{2,1,0:T(8,128)(2,1)}, u32[]{:S(2)}) %copy-start.5) | copy-done | bytes 655384
  89.9 1.1 %copy-done.7 = bf16[8,80,512]{2,1,0:T(8,128)(2,1)S(1)} copy-done((bf16[8,80,512]{2,1,0:T(8,128)(2,1)S(1)}, bf16[8,80,512]{2,1,0:T(8,128)(2,1)}, u32[]{:S(2)}) %copy-start.7) | copy-done | bytes 655384
  91.0 1.0 %copy-done.10 = bf16[512,512]{1,0:T(8,128)(2,1)S(1)} copy-done((bf16[512,512]{1,0:T(8,128)(2,1)S(1)}, bf16[512,512]{1,0:T(8,128)(2,1)}, u32[]{:S(2)}) %copy-start.10) | copy-done | bytes 524312
  92.1 1.0 %copy-done.12 = bf16[512,512]{1,0:T(8,128)(2,1)S(1)} copy-done((bf16[512,512]{1,0:T(8,128)(2,1)S(1)}, bf16[512,512]{1,0:T(8,128)(2,1)}, u32[]{:S(2)}) %copy-start.12) | copy-done | bytes 524312
  93.1 6.7 %weights.1 = (bf16[320,512]{1,0:T(8,128)(2,1)}, f32[32,512]{1,0:T(8,128)}, f32[32,512]{1,0:T(8,128)}, f32[8,512]{1,0:T(8,128)S(1)}) custom-call(s32[1]{0:T(128)} %bitcast.refs_0_.place, bf16[8,80,512]{2,1,0:T(8,128)(2,1)S(1)} %all_to_all.15.refs_1_, bf16[8,80,512]{2,1,0:T(8,128)(2,1)S(1)} %copy-done.5, bf16[8,80,512]{2,1,0:T(8,128)(2,1)S(1)} %all_to_all.16.first.refs_3_, ...), custom_call_target="tpu_custom_call" | custom-call | flops 1677721600 | bytes 4150272 | tf_op jit(solution)/shard_map/weights/pallas_call | solution.py:461
  99.9 0.6 dynamic-slice_bitcast_fusion
  100.5 1.7 %add_convert_fusion = bf16[1024,512]{1,0:T(8,128)(2,1)} fusion(bf16[1024,512]{1,0:T(8,128)(2,1)S(1)} %copy-done.3, bf16[1024,512]{1,0:T(8,128)(2,1)S(1)} %copy-done.24, bf16[512,512]{1,0:T(8,128)(2,1)S(1)} %copy-done.14), kind=kOutput, calls=%fused_computation.1 | convolution fusion | flops 538443776 | bytes 3670016 | tf_op jit(solution)/shard_map/dot_general | solution.py:572
  102.3 0.6 slice.10
  102.9 0.7 copy.45
  (53 shorter events, 0.2 us)
Async XLA Ops:
  0.6 2.9 %copy-start = (bf16[320,512]{1,0:T(8,128)(2,1)S(1)}, bf16[320,512]{1,0:T(8,128)(2,1)}, u32[]{:S(2)}) copy-start(bf16[320,512]{1,0:T(8,128)(2,1)} %param.16) | copy-start | bytes 983044
  4.4 1.2 %copy-start.1 = (bf16[1024,512]{1,0:T(8,128)(2,1)S(1)}, bf16[1024,512]{1,0:T(8,128)(2,1)}, u32[]{:S(2)}) copy-start(bf16[1024,512]{1,0:T(8,128)(2,1)} %latent.3) | copy-start | bytes 3145732
  5.7 1.0 %copy-start.13 = (bf16[512,512]{1,0:T(8,128)(2,1)S(1)}, bf16[512,512]{1,0:T(8,128)(2,1)}, u32[]{:S(2)}) copy-start(bf16[512,512]{1,0:T(8,128)(2,1)} %weight.1) | copy-start | bytes 1572868
  6.7 0.8 copy-start.16
  7.5 0.7 copy-start.19
  8.2 0.7 copy-start.21
  8.9 32.7 %copy-start.27 = (f32[512,4]{0,1:T(4,128)S(1)}, f32[512,4]{0,1:T(4,128)}, u32[]{:S(2)}) copy-start(f32[512,4]{0,1:T(4,128)} %param.29) | copy-start | bytes 24580
  14.9 1.4 %copy-start.25 = (bf16[2048,512]{1,0:T(8,128)(2,1)}, bf16[2048,512]{1,0:T(8,128)(2,1)S(1)}, u32[]{:S(2)}) copy-start(bf16[2048,512]{1,0:T(8,128)(2,1)S(1)} %get-tuple-element.24.slope) | copy-start | bytes 6291460
  16.2 27.0 %copy-start.3 = (bf16[1024,512]{1,0:T(8,128)(2,1)S(1)}, bf16[1024,512]{1,0:T(8,128)(2,1)}, u32[]{:S(2)}) copy-start(bf16[1024,512]{1,0:T(8,128)(2,1)} %refs_8_.1) | copy-start | bytes 3145732
  16.2 27.0 %copy-start.15 = (f32[3,4,1024]{2,1,0:T(4,128)S(1)}, f32[3,4,1024]{2,1,0:T(4,128)}, u32[]{:S(2)}) copy-start(f32[3,4,1024]{2,1,0:T(4,128)} %refs_6_.2) | copy-start | bytes 147460
  16.2 27.0 %copy-start.18 = (s32[3,1024]{1,0:T(4,128)S(1)}, s32[3,1024]{1,0:T(4,128)}, u32[]{:S(2)}) copy-start(s32[3,1024]{1,0:T(4,128)} %refs_5_.1) | copy-start | bytes 36868
  41.1 2.1 %collective-permute-start = (bf16[8,80,512]{2,1,0:T(8,128)(2,1)S(1)}, bf16[8,80,512]{2,1,0:T(8,128)(2,1)S(1)}, u32[]{:S(2)}, u32[]{:S(2)}) collective-permute-start(bf16[8,80,512]{2,1,0:T(8,128)(2,1)S(1)} %all_to_all.15.refs_1_), channel_id=1, source_target_pairs={{0,1},{1,0},{2,3},{3,2},{4,5},{5,4},{6,7},{7,6},{8,9},{9,8},{10,11... | collective-permute-start | bytes 1966088 | tf_op jit(solution)/shard_map/ppermute | solution.py:507
  43.2 8.4 %copy-start.4 = (bf16[8,80,512]{2,1,0:T(8,128)(2,1)}, bf16[8,80,512]{2,1,0:T(8,128)(2,1)S(1)}, u32[]{:S(2)}) copy-start(bf16[8,80,512]{2,1,0:T(8,128)(2,1)S(1)} %collective-permute-done.refs_2_) | copy-start | bytes 1966084
  43.2 1.3 %copy-start.8 = (bf16[512,512]{1,0:T(8,128)(2,1)S(1)}, bf16[512,512]{1,0:T(8,128)(2,1)}, u32[]{:S(2)}) copy-start(bf16[512,512]{1,0:T(8,128)(2,1)} %refs_6_.3) | copy-start | bytes 1572868
  44.5 1.0 %copy-start.11 = (bf16[512,512]{1,0:T(8,128)(2,1)S(1)}, bf16[512,512]{1,0:T(8,128)(2,1)}, u32[]{:S(2)}) copy-start(bf16[512,512]{1,0:T(8,128)(2,1)} %refs_7_.2) | copy-start | bytes 1572868
  45.5 29.1 %copy-start.2 = (bf16[1024,512]{1,0:T(8,128)(2,1)S(1)}, bf16[1024,512]{1,0:T(8,128)(2,1)}, u32[]{:S(2)}) copy-start(bf16[1024,512]{1,0:T(8,128)(2,1)} %latent.3) | copy-start | bytes 3145732
  45.5 29.1 %copy-start.9 = (bf16[512,512]{1,0:T(8,128)(2,1)S(1)}, bf16[512,512]{1,0:T(8,128)(2,1)}, u32[]{:S(2)}) copy-start(bf16[512,512]{1,0:T(8,128)(2,1)} %refs_6_.3) | copy-start | bytes 1572868
  45.5 29.1 %copy-start.17 = (f32[4,2048]{1,0:T(4,128)S(1)}, f32[4,2048]{1,0:T(4,128)}, u32[]{:S(2)}) copy-start(f32[4,2048]{1,0:T(4,128)} %feat.3) | copy-start | bytes 98308
  45.5 29.1 %copy-start.20 = (s32[2048]{0:T(1024)S(1)}, s32[2048]{0:T(1024)}, u32[]{:S(2)}) copy-start(s32[2048]{0:T(1024)} %param.18) | copy-start | bytes 24580
  45.5 29.1 %copy-start.22 = (s32[2048]{0:T(1024)S(1)}, s32[2048]{0:T(1024)}, u32[]{:S(2)}) copy-start(s32[2048]{0:T(1024)} %param.19) | copy-start | bytes 24580
  45.6 29.1 %copy-start.26 = (bf16[2048,512]{1,0:T(8,128)(2,1)S(1)}, bf16[2048,512]{1,0:T(8,128)(2,1)}, u32[]{:S(2)}) copy-start(bf16[2048,512]{1,0:T(8,128)(2,1)} %copy-done.25) | copy-start | bytes 6291460
  72.6 2.1 %collective-permute-start.1 = (bf16[8,80,512]{2,1,0:T(8,128)(2,1)S(1)}, bf16[8,80,512]{2,1,0:T(8,128)(2,1)S(1)}, u32[]{:S(2)}, u32[]{:S(2)}) collective-permute-start(bf16[8,80,512]{2,1,0:T(8,128)(2,1)S(1)} %all_to_all.16.first.refs_3_), channel_id=1, source_target_pairs={{0,1},{1,0},{2,3},{3,2},{4,5},{5,4},{6,7},{7,6},{8,9},{9,8},{10,11... | collective-permute-start | bytes 1966088 | tf_op jit(solution)/shard_map/ppermute | solution.py:507
  74.7 6.1 %copy-start.6 = (bf16[8,80,512]{2,1,0:T(8,128)(2,1)}, bf16[8,80,512]{2,1,0:T(8,128)(2,1)S(1)}, u32[]{:S(2)}) copy-start(bf16[8,80,512]{2,1,0:T(8,128)(2,1)S(1)} %collective-permute-done.1.second.refs_4_) | copy-start | bytes 1966084
  80.7 1.0 copy-start.23
  81.7 2.0 %collective-permute-start.2 = (bf16[8,32,640]{2,1,0:T(8,128)(2,1)}, bf16[8,32,640]{2,1,0:T(8,128)(2,1)}, u32[]{:S(2)}, u32[]{:S(2)}) collective-permute-start(bf16[8,32,640]{2,1,0:T(8,128)(2,1)} %get-tuple-element.29), channel_id=1, source_target_pairs={{0,1},{1,0},{2,3},{3,2},{4,5},{5,4},{6,7},{7,6},{8,9},{9,8},{10,11... | collective-permute-start | bytes 983048 | tf_op jit(solution)/shard_map/ppermute | solution.py:559
  85.4 16.8 %all-to-all-start.2 = ((bf16[8,32,640]{2,1,0:T(8,128)(2,1)}), bf16[8,32,640]{2,1,0:T(8,128)(2,1)S(1)}, u32[]{:S(2)}, u32[]{:S(2)}) async-start(bf16[8,32,640]{2,1,0:T(8,128)(2,1)} %add_convert_fusion.1), calls=%async_computation.2 | async-start | bytes 655360 | tf_op jit(solution)/shard_map/all_to_all | solution.py:560
  88.9 1.1 %copy-start.5 = (bf16[8,80,512]{2,1,0:T(8,128)(2,1)S(1)}, bf16[8,80,512]{2,1,0:T(8,128)(2,1)}, u32[]{:S(2)}) copy-start(bf16[8,80,512]{2,1,0:T(8,128)(2,1)} %copy-done.4) | copy-start | bytes 1966084
  89.9 1.1 %copy-start.7 = (bf16[8,80,512]{2,1,0:T(8,128)(2,1)S(1)}, bf16[8,80,512]{2,1,0:T(8,128)(2,1)}, u32[]{:S(2)}) copy-start(bf16[8,80,512]{2,1,0:T(8,128)(2,1)} %copy-done.6) | copy-start | bytes 1966084
  91.0 1.0 %copy-start.10 = (bf16[512,512]{1,0:T(8,128)(2,1)S(1)}, bf16[512,512]{1,0:T(8,128)(2,1)}, u32[]{:S(2)}) copy-start(bf16[512,512]{1,0:T(8,128)(2,1)} %refs_6_.3) | copy-start | bytes 1572868
  92.1 1.0 %copy-start.12 = (bf16[512,512]{1,0:T(8,128)(2,1)S(1)}, bf16[512,512]{1,0:T(8,128)(2,1)}, u32[]{:S(2)}) copy-start(bf16[512,512]{1,0:T(8,128)(2,1)} %refs_7_.2) | copy-start | bytes 1572868
  93.1 7.4 %copy-start.14 = (bf16[512,512]{1,0:T(8,128)(2,1)S(1)}, bf16[512,512]{1,0:T(8,128)(2,1)}, u32[]{:S(2)}) copy-start(bf16[512,512]{1,0:T(8,128)(2,1)} %weight.1) | copy-start | bytes 1572868
  93.1 7.4 %copy-start.24 = (bf16[1024,512]{1,0:T(8,128)(2,1)S(1)}, bf16[1024,512]{1,0:T(8,128)(2,1)}, u32[]{:S(2)}) copy-start(bf16[1024,512]{1,0:T(8,128)(2,1)} %copy-done.23) | copy-start | bytes 3145732

commit v2 on v1

--- a/solution.py
+++ b/solution.py
@@ -11,7 +11,6 @@
 F32 = jnp.float32
 HI = lax.Precision.HIGHEST
 MIB = 1 << 20
-TAIL = 16
 NN = (((1,), (0,)), ((), ()))
 NT = (((1,), (1,)), ((), ()))
 TN = (((0,), (0,)), ((), ()))
@@ -217,10 +216,11 @@
 WEIGHT_ORDER = (0, 1, 0, 1, 0, 2)
 
 
-def weight_rows(weight):
-    feats = weight.shape[1]
-    eye = (iota((8, feats), 0) == iota((8, feats), 1)).astype(F32)
-    return stack_terms(mm(eye, weight, NT, HI)[:feats], WEIGHT_ORDER)
+def fetch(sources, targets, sems):
+    copies = [pltpu.make_async_copy(src, dst, sems.at[i]) for i, (src, dst) in enumerate(zip(sources, targets))]
+    for copy in copies:
+        copy.start()
+    return copies
 
 
 def feature_grad(terms, feats):
@@ -231,88 +231,171 @@
     return mm(want.astype(F32), terms, precision=HI)
 
 
-def encoder_kernel(count, latent, weight, send, receive, feat, feat_w, extra, message, slope, px):
+def encoder_kernel(
+    cap, count, latent_any, weight_any, mesh_any, send_any, receive_any, feat_any, feat_w_any, serve_any,
+    message, slope_far, served_out, px, picks, slope, slope_sems,
+    latent, weight, mesh, send, receive, feat, feat_w, serve, sems,
+):
+    sources = (send_any, latent_any, weight_any, feat_any, feat_w_any, receive_any, mesh_any, serve_any)
+    targets = (send, latent, weight, feat, feat_w, receive, mesh, serve)
+    copies = fetch(sources, targets, sems)
     edges = send.shape[1]
-    grid_rows = latent.shape[0]
-    slots = message.shape[1] - TAIL
+    grid_rows, width = latent.shape
+    chips = message.shape[0]
+    slots = served_out.shape[0]
     block = math.gcd(edges, 512)
-    px[...] = mm(latent[...], weight[...]).astype(BF)
-    w_rows = weight_rows(feat_w[...])
-    total = jnp.zeros((slots, latent.shape[1]), F32)
+    copies[0].wait()
     for start in range(0, edges, block):
         part = slice(start, start + block)
         ids = jnp.broadcast_to(send[:, part].astype(F32), (128, block)).T
-        picks = [
-            hot(ids == (iota((block, 128), 1) + base).astype(F32))
-            for base in range(0, grid_rows, 128)
-        ]
-        pre = mm(jnp.concatenate(picks, 1), px[...])
+        for base in range(0, grid_rows, 128):
+            lane = (iota((block, 128), 1) + base).astype(F32)
+            picks[part, base : base + 128] = hot(ids == lane)
+    copies[1].wait()
+    copies[2].wait()
+    px[...] = mm(latent[...], weight[...]).astype(BF)
+    for copy in copies[3:6]:
+        copy.wait()
+    w_rows = stack_terms(feat_w[...], WEIGHT_ORDER)
+    total = jnp.zeros((slots, width), F32)
+    stores = []
+    for start in range(0, edges, block):
+        part = slice(start, start + block)
+        pre = mm(picks[part, :], px[...])
         pre = pre + mm(stack_terms(feat[:, part], FEAT_ORDER), w_rows, TN)
         sig = sigmoid(pre)
         silu = pre * sig
         slope[part, :] = (sig + silu * (1.0 - sig)).astype(BF)
+        out = pltpu.make_async_copy(slope.at[part, :], slope_far.at[part, :], slope_sems.at[len(stores)])
+        out.start()
+        stores.append(out)
         live = iota((1, block), 1) + start < count[0]
         slot = jnp.where(live, receive[:, part], -1)
         to_slot = hot(iota((slots, block), 0) == slot)
         total = total + mm(to_slot, silu.astype(BF))
+    copies[6].wait()
+    copies[7].wait()
+    owners = slots // cap
+    ids = serve[...]
+    spread = hot(iota((owners, slots), 0) == lax.div(iota((owners, slots), 1), cap))
+    turn = iota((cap, slots), 0) == iota((cap, slots), 1) % cap
+    digits = []
+    for value in (lax.shift_right_logical(ids, 8), ids & 255):
+        wide = mm(value.astype(F32).astype(BF), spread)
+        digits.append(jnp.sum(jnp.where(turn, wide, 0.0), 0, keepdims=True))
+    id_row = (digits[0] * 256.0 + digits[1]).astype(jnp.int32)
+    served = mm(hot(iota((mesh.shape[0], slots), 0) == id_row), mesh[...], TN)
+    served_out[...] = served.astype(BF)
+    lane = iota((slots, 128), 1)
+    back = iota((slots, 128), 0)
+    wide = mm(digits[0].astype(BF), hot(lane == back)) + mm(digits[1].astype(BF), hot(lane == back + slots))
+    id_rows = jnp.where(iota((8, 128), 0) == 0, wide, 0.0)
     half = total.astype(BF)
-    for chip in range(message.shape[0]):
-        message[chip, :slots, :] = half
-        message[chip, slots:, :] = extra[chip]
-
-
-def gathered_rows(piece, chips, rows, core, cap, shape, dim):
+    for chip in range(chips):
+        write_slots(message, chip, half)
+        rows = served[2 * cap * chip : 2 * cap * (chip + 1)]
+        tail = [rows[:, base : base + 128] for base in range(0, width, 128)]
+        message[chip, slots * (width // 128) :, :] = jnp.concatenate([*tail, id_rows], 0).astype(BF)
+    for out in stores:
+        out.wait()
+
+
+def write_slots(message, chip, value):
+    slots = value.shape[0]
+    for part in range(value.shape[1] // 128):
+        message[chip, part * slots : (part + 1) * slots, :] = value[:, part * 128 : (part + 1) * 128]
+
+
+def slot_rows(ref, slots, width):
+    parts = [
+        jnp.concatenate([ref[chip, base : base + slots, :] for chip in range(ref.shape[0])], 0)
+        for base in range(0, slots * (width // 128), slots)
+    ]
+    return jnp.concatenate(parts, 1)
+
+
+def gathered_slots(piece, chips, core, cap, shape, dim):
+    slots = 2 * chips * cap
     index = iota(shape, dim)
-    chip = lax.div(index, rows)
-    slot = index - chip * rows
+    chip = lax.div(index, slots)
+    slot = index - chip * slots
     band = 2 * chip + jnp.where(piece == 0, core, 1 - core)
-    return band, slot, lax.div(slot, cap)
-
-
-def slot_matches(first, second, me, cap, mesh_rows):
-    chips, rows = first.shape[0], first.shape[1]
-    span = chips * rows
-    slots = rows - TAIL
+    return band, lax.div(slot, cap), lax.rem(slot, cap)
+
+
+def holder_of(shape, dim, chips, core):
+    index = iota(shape, dim)
+    return jnp.where(index < chips, 2 * index + core, 2 * (index - chips) + 1 - core)
+
+
+def slot_matches(first, second, me, cap, mesh_rows, width):
+    chips = first.shape[0]
     owners = 2 * chips
+    slots = owners * cap
+    span = chips * slots
+    parts = width // 128
     core = lax.rem(me, 2)
-    flat = [ref[...].reshape(span, -1) for ref in (first, second)]
-    table = jnp.zeros((owners, 256), F32)
+    table = jnp.zeros((owners, 128), F32)
+    latent = jnp.zeros((slots, width), F32)
+    for piece, ref in enumerate((first, second)):
+        ids, rows = [], []
+        for chip in range(chips):
+            tail = ref[chip, slots * parts :, :].astype(F32)
+            ids.append(tail[8 * parts :])
+            rows.append(jnp.concatenate([tail[8 * part : 8 * part + 8] for part in range(parts)], 1))
+        ids = jnp.concatenate(ids, 0).astype(BF)
+        rows = jnp.concatenate(rows, 0).astype(BF)
+        shape = (owners, 8 * chips)
+        table = table + mm(hot(iota(shape, 1) == (iota(shape, 0) - piece * chips) * 8), ids)
+        shape = (slots, 8 * chips)
+        window = iota(shape, 0)
+        owner = lax.div(window, cap)
+        held = lax.rem(owner, 2) == (core if piece == 0 else 1 - core)
+        at = lax.div(owner, 2) * 8 + cap * core + lax.rem(window, cap)
+        latent = latent + mm(hot(held & (iota(shape, 1) == at)), rows)
+    digits = table.astype(BF)
+    shape = (slots, owners)
+    mine = mm(hot(holder_of(shape, 1, chips, core) == lax.div(iota(shape, 0), cap)), digits)
+    lane = iota((slots, 128), 1) - cap * me - lax.rem(iota((slots, 128), 0), cap)
+    scaled = jnp.where(lane == 0, 256.0 * mine, jnp.where(lane == slots, mine, 0.0))
+    own_key = jnp.sum(scaled, 1, keepdims=True)
+    own_key = own_key + (lax.div(iota((slots, 1), 0), cap) * mesh_rows).astype(F32)
+    keys, same = [], []
     for piece in range(2):
-        shape = (owners, span)
-        at = (iota(shape, 0) - piece * chips) * rows + slots + 2 * cap
-        table = table + mm(hot(iota(shape, 1) == at), flat[piece][:, :256])
-    digits = jnp.concatenate([table[:, :128], table[:, 128:]], 0).astype(BF)
-    half = iota((slots, 2 * owners), 1)
-    holder = half % owners
-    holder = 2 * (holder % chips) + jnp.where(holder < chips, core, 1 - core)
-    wanted = holder == lax.div(iota((slots, 2 * owners), 0), cap)
-    mine = 256.0 * mm(hot(wanted & (half < owners)), digits) + mm(hot(wanted & (half >= owners)), digits)
-    lane = cap * me + iota((slots, 128), 0) % cap
-    own_key = jnp.sum(jnp.where(iota((slots, 128), 1) == lane, mine, 0.0), 1, keepdims=True)
-    own_key = own_key + (lax.div(iota((slots, 1), 0), cap) * mesh_rows).astype(F32)
-    keys, same, served = [], [], []
-    for piece in range(2):
-        band, slot, owner = gathered_rows(piece, chips, rows, core, cap, (1, span), 1)
-        spread = mm(digits, hot(iota((128, span), 0) == cap * band + slot % cap))
-        value = 256.0 * spread[:owners] + spread[owners:]
-        holder = iota((owners, 1), 0)
-        holder = 2 * (holder % chips) + jnp.where(holder < chips, core, 1 - core)
-        value = jnp.sum(jnp.where(holder == owner, value, 0.0), 0, keepdims=True)
-        key = jnp.where(slot < slots, value + (owner * mesh_rows).astype(F32), -1.0)
+        band, owner, place = gathered_slots(piece, chips, core, cap, (1, span), 1)
+        at = iota((128, span), 0) - cap * band - place
+        weight = jnp.where(at == 0, 256.0, jnp.where(at == slots, 1.0, 0.0)).astype(BF)
+        value = jnp.where(holder_of((owners, 1), 0, chips, core) == owner, mm(digits, weight), 0.0)
+        key = jnp.sum(value, 0, keepdims=True) + (owner * mesh_rows).astype(F32)
         keys.append(key)
         same.append(hot(key == own_key))
-        window = iota((slots, 1), 0)
-        row = slots + cap * core + window % cap
-        served.append(hot((band == lax.div(window, cap)) & (slot == row)))
-    return flat, keys, same, served
-
-
-def decoder_body(proj, send, feat, feat_w, cotangent):
-    slots = proj.shape[0]
+    return keys, same, latent
+
+
+def decoder_kernel(
+    cap, mesh_rows, place, first, second, extra, node_any, dec_any, send_any, feat_any, feat_w_any, cot_any,
+    message, keys_out, same_out, slope_out, grad_out, node_w, dec_w, send, feat, feat_w, cotangent, sems,
+):
+    sources = (node_any, dec_any, send_any, feat_any, feat_w_any, cot_any)
+    copies = fetch(sources, (node_w, dec_w, send, feat, feat_w, cotangent), sems)
+    slots, width = extra.shape
+    keys, same, latent = slot_matches(first, second, place[0], cap, mesh_rows, width)
+    agg = jnp.zeros((slots, width), F32)
+    for piece, ref in enumerate((first, second)):
+        keys_out[piece : piece + 1, :] = keys[piece]
+        same_out[piece] = same[piece]
+        agg = agg + mm(same[piece], slot_rows(ref, slots, width))
+    sig = sigmoid(agg)
+    silu = agg * sig
+    slope_out[...] = sig + silu * (1.0 - sig)
+    for copy in copies:
+        copy.wait()
+    hmesh = (latent + mm(silu.astype(BF), node_w[...])).astype(BF)
+    proj = mm(hmesh, dec_w[...]).astype(BF)
+    table = jnp.concatenate([proj, stack_terms(feat_w[...], WEIGHT_ORDER)], 0)
     grid_rows = cotangent.shape[0]
     block = math.gcd(grid_rows, 512)
-    table = jnp.concatenate([proj, weight_rows(feat_w[...])], 0)
-    total = jnp.zeros((table.shape[0], proj.shape[1]), F32)
+    total = jnp.zeros((table.shape[0], width), F32)
     for start in range(0, grid_rows, block):
         part = slice(start, start + block)
         cot = cotangent[part, :].astype(F32)
@@ -323,51 +406,40 @@
             sig = sigmoid(pre)
             slope = sig + pre * sig * (1.0 - sig)
             total = total + mm(pick, (cot * slope).astype(BF))
-    return total
-
-
-def decoder_kernel(
-    cap, mesh_rows, place, first, second, node_w, dec_w, send, feat, feat_w, cotangent, extra,
-    message, keys_out, same_out, slope_out,
+    half = total[:slots].astype(BF)
+    grad_out[...] = feature_grad(total[slots:], feat_w.shape[0])
+    chips = message.shape[0]
+    share = width // chips
+    step = slots * share // 128
+    for chip in range(chips):
+        write_slots(message, chip, half)
+        columns = extra[:, chip * share : (chip + 1) * share].astype(F32)
+        columns = jnp.concatenate([columns[base : base + step] for base in range(0, slots, step)], 1)
+        message[chip, slots * (width // 128) :, :] = columns.astype(BF)
+
+
+def backward_kernel(
+    place, count, first, second, same, agg_slope, dec_grad, node_any, dec_any, send_any, receive_any, feat_any,
+    latent_any, slope_any, dpx_out, keep, give, hots, grads, part, node_w, dec_w, send, receive, feat, latent, slope,
+    sems,
 ):
-    slots = first.shape[1] - TAIL
-    flat, keys, same, served = slot_matches(first, second, place[0], cap, mesh_rows)
-    both = jnp.zeros((2 * slots, first.shape[2]), F32)
-    for piece in range(2):
-        keys_out[piece : piece + 1, :] = keys[piece]
-        same_out[piece] = same[piece]
-        both = both + mm(jnp.concatenate([same[piece], served[piece]], 0), flat[piece])
-    agg, latent = both[:slots], both[slots:]
-    sig = sigmoid(agg)
-    silu = agg * sig
-    slope_out[...] = sig + silu * (1.0 - sig)
-    hmesh = (latent + mm(silu.astype(BF), node_w[...])).astype(BF)
-    proj = mm(hmesh, dec_w[...]).astype(BF)
-    total = decoder_body(proj, send, feat, feat_w, cotangent)
-    feats = feat_w.shape[1]
-    half = total[:slots].astype(BF)
-    grad = feature_grad(total[slots:], feats).astype(BF)
-    for chip in range(message.shape[0]):
-        message[chip, :slots, :] = half
-        message[chip, slots:, :] = jnp.concatenate([grad, extra[chip]], 0)
-
-
-def backward_kernel(
-    place, count, first, second, same, agg_slope, node_w, dec_w, send, receive, feat, slope, latent,
-    dpx_out, keep, give, hots, grads, part,
-):
+    sources = (send_any, feat_any, receive_any, dec_any, node_any, slope_any, latent_any)
+    copies = fetch(sources, (send, feat, receive, dec_w, node_w, slope, latent), sems)
     slots = same.shape[1]
     edges = send.shape[1]
     grid_rows, width = latent.shape
     feats = feat.shape[0]
     core = lax.rem(place[0], 2)
-    dproj = mm(same[0], first[...].reshape(-1, width)) + mm(same[1], second[...].reshape(-1, width))
+    dproj = mm(same[0], slot_rows(first, slots, width)) + mm(same[1], slot_rows(second, slots, width))
     high = dproj.astype(BF)
     low = (dproj - high.astype(F32)).astype(BF)
+    for copy in copies[:5]:
+        copy.wait()
     dhmesh = mm(jnp.concatenate([high, low], 0), dec_w[...], NT)
     mesh_grad = (dhmesh[:slots] + dhmesh[slots:]).astype(BF)
     dagg = (mm(mesh_grad, node_w[...], NT) * agg_slope[...]).astype(BF)
     block = math.gcd(edges, 512)
+    copies[5].wait()
     for start in range(0, edges, block):
         cut = slice(start, start + block)
         live = iota((1, block), 1) + start < count[0]
@@ -380,58 +452,85 @@
     for start in range(0, grid_rows, step):
         cut = slice(start, start + step)
         dpx_out[cut, :] = mm(hots[cut, :], grads[...]).astype(BF)
-    terms = mm(hots[grid_rows:, :], grads[...])
-    pick = iota((128, terms.shape[0]), 1)
-    row = iota((128, terms.shape[0]), 0)
-    want = (pick % feats == row) & (row < feats)
-    group = lax.div(pick, feats)
-    want = want & ((group == 0) | (group == 2) | (group == 4))
-    part[:, width:] = mm(want.astype(F32), terms, precision=HI).T
-    part[:, :width] = mm(latent[...], dpx_out[...], TN)
-    chips, rows = keep.shape[0], keep.shape[1]
-    for chip in range(chips):
-        keep[chip] = part[pl.ds((2 * chip + core) * rows, rows), :]
-        give[chip] = part[pl.ds((2 * chip + 1 - core) * rows, rows), :].astype(BF)
+    enc_grad = feature_grad(mm(hots[grid_rows:, :], grads[...]), feats)
+    sums = jnp.where(iota(enc_grad.shape, 0) < feats, enc_grad, pltpu.roll(dec_grad[...], feats, 0))
+    copies[6].wait()
+    part[...] = mm(latent[...], dpx_out[...], TN)
+    rows = width // (2 * keep.shape[0])
+    blank = jnp.zeros((8, 128 - rows), F32)
+    for chip in range(keep.shape[0]):
+        pair = [sums[:, base : base + rows] for base in (2 * chip * rows, (2 * chip + 1) * rows)]
+        for out, side in ((keep, core), (give, 1 - core)):
+            block = part[pl.ds((2 * chip + side) * rows, rows), :]
+            small = jnp.where(side == 0, pair[0], pair[1])
+            pieces = [block[:, base : base + 128] for base in range(0, width, 128)]
+            whole = jnp.concatenate([*pieces, jnp.concatenate([small, blank], 1)], 0)
+            out[chip] = whole.astype(out.dtype)
+
+
+def pair_kernel(keep, given, out):
+    out[...] = (keep[...] + given[...].astype(F32)).astype(BF)
+
+
+def grid_kernel(dpx, weight_any, cot_any, out, weight, cotangent, sems):
+    copies = fetch((weight_any, cot_any), (weight, cotangent), sems)
+    for copy in copies:
+        copy.wait()
+    out[...] = (cotangent[...].astype(F32) + mm(dpx[...], weight[...], NT)).astype(BF)
+
+
+def final_kernel(feats, arrived, out, enc_out, dec_out):
+    total = jnp.sum(arrived[...].astype(F32), 0)
+    rows, width = out.shape
+    for part in range(width // 128):
+        out[:, part * 128 : (part + 1) * 128] = total[part * rows : (part + 1) * rows]
+    base = rows * (width // 128)
+    enc_out[...] = total[base : base + feats, :rows]
+    dec_out[...] = total[base + feats : base + 2 * feats, :rows]
 
 
 def weight_kernel(
-    cap, mesh_rows, feats, place, first, second, first_back, second_back, keys, node_w, dec_w,
-    mesh_out, dec_out, node_out, feat_out,
+    cap, mesh_rows, place, first, second, first_back, second_back, keys, node_any, dec_any,
+    mesh_out, dec_out, node_out, node_w, dec_w, sems,
 ):
-    chips, rows, width = first.shape
-    slots = rows - TAIL
-    span = chips * rows
+    copies = fetch((node_any, dec_any), (node_w, dec_w), sems)
+    width = node_w.shape[0]
+    chips = first.shape[0]
     owners = 2 * chips
+    slots = owners * cap
+    span = chips * slots
     me = place[0]
     core = lax.rem(me, 2)
     block = width // owners
-    forward = jnp.concatenate([first[...].reshape(span, width), second[...].reshape(span, width)], 0)
-    back = jnp.concatenate([first_back[...].reshape(span, width), second_back[...].reshape(span, width)], 0)
+    forward = jnp.concatenate([slot_rows(ref, slots, width) for ref in (first, second)], 0)
+    back = jnp.concatenate([slot_rows(ref, slots, width) for ref in (first_back, second_back)], 0)
+    tail = slots * (width // 128)
+    columns = [ref[chip, tail:, :] for ref in (first_back, second_back) for chip in range(chips)]
+    step = columns[0].shape[0]
+    columns = jnp.concatenate(columns, 0)
     key = jnp.concatenate([keys[0:1, :], keys[1:2, :]], 1)
     down = jnp.broadcast_to(key, (128, 2 * span)).T
-    down = jnp.where(down < 0.0, -2.0, down)
     same = jnp.concatenate([hot(down == key[:, base : base + 128]) for base in range(0, 2 * span, 128)], 1)
     agg = mm(same, forward)
     act = (agg * sigmoid(agg)).astype(BF)
     shape = (width, 128)
     mine = hot((iota(shape, 0) == block * me + iota(shape, 1)) & (iota(shape, 1) < block))
+    for copy in copies:
+        copy.wait()
     node_cols = mm(node_w[...], mine).astype(BF)
     both = mm(act, jnp.concatenate([node_cols, mine], 1))
-    pieces = [gathered_rows(piece, chips, rows, core, cap, (span, 1), 0) for piece in range(2)]
-    band, slot, owner = [jnp.concatenate([a, b], 0) for a, b in zip(*pieces)]
-    number = cap * band + slot % cap
+    pieces = [gathered_slots(piece, chips, core, cap, (span, 1), 0) for piece in range(2)]
+    band, owner, turn = [jnp.concatenate([a, b], 0) for a, b in zip(*pieces)]
     source = jnp.where(lax.rem(owner, 2) == core, 0, chips) + lax.div(owner, 2)
-    at = jnp.where(slot < slots, source * TAIL + TAIL - 2 * cap + lax.div(number, chips), -1)
-    tails = jnp.concatenate(
-        [ref[chip, slots:, :] for ref in (first_back, second_back) for chip in range(chips)], 0
-    )
-    shape = (2 * span, tails.shape[0])
-    wide = mm(hot(iota(shape, 1) == at), tails)
-    shape = (2 * span, width)
-    wide = jnp.where(lax.div(iota(shape, 1), 2 * block) == lax.rem(number, chips), wide, 0.0).astype(BF)
-    shape = (width, 128)
-    fold = hot((iota(shape, 0) % (2 * block) == block * core + iota(shape, 1)) & (iota(shape, 1) < block))
-    hmesh = (both[:, :128] + mm(wide, fold)).astype(BF)
+    number = cap * band + turn
+    at = lax.div(number, step) * (owners * step) + source * step + lax.rem(number, step)
+    shape = (128, 128)
+    folded = []
+    for base in range(0, 128, 2 * block):
+        fold = hot((iota(shape, 0) == base + block * core + iota(shape, 1)) & (iota(shape, 1) < block))
+        folded.append(mm(columns, fold).astype(BF))
+    latent = mm(hot(iota((2 * span, 2 * span), 1) == at), jnp.concatenate(folded, 0))
+    hmesh = (both[:, :128] + latent).astype(BF)
     left = jnp.concatenate([hmesh, both[:, 128:].astype(BF)], 1)
     sums = mm(left, back, TN)
     dec_out[...] = sums[:block]
@@ -439,9 +538,6 @@
     high = lead.astype(BF)
     low = (lead - high.astype(F32)).astype(BF)
     node_out[...] = mm(high, dec_w[...], NT) + mm(low, dec_w[...], NT)
-    shape = (8, 2 * span)
-    index = lax.rem(iota(shape, 1), rows)
-    feat_out[...] = mm(hot((index == slots + iota(shape, 0)) & (iota(shape, 0) < feats)), back)
     mesh = mesh_out.shape[0]
     shape = (mesh, 2 * span)
     own = (me * mesh_rows + iota(shape, 0)).astype(F32)
@@ -453,21 +549,25 @@
 
 SMEM = pl.BlockSpec(memory_space=pltpu.SMEM)
 VMEM = pl.BlockSpec(memory_space=pltpu.VMEM)
-
-
-def kernel_call(body, name, scalars, arrays, outs, scratch, flops, limit):
+FAR = pl.BlockSpec(memory_space=pltpu.HBM)
+
+
+def kernel_call(body, name, scalars, near, far, outs, scratch, flops, limit, out_specs=None):
     shapes = [jax.ShapeDtypeStruct(shape, dtype) for shape, dtype in outs]
-    moved = sum(a.size * a.dtype.itemsize for a in arrays) + sum(s.size * s.dtype.itemsize for s in shapes)
+    moved = sum(a.size * a.dtype.itemsize for a in (*near, *far)) + sum(s.size * s.dtype.itemsize for s in shapes)
+    buffers = [pltpu.VMEM(a.shape, a.dtype) for a in far]
+    if far:
+        buffers.append(pltpu.SemaphoreType.DMA((len(far),)))
     return pl.pallas_call(
         body,
         name=name,
         out_shape=shapes,
-        in_specs=[SMEM] * len(scalars) + [VMEM] * len(arrays),
-        out_specs=[VMEM] * len(shapes),
-        scratch_shapes=scratch,
+        in_specs=[SMEM] * len(scalars) + [VMEM] * len(near) + [FAR] * len(far),
+        out_specs=out_specs or [VMEM] * len(shapes),
+        scratch_shapes=[*scratch, *buffers],
         compiler_params=pltpu.CompilerParams(vmem_limit_bytes=limit * MIB),
         cost_estimate=pl.CostEstimate(flops=flops, bytes_accessed=moved, transcendentals=0),
-    )(*scalars, *arrays)
+    )(*scalars, *near, *far)
 
 
 def gather_plan(
@@ -496,8 +596,9 @@
     edges = enc_sender.shape[0]
     feats = enc_feat.shape[0]
     block = width // owners
-    rows = slots + TAIL
-    span = chips * rows
+    span = chips * slots
+    parts = width // 128
+    share = width // chips
     groups = [[core + 2 * chip for chip in range(chips)] for core in range(2)]
     swap = [(index, index ^ 1) for index in range(owners)]
     place = lax.axis_index("lat").astype(jnp.int32).reshape(1)
@@ -506,81 +607,106 @@
         first = lax.all_to_all(message, "lat", 0, 0, tiled=True, axis_index_groups=groups)
         return first, lax.ppermute(first, "lat", swap)
 
-    served_ids = serve_rows.reshape(1, slots)
-    served = jnp.take(mesh_latent, served_ids[0], axis=0)
-    id_row = jnp.zeros((1, width), jnp.int32)
-    id_row = lax.dynamic_update_slice(id_row, served_ids // 256, (0, 0))
-    id_row = lax.dynamic_update_slice(id_row, served_ids % 256, (0, 128))
-    own_rows = served.reshape(chips, 2 * cap, width)
-    id_rows = jnp.broadcast_to(id_row.astype(BF)[None], (chips, 1, width))
-    extra = jnp.concatenate([own_rows, id_rows, jnp.zeros((chips, TAIL - 2 * cap - 1, width), BF)], 1)
-    columns = served.reshape(slots, chips, 2 * block).transpose(1, 0, 2).reshape(chips, 2 * cap, width)
-
     send = enc_sender.reshape(1, edges)
     receive = enc_receiver.reshape(1, edges)
-    message, slope = kernel_call(
-        encoder_kernel,
+    message, slope, served = kernel_call(
+        lambda *refs: encoder_kernel(cap, *refs),
         "encoder",
         [enc_count],
-        [grid_latent, enc_proj, send, receive, enc_feat, enc_feat_w, extra],
-        [((chips, rows, width), BF), ((edges, width), BF)],
-        [pltpu.VMEM((grid_rows, width), BF)],
+        [],
+        [grid_latent, enc_proj, mesh_latent, send, receive, enc_feat, enc_feat_w.T, serve_rows[0].T],
+        [((chips, parts * (slots + 8) + 8, 128), BF), ((edges, width), BF), ((slots, width), BF)],
+        [
+            pltpu.VMEM((grid_rows, width), BF),
+            pltpu.VMEM((edges, grid_rows), BF),
+            pltpu.VMEM((edges, width), BF),
+            pltpu.SemaphoreType.DMA((edges // math.gcd(edges, 512),)),
+        ],
         2 * edges * grid_rows * width,
-        32,
+        60,
+        [VMEM, FAR, VMEM],
     )
     first, second = gather(message)
-    message, keys, same, agg_slope = kernel_call(
+    message, keys, same, agg_slope, dec_grad = kernel_call(
         lambda *refs: decoder_kernel(cap, mesh_rows, *refs),
         "decoder",
         [place],
-        [first, second, node_proj, dec_proj, dec_sender, dec_feat, dec_feat_w, grid_cotangent, columns],
-        [((chips, rows, width), BF), ((2, span), F32), ((2, slots, span), BF), ((slots, width), F32)],
+        [first, second, served],
+        [node_proj, dec_proj, dec_sender, dec_feat, dec_feat_w.T, grid_cotangent],
+        [
+            ((chips, parts * slots + slots * share // 128, 128), BF),
+            ((2, span), F32),
+            ((2, slots, span), BF),
+            ((slots, width), F32),
+            ((8, width), F32),
+        ],
         [],
         24 * grid_rows * 128 * width,
-        32,
+        20,
     )
     first_back, second_back = gather(message)
-    wide = width + 128
     term_rows = -(-6 * feats // 16) * 16
     dpx, keep, give = kernel_call(
         backward_kernel,
         "backward",
         [place, enc_count],
-        [first_back, second_back, same, agg_slope, node_proj, dec_proj, send, receive, enc_feat, slope, grid_latent],
-        [((grid_rows, width), BF), ((chips, block, wide), F32), ((chips, block, wide), BF)],
+        [first_back, second_back, same, agg_slope, dec_grad],
+        [node_proj, dec_proj, send, receive, enc_feat, grid_latent, slope],
+        [((grid_rows, width), BF), ((chips, parts * block + 8, 128), F32), ((chips, parts * block + 8, 128), BF)],
         [
             pltpu.VMEM((grid_rows + term_rows, edges), BF),
             pltpu.VMEM((edges, width), BF),
-            pltpu.VMEM((width, wide), F32),
+            pltpu.VMEM((width, width), F32),
         ],
         2 * edges * grid_rows * width,
-        32,
-    )
-    pair = (keep + lax.ppermute(give, "lat", swap).astype(F32)).astype(BF)
+        24,
+    )
+    given = lax.ppermute(give, "lat", swap)
+    (grid_grad,) = kernel_call(
+        grid_kernel,
+        "grid",
+        [],
+        [dpx],
+        [enc_proj, grid_cotangent],
+        [((grid_rows, width), BF)],
+        [],
+        2 * grid_rows * width * width,
+        16,
+    )
+    given, grid_grad = lax.optimization_barrier((given, grid_grad))
+    (pair,) = kernel_call(pair_kernel, "pair", [], [keep, given], [], [(give.shape, BF)], [], keep.size, 8)
+    pair, keys = lax.optimization_barrier((pair, keys))
     arrived = lax.all_to_all(pair, "lat", 0, 0, tiled=True, axis_index_groups=groups)
-    mesh_grad, dec_proj_grad, node_proj_grad, dec_feat_sum = kernel_call(
-        lambda *refs: weight_kernel(cap, mesh_rows, feats, *refs),
+    mesh_grad, dec_proj_grad, node_proj_grad = kernel_call(
+        lambda *refs: weight_kernel(cap, mesh_rows, *refs),
         "weights",
         [place],
-        [first, second, first_back, second_back, keys, node_proj, dec_proj],
-        [((mesh_rows, width), BF), ((block, width), F32), ((block, width), F32), ((8, width), F32)],
+        [first, second, first_back, second_back, keys],
+        [node_proj, dec_proj],
+        [((mesh_rows, width), BF), ((block, width), F32), ((block, width), F32)],
         [],
         2 * (2 * span) * (2 * span) * width,
-        32,
-    )
-    grid_grad = (
-        grid_cotangent.astype(F32) + lax.dot_general(dpx, enc_proj, NT, preferred_element_type=F32)
-    ).astype(BF)
-    total = jnp.sum(arrived.astype(F32), axis=0)
-    dec_feat_w_grad = lax.dynamic_slice(dec_feat_sum, (0, place[0] * block), (feats, block)).T
+        24,
+    )
+    enc_proj_grad, enc_feat_grad, dec_feat_grad = kernel_call(
+        lambda *refs: final_kernel(feats, *refs),
+        "final",
+        [],
+        [arrived],
+        [],
+        [((block, width), F32), ((feats, block), F32), ((feats, block), F32)],
+        [],
+        arrived.size,
+        8,
+    )
     return (
         grid_grad,
         mesh_grad,
-        total[:, :width],
+        enc_proj_grad,
         node_proj_grad,
         dec_proj_grad,
-        total[:, width : width + feats],
-        dec_feat_w_grad,
+        enc_feat_grad.T,
+        dec_feat_grad.T,
     )
 
 
@@ -588,11 +714,15 @@
     mesh_latent, serve_rows = args[1], args[9]
     owners, cap = serve_rows.shape[1], serve_rows.shape[2]
     width = mesh_latent.shape[1]
+    chips = owners // 2
     return (
-        owners * cap <= 128
-        and owners % 8 == 0
-        and cap == 4
-        and width % (128 * owners // 8) == 0
+        owners % 2 == 0
+        and 2 * cap == 8
+        and owners * cap <= 64
+        and width % 128 == 0
+        and width % (8 * owners) == 0
+        and 128 % (width // chips) == 0
+        and owners * cap * (width // chips) % 2048 == 0
         and mesh_latent.shape[0] <= 65536
         and mesh_latent.shape[0] * owners < 1 << 24
         and args[0].shape[0] % 128 == 0

time: 104 us -> 88.2 us (0.85)
  local copies, waits for them, and re-layouts: 18.6 us -> 2.98 us
  Pallas kernels: 24.7 us -> 29.9 us
  other arithmetic: 2.12 us -> 0 us
  blocking collectives: 45.8 us -> 43.8 us
  matrix products: 1.71 us -> 0 us
    unnamed x60 -> x34, local copies, waits for them, and re-layouts: 15.8 us -> 2.98 us
    pallas_call x4 -> x7, Pallas kernels: 24.7 us -> 29.9 us  [kernel_call(): pl.pallas_call(body, name=name, out_shape=shapes, in_specs=[SMEM] * len(s...]
    all_to_all x2, blocking collectives: 45.8 us -> 43.8 us  [gather(): lax.all_to_all(message, 'lat', 0, 0, tiled=True, axis_index_groups=groups)]
    all_to_all x1, waiting for transfers between devices: 0.01 us -> 1.9 us  [gather_plan(): lax.all_to_all(pair, 'lat', 0, 0, tiled=True, axis_index_groups=groups)]
    ppermute x1, waiting for transfers between devices: 1.83 us -> 0.01 us  [gather_plan(): given = lax.ppermute(give, 'lat', swap)]
    convert_element_type x2 -> x0, other arithmetic: 1.79 us -> none  [the longest x1 1.77 us: gather_plan(): pair = (keep + lax.ppermute(give, 'lat', swap).astype(F32)).astype(BF)]
    dot_general x1 -> x0, matrix products: 1.71 us -> none  [gather_plan(): lax.dot_general(dpx, enc_proj, NT, preferred_element_type=F32)]
  transfers between devices with their start and end apart: 4 -> 4, of which waited for: 3 -> 3; matrix products, arithmetic and copies ran while one was open for 3% -> 0% of each run, Pallas kernels for 6% -> 9%
where the time goes in v2:
time: 88.2 us; the launch traced here: 87.8 us
  blocking collectives  43.8 us (50%)
  Pallas kernels  29.9 us (34%)
  waiting for transfers between devices  5.93 us (7%)
  starting transfers between devices  3.64 us (4%)
  local copies, waits for them, and re-layouts  2.98 us (3%)
  between operations  1.51 us (2%)
    all_to_all x2, blocking collectives, gather(): lax.all_to_all(message, 'lat', 0, 0, tiled=True, axis_index_groups=groups)  43.8 us
    pallas_call x7, Pallas kernels, kernel_call(): pl.pallas_call(body, name=name, out_shape=shapes, in_specs=[SMEM] * len(s...  29.9 us
    ppermute x2, waiting for transfers between devices, gather(): return (first, lax.ppermute(first, 'lat', swap))  4.03 us
    all_to_all x1, starting transfers between devices, gather_plan(): lax.all_to_all(pair, 'lat', 0, 0, tiled=True, axis_index_groups=groups)  3.42 us
    unnamed x34, local copies, waits for them, and re-layouts  2.98 us
    all_to_all x1, waiting for transfers between devices, gather_plan(): lax.all_to_all(pair, 'lat', 0, 0, tiled=True, axis_index_groups=groups)  1.9 us
  transfers between devices with their start and end apart: 4, of which 3 were waited for; matrix products, arithmetic and copies ran while one was open for 0% of the time, Pallas kernels for 9%

profile of v2, /device:TPU:0, one launch (start us, length us, event | category | flops | bytes accessed | tf_op | source)
XLA Modules:
  0.0 87.8 jit_solution(383968311339015191)
XLA Ops:
  1.3 0.0 copy-start
  1.3 0.0 copy-start.3
  1.3 0.0 copy-start.6
  1.3 0.0 copy-start.9
  1.3 0.0 copy-start.11
  1.3 0.0 copy-start.12
  1.3 9.2 %encoder.1 = (bf16[8,296,128]{2,1,0:T(8,128)(2,1)}, bf16[2048,512]{1,0:T(8,128)(2,1)}, bf16[64,512]{1,0:T(8,128)(2,1)}) custom-call(s32[1]{0:T(128)S(6)} %copy.22.refs_0_.count, bf16[1024,512]{1,0:T(8,128)(2,1)} %latent_any.1, bf16[512,512]{1,0:T(8,128)(2,1)} %weight_any.1, bf16[320,512]{1,0:T(8,128)(2,1)} %refs_3_.1, s32[1,2048]{1,0:T(1,128)} %bitcast.11, ...), custom_call_target="tpu_custom_call" | custom-call | flops 2147483648 | bytes 4727040 | tf_op jit(solution)/shard_map/encoder/pallas_call | solution.py:561
  10.6 24.1 %all_to_all.15.refs_1_ = bf16[8,296,128]{2,1,0:T(8,128)(2,1)S(1)} all-to-all(bf16[8,296,128]{2,1,0:T(8,128)(2,1)} %get-tuple-element.28), channel_id=1, replica_groups={{0,2,4,6,8,10,12,14},{1,3,5,7,9,11,13,15},{16,18,20,22,24,26,28,30},{17..., dimensions={0} | all-to-all | bytes 1212416 | tf_op jit(solution)/shard_map/all_to_all | solution.py:607
  34.7 0.0 collective-permute-start
  34.7 2.0 %collective-permute-done.refs_2_ = bf16[8,296,128]{2,1,0:T(8,128)(2,1)S(1)} collective-permute-done((bf16[8,296,128]{2,1,0:T(8,128)(2,1)S(1)}, bf16[8,296,128]{2,1,0:T(8,128)(2,1)S(1)}, u32[]{:S(2)}, u32[]{:S(2)}) %collective-permute-start) | collective-permute-done | bytes 606240 | tf_op jit(solution)/shard_map/ppermute | solution.py:608
  36.7 0.0 copy-done
  36.7 0.0 copy-done.3
  36.7 0.0 copy-done.6
  36.7 0.0 copy-done.9
  36.7 0.0 copy-done.11
  36.7 0.0 copy-done.12
  36.7 0.0 copy-start.16
  36.8 0.8 copy-done.16
  37.6 0.0 copy-start.2
  37.6 0.0 copy-start.4
  37.6 0.0 copy-start.13
  37.6 0.0 copy-start.14
  37.6 0.0 copy-start.15
  37.6 5.9 %decoder.1 = (bf16[8,288,128]{2,1,0:T(8,128)(2,1)S(1)}, f32[2,512]{1,0:T(2,128)S(1)}, bf16[2,64,512]{2,1,0:T(8,128)(2,1)S(1)}, f32[64,512]{1,0:T(8,128)S(1)}, f32[8,512]{1,0:T(8,128)S(1)}) custom-call(s32[1]{0:T(128)} %bitcast.refs_0_.place, bf16[8,296,128]{2,1,0:T(8,128)(2,1)S(1)} %all_to_all.15.refs_1_, ...), custom_call_target="tpu_custom_call" | custom-call | flops 1610612736 | bytes 4317184 | tf_op jit(solution)/shard_map/decoder/pallas_call | solution.py:561
  43.5 19.6 %all_to_all.16.first.refs_3_ = bf16[8,288,128]{2,1,0:T(8,128)(2,1)S(1)} all-to-all(bf16[8,288,128]{2,1,0:T(8,128)(2,1)S(1)} %get-tuple-element.30), channel_id=1, replica_groups={{0,2,4,6,8,10,12,14},{1,3,5,7,9,11,13,15},{16,18,20,22,24,26,28,30},{17..., dimensions={0} | all-to-all | bytes 1179648 | tf_op jit(solution)/shard_map/all_to_all | solution.py:607
  63.1 0.0 collective-permute-start.1
  63.1 2.0 %collective-permute-done.1.second.refs_4_ = bf16[8,288,128]{2,1,0:T(8,128)(2,1)S(1)} collective-permute-done((bf16[8,288,128]{2,1,0:T(8,128)(2,1)S(1)}, bf16[8,288,128]{2,1,0:T(8,128)(2,1)S(1)}, u32[]{:S(2)}, u32[]{:S(2)}) %collective-permute-start.1) | collective-permute-done | bytes 589856 | tf_op jit(solution)/shard_map/ppermute | solution.py:608
  65.1 0.0 copy-done.2
  65.1 0.0 copy-done.4
  65.1 0.0 copy-done.7
  65.2 0.0 copy-done.10
  65.2 0.0 copy-done.13
  65.2 0.0 copy-done.14
  65.2 0.0 copy-done.15
  65.2 0.0 copy-start.1
  65.2 5.7 %backward.1 = (bf16[1024,512]{1,0:T(8,128)(2,1)S(1)}, f32[8,136,128]{2,1,0:T(8,128)S(1)}, bf16[8,136,128]{2,1,0:T(8,128)(2,1)S(1)}) custom-call(s32[1]{0:T(128)} %bitcast.refs_0_.place, s32[1]{0:T(128)S(6)} %copy.22.refs_0_.count, bf16[8,288,128]{2,1,0:T(8,128)(2,1)S(1)} %all_to_all.16.first.refs_3_, ...), custom_call_target="tpu_custom_call" | custom-call | flops 2147483648 | bytes 7585792 | tf_op jit(solution)/shard_map/backward/pallas_call | solution.py:561
  70.9 0.2 collective-permute-start.2
  71.1 0.0 copy-done.1
  71.1 1.8 %grid.1 = bf16[1024,512]{1,0:T(8,128)(2,1)} custom-call(bf16[1024,512]{1,0:T(8,128)(2,1)S(1)} %get-tuple-element.36.dpx, bf16[512,512]{1,0:T(8,128)(2,1)S(1)} %copy-done.1, bf16[1024,512]{1,0:T(8,128)(2,1)S(1)} %copy-done), custom_call_target="tpu_custom_call" | custom-call | flops 536870912 | bytes 3670016 | tf_op jit(solution)/shard_map/grid/pallas_call | solution.py:561
  73.0 0.0 collective-permute-done.2.given
  73.0 0.8 pair.1
  73.7 3.4 %all-to-all-start.2 = ((bf16[8,136,128]{2,1,0:T(8,128)(2,1)}), bf16[8,136,128]{2,1,0:T(8,128)(2,1)S(1)}, u32[]{:S(2)}, u32[]{:S(2)}) async-start(bf16[8,136,128]{2,1,0:T(8,128)(2,1)} %pair.1), calls=%async_computation.2 | async-start | bytes 557056 | tf_op jit(solution)/shard_map/all_to_all | solution.py:679
  77.2 0.0 copy-start.5
  77.2 1.0 %copy-done.5 = bf16[512,512]{1,0:T(8,128)(2,1)S(1)} copy-done((bf16[512,512]{1,0:T(8,128)(2,1)S(1)}, bf16[512,512]{1,0:T(8,128)(2,1)}, u32[]{:S(2)}) %copy-start.5) | copy-done | bytes 524312
  78.2 1.0 %copy-done.8 = bf16[512,512]{1,0:T(8,128)(2,1)S(1)} copy-done((bf16[512,512]{1,0:T(8,128)(2,1)S(1)}, bf16[512,512]{1,0:T(8,128)(2,1)}, u32[]{:S(2)}) %copy-start.8) | copy-done | bytes 524312
  79.2 5.9 %weights.1 = (bf16[320,512]{1,0:T(8,128)(2,1)}, f32[32,512]{1,0:T(8,128)}, f32[32,512]{1,0:T(8,128)}) custom-call(s32[1]{0:T(128)} %bitcast.refs_0_.place, bf16[8,296,128]{2,1,0:T(8,128)(2,1)S(1)} %all_to_all.15.refs_1_, bf16[8,296,128]{2,1,0:T(8,128)(2,1)S(1)} %collective-permute-done.refs_2_, bf16[8,288,128]{2,1,0:T(8,128)(2,1)S(1)} %all_to_all.16.first.refs_3_, ...), custom_call_target="tpu_custom_call" | custom-call | flops 1073741824 | bytes 3903488 | tf_op jit(solution)/shard_map/weights/pallas_call | solution.py:561
  85.2 1.9 %all-to-all-done.2.refs_0_ = bf16[8,136,128]{2,1,0:T(8,128)(2,1)S(1)} async-done(((bf16[8,136,128]{2,1,0:T(8,128)(2,1)}), bf16[8,136,128]{2,1,0:T(8,128)(2,1)S(1)}, u32[]{:S(2)}, u32[]{:S(2)}) %all-to-all-start.2) | async-done | bytes 278560 | tf_op jit(solution)/shard_map/all_to_all | solution.py:679
  87.1 0.7 final.1
  (3 shorter events, 0.0 us)
Async XLA Ops:
  1.3 35.4 %copy-start = (bf16[1024,512]{1,0:T(8,128)(2,1)S(1)}, bf16[1024,512]{1,0:T(8,128)(2,1)}, u32[]{:S(2)}) copy-start(bf16[1024,512]{1,0:T(8,128)(2,1)} %cot_any.1) | copy-start | bytes 3145732
  1.3 35.4 %copy-start.3 = (bf16[512,512]{1,0:T(8,128)(2,1)S(1)}, bf16[512,512]{1,0:T(8,128)(2,1)}, u32[]{:S(2)}) copy-start(bf16[512,512]{1,0:T(8,128)(2,1)} %refs_6_.5) | copy-start | bytes 1572868
  1.3 35.4 %copy-start.6 = (bf16[512,512]{1,0:T(8,128)(2,1)S(1)}, bf16[512,512]{1,0:T(8,128)(2,1)}, u32[]{:S(2)}) copy-start(bf16[512,512]{1,0:T(8,128)(2,1)} %refs_7_.3) | copy-start | bytes 1572868
  1.3 35.4 %copy-start.9 = (f32[3,4,1024]{2,1,0:T(4,128)S(1)}, f32[3,4,1024]{2,1,0:T(4,128)}, u32[]{:S(2)}) copy-start(f32[3,4,1024]{2,1,0:T(4,128)} %refs_7_.2) | copy-start | bytes 147460
  1.3 35.4 %copy-start.11 = (s32[3,1024]{1,0:T(4,128)S(1)}, s32[3,1024]{1,0:T(4,128)}, u32[]{:S(2)}) copy-start(s32[3,1024]{1,0:T(4,128)} %refs_6_.4) | copy-start | bytes 36868
  1.3 35.4 %copy-start.12 = (f32[512,4]{0,1:T(4,128)S(1)}, f32[512,4]{0,1:T(4,128)}, u32[]{:S(2)}) copy-start(f32[512,4]{0,1:T(4,128)} %param.29) | copy-start | bytes 24580
  34.7 2.0 %collective-permute-start = (bf16[8,296,128]{2,1,0:T(8,128)(2,1)S(1)}, bf16[8,296,128]{2,1,0:T(8,128)(2,1)S(1)}, u32[]{:S(2)}, u32[]{:S(2)}) collective-permute-start(bf16[8,296,128]{2,1,0:T(8,128)(2,1)S(1)} %all_to_all.15.refs_1_), channel_id=1, source_target_pairs={{0,1},{1,0},{2,3},{3,2},{4,5},{5,4},{6,7},{7,6},{8,9},{9,8},{10,11... | collective-permute-start | bytes 1818632 | tf_op jit(solution)/shard_map/ppermute | solution.py:608
  36.7 0.8 copy-start.16
  37.6 27.6 %copy-start.2 = (bf16[1024,512]{1,0:T(8,128)(2,1)S(1)}, bf16[1024,512]{1,0:T(8,128)(2,1)}, u32[]{:S(2)}) copy-start(bf16[1024,512]{1,0:T(8,128)(2,1)} %latent_any.1) | copy-start | bytes 3145732
  37.6 27.6 %copy-start.4 = (bf16[512,512]{1,0:T(8,128)(2,1)S(1)}, bf16[512,512]{1,0:T(8,128)(2,1)}, u32[]{:S(2)}) copy-start(bf16[512,512]{1,0:T(8,128)(2,1)} %refs_6_.5) | copy-start | bytes 1572868
  37.6 27.6 %copy-start.7 = (bf16[512,512]{1,0:T(8,128)(2,1)S(1)}, bf16[512,512]{1,0:T(8,128)(2,1)}, u32[]{:S(2)}) copy-start(bf16[512,512]{1,0:T(8,128)(2,1)} %refs_7_.3) | copy-start | bytes 1572868
  37.6 27.6 %copy-start.10 = (f32[4,2048]{1,0:T(4,128)S(1)}, f32[4,2048]{1,0:T(4,128)}, u32[]{:S(2)}) copy-start(f32[4,2048]{1,0:T(4,128)} %feat_any.1) | copy-start | bytes 98308
  37.6 27.6 %copy-start.13 = (s32[2048]{0:T(1024)S(1)}, s32[2048]{0:T(1024)}, u32[]{:S(2)}) copy-start(s32[2048]{0:T(1024)} %param.18) | copy-start | bytes 24580
  37.6 27.6 %copy-start.14 = (s32[2048]{0:T(1024)S(1)}, s32[2048]{0:T(1024)}, u32[]{:S(2)}) copy-start(s32[2048]{0:T(1024)} %param.19) | copy-start | bytes 24580
  37.6 27.6 %copy-start.15 = (bf16[2048,512]{1,0:T(8,128)(2,1)S(1)}, bf16[2048,512]{1,0:T(8,128)(2,1)}, u32[]{:S(2)}) copy-start(bf16[2048,512]{1,0:T(8,128)(2,1)} %get-tuple-element.34.slope_any) | copy-start | bytes 6291460
  63.1 2.0 %collective-permute-start.1 = (bf16[8,288,128]{2,1,0:T(8,128)(2,1)S(1)}, bf16[8,288,128]{2,1,0:T(8,128)(2,1)S(1)}, u32[]{:S(2)}, u32[]{:S(2)}) collective-permute-start(bf16[8,288,128]{2,1,0:T(8,128)(2,1)S(1)} %all_to_all.16.first.refs_3_), channel_id=1, source_target_pairs={{0,1},{1,0},{2,3},{3,2},{4,5},{5,4},{6,7},{7,6},{8,9},{9,8},{10,11... | collective-permute-start | bytes 1769480 | tf_op jit(solution)/shard_map/ppermute | solution.py:608
  65.2 5.9 %copy-start.1 = (bf16[512,512]{1,0:T(8,128)(2,1)S(1)}, bf16[512,512]{1,0:T(8,128)(2,1)}, u32[]{:S(2)}) copy-start(bf16[512,512]{1,0:T(8,128)(2,1)} %weight_any.1) | copy-start | bytes 1572868
  70.9 2.1 %collective-permute-start.2 = (bf16[8,136,128]{2,1,0:T(8,128)(2,1)S(1)}, bf16[8,136,128]{2,1,0:T(8,128)(2,1)S(1)}, u32[]{:S(2)}, u32[]{:S(2)}) collective-permute-start(bf16[8,136,128]{2,1,0:T(8,128)(2,1)S(1)} %get-tuple-element.35), channel_id=1, source_target_pairs={{0,1},{1,0},{2,3},{3,2},{4,5},{5,4},{6,7},{7,6},{8,9},{9,8},{10,11... | collective-permute-start | bytes 835592 | tf_op jit(solution)/shard_map/ppermute | solution.py:664
  73.7 13.4 %all-to-all-start.2 = ((bf16[8,136,128]{2,1,0:T(8,128)(2,1)}), bf16[8,136,128]{2,1,0:T(8,128)(2,1)S(1)}, u32[]{:S(2)}, u32[]{:S(2)}) async-start(bf16[8,136,128]{2,1,0:T(8,128)(2,1)} %pair.1), calls=%async_computation.2 | async-start | bytes 557056 | tf_op jit(solution)/shard_map/all_to_all | solution.py:679
  77.2 1.0 %copy-start.5 = (bf16[512,512]{1,0:T(8,128)(2,1)S(1)}, bf16[512,512]{1,0:T(8,128)(2,1)}, u32[]{:S(2)}) copy-start(bf16[512,512]{1,0:T(8,128)(2,1)} %refs_6_.5) | copy-start | bytes 1572868
  78.2 1.0 %copy-start.8 = (bf16[512,512]{1,0:T(8,128)(2,1)S(1)}, bf16[512,512]{1,0:T(8,128)(2,1)}, u32[]{:S(2)}) copy-start(bf16[512,512]{1,0:T(8,128)(2,1)} %refs_7_.3) | copy-start | bytes 1572868

commit v3 on v2

--- a/solution.py
+++ b/solution.py
@@ -184,8 +184,11 @@
     return lax.broadcasted_iota(jnp.int32, shape, dim)
 
 
-def sigmoid(value):
-    return 0.5 * jnp.tanh(0.5 * value) + 0.5
+def halves(value):
+    turn = jnp.tanh(value)
+    up = 1.0 + turn
+    silu = value * up
+    return silu, up + silu * (1.0 - turn)
 
 
 def hot(mask):
@@ -199,17 +202,15 @@
     return high, middle, rest - middle
 
 
+def stack_rows(feats):
+    return -(-6 * feats // 16) * 16
+
+
 def stack_terms(value, order):
-    feats = value.shape[0]
-    rows = -(-6 * feats // 16) * 16
-    pick = (iota((rows, feats), 0) % feats == iota((rows, feats), 1)).astype(F32)
-    spread = mm(pick, value, precision=HI)
-    parts = split3(spread)
-    group = iota(spread.shape, 0) // feats
-    out = jnp.zeros_like(spread)
-    for index, which in enumerate(order):
-        out = jnp.where(group == index, parts[which], out)
-    return out.astype(BF)
+    parts = split3(value)
+    rows = len(order) * value.shape[0]
+    blank = jnp.zeros((stack_rows(value.shape[0]) - rows, value.shape[1]), F32)
+    return jnp.concatenate([*(parts[which] for which in order), blank], 0)
 
 
 FEAT_ORDER = (0, 0, 1, 1, 2, 0)
@@ -224,48 +225,57 @@
 
 
 def feature_grad(terms, feats):
-    pick = iota((8, terms.shape[0]), 1)
-    row = iota((8, terms.shape[0]), 0)
-    want = (pick % feats == row) & (row < feats)
-    want = want & ((pick // feats == 0) | (pick // feats == 2) | (pick // feats == 4))
-    return mm(want.astype(F32), terms, precision=HI)
+    total = terms[: 2 * feats] + terms[2 * feats : 4 * feats] + terms[4 * feats : 6 * feats]
+    return jnp.where(iota(total.shape, 0) < feats, total, 0.0)
 
 
 def encoder_kernel(
     cap, count, latent_any, weight_any, mesh_any, send_any, receive_any, feat_any, feat_w_any, serve_any,
     message, slope_far, served_out, px, picks, slope, slope_sems,
-    latent, weight, mesh, send, receive, feat, feat_w, serve, sems,
+    latent, weight, mesh, send, receive, feat, feat_w, serve, sems, latent_sems,
 ):
-    sources = (send_any, latent_any, weight_any, feat_any, feat_w_any, receive_any, mesh_any, serve_any)
-    targets = (send, latent, weight, feat, feat_w, receive, mesh, serve)
-    copies = fetch(sources, targets, sems)
+    sources = (send_any, feat_any, weight_any, feat_w_any, receive_any, mesh_any, serve_any)
+    targets = (send, feat, weight, feat_w, receive, mesh, serve)
+    copies = fetch(sources[:3], targets[:3], sems)
     edges = send.shape[1]
     grid_rows, width = latent.shape
     chips = message.shape[0]
     slots = served_out.shape[0]
+    step = math.gcd(grid_rows, 256)
+    cuts = [slice(start, start + step) for start in range(0, grid_rows, step)]
+    chunks = fetch([latent_any.at[cut, :] for cut in cuts], [latent.at[cut, :] for cut in cuts], latent_sems)
+    copies += fetch(sources[3:], targets[3:], sems.at[pl.ds(3, 4)])
     block = math.gcd(edges, 512)
     copies[0].wait()
-    for start in range(0, edges, block):
+    copies[1].wait()
+
+    def build(start):
         part = slice(start, start + block)
         ids = jnp.broadcast_to(send[:, part].astype(F32), (128, block)).T
         for base in range(0, grid_rows, 128):
             lane = (iota((block, 128), 1) + base).astype(F32)
             picks[part, base : base + 128] = hot(ids == lane)
-    copies[1].wait()
+
+    for start in range(0, edges // 2, block):
+        build(start)
     copies[2].wait()
-    px[...] = mm(latent[...], weight[...]).astype(BF)
-    for copy in copies[3:6]:
+    for cut, chunk in zip(cuts, chunks):
+        chunk.wait()
+    px[:grid_rows, :] = (0.5 * mm(latent[...], weight[...]).astype(BF).astype(F32)).astype(BF)
+    for copy in copies[3:5]:
         copy.wait()
-    w_rows = stack_terms(feat_w[...], WEIGHT_ORDER)
+    terms = stack_terms(0.5 * feat_w[...], WEIGHT_ORDER)
+    px[grid_rows:, :] = jnp.concatenate([terms, jnp.zeros((128 - terms.shape[0], width), F32)], 0).astype(BF)
     total = jnp.zeros((slots, width), F32)
     stores = []
     for start in range(0, edges, block):
         part = slice(start, start + block)
-        pre = mm(picks[part, :], px[...])
-        pre = pre + mm(stack_terms(feat[:, part], FEAT_ORDER), w_rows, TN)
-        sig = sigmoid(pre)
-        silu = pre * sig
-        slope[part, :] = (sig + silu * (1.0 - sig)).astype(BF)
+        if start >= edges // 2:
+            build(start)
+        pre = mm(picks[part, :grid_rows], px[:grid_rows, :])
+        pre = pre + mm(stack_terms(feat[:, part], FEAT_ORDER).astype(BF), px[grid_rows : grid_rows + 32, :], TN)
+        silu, double = halves(pre)
+        slope[part, :] = double.astype(BF)
         out = pltpu.make_async_copy(slope.at[part, :], slope_far.at[part, :], slope_sems.at[len(stores)])
         out.start()
         stores.append(out)
@@ -273,8 +283,8 @@
         slot = jnp.where(live, receive[:, part], -1)
         to_slot = hot(iota((slots, block), 0) == slot)
         total = total + mm(to_slot, silu.astype(BF))
+    copies[5].wait()
     copies[6].wait()
-    copies[7].wait()
     owners = slots // cap
     ids = serve[...]
     spread = hot(iota((owners, slots), 0) == lax.div(iota((owners, slots), 1), cap))
@@ -372,12 +382,57 @@
     return keys, same, latent
 
 
+def decoder_picks(
+    after, send_any, feat_any, node_any, dec_any, feat_w_any, cot_any,
+    pick, pick_turned, node_w, dec_w, feat_w, cotangent, send, feat, sems,
+):
+    sources = (send_any, feat_any, node_any, dec_any, feat_w_any, cot_any)
+    copies = fetch(sources, (send, feat, node_w, dec_w, feat_w, cotangent), sems)
+    slots = after.shape[0]
+    grid_rows = send.shape[1]
+    copies[0].wait()
+    copies[1].wait()
+    block = math.gcd(grid_rows, 512)
+    for k in range(3):
+        for start in range(0, grid_rows, block):
+            part = slice(start, start + block)
+            to = slice(k * grid_rows + start, k * grid_rows + start + block)
+            to_slot = jnp.where(iota((slots, block), 0) == send[k : k + 1, part], 1.0, 0.0)
+            rows = jnp.concatenate([to_slot, stack_terms(feat[k, :, part], FEAT_ORDER)], 0)
+            pick[:, to] = rows.astype(BF)
+            rows = jnp.concatenate([rows, jnp.zeros((128 - rows.shape[0], block), F32)], 0)
+            pick_turned[to, :] = rows.T.astype(BF)
+    for copy in copies[2:]:
+        copy.wait()
+
+
+def encoder_picks(
+    count, receive_any, latent_any, dec_any, node_any, send_any, feat_any, slope_any,
+    to_edge, latent_turned, dec_turned, node_turned, send, feat, slope, receive, latent, dec_w, node_w, sems,
+):
+    sources = (receive_any, dec_any, node_any, latent_any, send_any, feat_any, slope_any)
+    copies = fetch(sources, (receive, dec_w, node_w, latent, send, feat, slope), sems)
+    edges = receive.shape[1]
+    copies[0].wait()
+    block = math.gcd(edges, 512)
+    for start in range(0, edges, block):
+        part = slice(start, start + block)
+        live = iota((1, block), 1) + start < count[0]
+        slot = jnp.where(live, receive[:, part], -1)
+        to_edge[part, :] = jnp.where(iota((128, block), 0) == slot, 1.0, 0.0).T.astype(BF)
+    for copy in copies[1:4]:
+        copy.wait()
+    dec_turned[...] = dec_w[...].T
+    node_turned[...] = node_w[...].T
+    latent_turned[...] = latent[...].T
+    for copy in copies[4:]:
+        copy.wait()
+
+
 def decoder_kernel(
-    cap, mesh_rows, place, first, second, extra, node_any, dec_any, send_any, feat_any, feat_w_any, cot_any,
-    message, keys_out, same_out, slope_out, grad_out, node_w, dec_w, send, feat, feat_w, cotangent, sems,
+    cap, mesh_rows, place, first, second, extra, pick, pick_turned, node_w, dec_w, feat_w, cotangent,
+    message, keys_out, same_out, slope_out, grad_out,
 ):
-    sources = (node_any, dec_any, send_any, feat_any, feat_w_any, cot_any)
-    copies = fetch(sources, (node_w, dec_w, send, feat, feat_w, cotangent), sems)
     slots, width = extra.shape
     keys, same, latent = slot_matches(first, second, place[0], cap, mesh_rows, width)
     agg = jnp.zeros((slots, width), F32)
@@ -385,27 +440,24 @@
         keys_out[piece : piece + 1, :] = keys[piece]
         same_out[piece] = same[piece]
         agg = agg + mm(same[piece], slot_rows(ref, slots, width))
-    sig = sigmoid(agg)
-    silu = agg * sig
-    slope_out[...] = sig + silu * (1.0 - sig)
-    for copy in copies:
-        copy.wait()
+    silu, double = halves(0.5 * agg)
+    slope_out[...] = 0.25 * double
     hmesh = (latent + mm(silu.astype(BF), node_w[...])).astype(BF)
     proj = mm(hmesh, dec_w[...]).astype(BF)
-    table = jnp.concatenate([proj, stack_terms(feat_w[...], WEIGHT_ORDER)], 0)
+    rows = pick.shape[0]
+    blank = jnp.zeros((128 - rows, width), F32)
+    terms = jnp.concatenate([stack_terms(0.5 * feat_w[...], WEIGHT_ORDER), blank], 0).astype(BF)
+    table = jnp.concatenate([(0.5 * proj.astype(F32)).astype(BF), terms], 0)
     grid_rows = cotangent.shape[0]
     block = math.gcd(grid_rows, 512)
-    total = jnp.zeros((table.shape[0], width), F32)
+    total = jnp.zeros((rows, width), F32)
     for start in range(0, grid_rows, block):
-        part = slice(start, start + block)
-        cot = cotangent[part, :].astype(F32)
-        for k in range(3):
-            to_slot = hot(iota((slots, block), 0) == send[k : k + 1, part])
-            pick = jnp.concatenate([to_slot, stack_terms(feat[k, :, part], FEAT_ORDER)], 0)
-            pre = mm(pick, table, TN)
-            sig = sigmoid(pre)
-            slope = sig + pre * sig * (1.0 - sig)
-            total = total + mm(pick, (cot * slope).astype(BF))
+        cot = cotangent[start : start + block, :].astype(F32)
+        for base in range(start, 3 * grid_rows, grid_rows):
+            part = slice(base, base + block)
+            double = halves(mm(pick_turned[part, :], table))[1]
+            total = total + mm(pick[:, part], (cot * double).astype(BF))
+    total = 0.5 * total
     half = total[:slots].astype(BF)
     grad_out[...] = feature_grad(total[slots:], feat_w.shape[0])
     chips = message.shape[0]
@@ -419,43 +471,37 @@
 
 
 def backward_kernel(
-    place, count, first, second, same, agg_slope, dec_grad, node_any, dec_any, send_any, receive_any, feat_any,
-    latent_any, slope_any, dpx_out, keep, give, hots, grads, part, node_w, dec_w, send, receive, feat, latent, slope,
-    sems,
+    place, first, second, same, agg_slope, dec_grad, to_edge, latent_turned, dec_turned, node_turned,
+    send, feat, slope, dpx_far, keep, give, grads, part, dpx, dpx_sems,
 ):
-    sources = (send_any, feat_any, receive_any, dec_any, node_any, slope_any, latent_any)
-    copies = fetch(sources, (send, feat, receive, dec_w, node_w, slope, latent), sems)
     slots = same.shape[1]
-    edges = send.shape[1]
-    grid_rows, width = latent.shape
+    edges, width = grads.shape
+    grid_rows = dpx.shape[0]
     feats = feat.shape[0]
     core = lax.rem(place[0], 2)
     dproj = mm(same[0], slot_rows(first, slots, width)) + mm(same[1], slot_rows(second, slots, width))
     high = dproj.astype(BF)
     low = (dproj - high.astype(F32)).astype(BF)
-    for copy in copies[:5]:
-        copy.wait()
-    dhmesh = mm(jnp.concatenate([high, low], 0), dec_w[...], NT)
+    dhmesh = mm(jnp.concatenate([high, low], 0), dec_turned[...])
     mesh_grad = (dhmesh[:slots] + dhmesh[slots:]).astype(BF)
-    dagg = (mm(mesh_grad, node_w[...], NT) * agg_slope[...]).astype(BF)
+    dagg = mm(mesh_grad, node_turned[...]) * agg_slope[...]
+    dagg = jnp.concatenate([dagg, jnp.zeros((128 - slots, width), F32)], 0).astype(BF)
     block = math.gcd(edges, 512)
-    copies[5].wait()
     for start in range(0, edges, block):
         cut = slice(start, start + block)
-        live = iota((1, block), 1) + start < count[0]
-        slot = jnp.where(live, receive[:, cut], -1)
-        upstream = mm(hot(iota((slots, block), 0) == slot), dagg, TN)
-        grads[cut, :] = (upstream * slope[cut, :].astype(F32)).astype(BF)
-        hots[:grid_rows, cut] = hot(iota((grid_rows, block), 0) == send[:, cut])
-        hots[grid_rows:, cut] = stack_terms(feat[:, cut], FEAT_ORDER)
+        grads[cut, :] = (mm(to_edge[cut, :], dagg) * slope[cut, :].astype(F32)).astype(BF)
     step = math.gcd(grid_rows, 256)
+    stores = []
     for start in range(0, grid_rows, step):
         cut = slice(start, start + step)
-        dpx_out[cut, :] = mm(hots[cut, :], grads[...]).astype(BF)
-    enc_grad = feature_grad(mm(hots[grid_rows:, :], grads[...]), feats)
+        from_row = hot(iota((step, edges), 0) + start == send[...])
+        dpx[cut, :] = mm(from_row, grads[...]).astype(BF)
+        out = pltpu.make_async_copy(dpx.at[cut, :], dpx_far.at[cut, :], dpx_sems.at[len(stores)])
+        out.start()
+        stores.append(out)
+    enc_grad = feature_grad(mm(stack_terms(feat[...], FEAT_ORDER).astype(BF), grads[...]), feats)
     sums = jnp.where(iota(enc_grad.shape, 0) < feats, enc_grad, pltpu.roll(dec_grad[...], feats, 0))
-    copies[6].wait()
-    part[...] = mm(latent[...], dpx_out[...], TN)
+    part[...] = mm(latent_turned[...], dpx[...])
     rows = width // (2 * keep.shape[0])
     blank = jnp.zeros((8, 128 - rows), F32)
     for chip in range(keep.shape[0]):
@@ -466,14 +512,16 @@
             pieces = [block[:, base : base + 128] for base in range(0, width, 128)]
             whole = jnp.concatenate([*pieces, jnp.concatenate([small, blank], 1)], 0)
             out[chip] = whole.astype(out.dtype)
+    for out in stores:
+        out.wait()
 
 
 def pair_kernel(keep, given, out):
     out[...] = (keep[...] + given[...].astype(F32)).astype(BF)
 
 
-def grid_kernel(dpx, weight_any, cot_any, out, weight, cotangent, sems):
-    copies = fetch((weight_any, cot_any), (weight, cotangent), sems)
+def grid_kernel(dpx_any, weight_any, cot_any, out, dpx, weight, cotangent, sems):
+    copies = fetch((dpx_any, weight_any, cot_any), (dpx, weight, cotangent), sems)
     for copy in copies:
         copy.wait()
     out[...] = (cotangent[...].astype(F32) + mm(dpx[...], weight[...], NT)).astype(BF)
@@ -489,11 +537,8 @@
     dec_out[...] = total[base + feats : base + 2 * feats, :rows]
 
 
-def weight_kernel(
-    cap, mesh_rows, place, first, second, first_back, second_back, keys, node_any, dec_any,
-    mesh_out, dec_out, node_out, node_w, dec_w, sems,
-):
-    copies = fetch((node_any, dec_any), (node_w, dec_w), sems)
+def act_kernel(cap, mesh_rows, place, first, second, keys, node_any, both_out, turn_out, own_out, node_w, sems):
+    copies = fetch((node_any,), (node_w,), sems)
     width = node_w.shape[0]
     chips = first.shape[0]
     owners = 2 * chips
@@ -503,33 +548,42 @@
     core = lax.rem(me, 2)
     block = width // owners
     forward = jnp.concatenate([slot_rows(ref, slots, width) for ref in (first, second)], 0)
-    back = jnp.concatenate([slot_rows(ref, slots, width) for ref in (first_back, second_back)], 0)
-    tail = slots * (width // 128)
-    columns = [ref[chip, tail:, :] for ref in (first_back, second_back) for chip in range(chips)]
-    step = columns[0].shape[0]
-    columns = jnp.concatenate(columns, 0)
     key = jnp.concatenate([keys[0:1, :], keys[1:2, :]], 1)
     down = jnp.broadcast_to(key, (128, 2 * span)).T
     same = jnp.concatenate([hot(down == key[:, base : base + 128]) for base in range(0, 2 * span, 128)], 1)
     agg = mm(same, forward)
-    act = (agg * sigmoid(agg)).astype(BF)
+    act = halves(0.5 * agg)[0].astype(BF)
     shape = (width, 128)
     mine = hot((iota(shape, 0) == block * me + iota(shape, 1)) & (iota(shape, 1) < block))
-    for copy in copies:
-        copy.wait()
+    copies[0].wait()
     node_cols = mm(node_w[...], mine).astype(BF)
-    both = mm(act, jnp.concatenate([node_cols, mine], 1))
+    both_out[...] = mm(act, jnp.concatenate([node_cols, mine], 1))
+    step = slots * 2 * block // 128
     pieces = [gathered_slots(piece, chips, core, cap, (span, 1), 0) for piece in range(2)]
     band, owner, turn = [jnp.concatenate([a, b], 0) for a, b in zip(*pieces)]
     source = jnp.where(lax.rem(owner, 2) == core, 0, chips) + lax.div(owner, 2)
     number = cap * band + turn
     at = lax.div(number, step) * (owners * step) + source * step + lax.rem(number, step)
+    turn_out[...] = hot(iota((2 * span, 2 * span), 1) == at)
+    own = (me * mesh_rows + iota((own_out.shape[0], 2 * span), 0)).astype(F32)
+    own_out[...] = hot(own == key)
+
+
+def weight_kernel(place, first, second, both, turn, own, dec_turned, mesh_out, dec_out, node_out):
+    width = dec_turned.shape[0]
+    chips = first.shape[0]
+    slots = turn.shape[0] // (2 * chips)
+    block = dec_out.shape[0]
+    core = lax.rem(place[0], 2)
+    back = jnp.concatenate([slot_rows(ref, slots, width) for ref in (first, second)], 0)
+    tail = slots * (width // 128)
+    columns = jnp.concatenate([ref[chip, tail:, :] for ref in (first, second) for chip in range(chips)], 0)
     shape = (128, 128)
     folded = []
     for base in range(0, 128, 2 * block):
         fold = hot((iota(shape, 0) == base + block * core + iota(shape, 1)) & (iota(shape, 1) < block))
         folded.append(mm(columns, fold).astype(BF))
-    latent = mm(hot(iota((2 * span, 2 * span), 1) == at), jnp.concatenate(folded, 0))
+    latent = mm(turn[...], jnp.concatenate(folded, 0))
     hmesh = (both[:, :128] + latent).astype(BF)
     left = jnp.concatenate([hmesh, both[:, 128:].astype(BF)], 1)
     sums = mm(left, back, TN)
@@ -537,14 +591,11 @@
     lead = sums[128 : 128 + block]
     high = lead.astype(BF)
     low = (lead - high.astype(F32)).astype(BF)
-    node_out[...] = mm(high, dec_w[...], NT) + mm(low, dec_w[...], NT)
-    mesh = mesh_out.shape[0]
-    shape = (mesh, 2 * span)
-    own = (me * mesh_rows + iota(shape, 0)).astype(F32)
-    dproj = mm(hot(own == key), back)
+    node_out[...] = mm(high, dec_turned[...]) + mm(low, dec_turned[...])
+    dproj = mm(own[...], back)
     high = dproj.astype(BF)
     low = (dproj - high.astype(F32)).astype(BF)
-    mesh_out[...] = (mm(high, dec_w[...], NT) + mm(low, dec_w[...], NT)).astype(BF)
+    mesh_out[...] = (mm(high, dec_turned[...]) + mm(low, dec_turned[...])).astype(BF)
 
 
 SMEM = pl.BlockSpec(memory_space=pltpu.SMEM)
@@ -552,19 +603,23 @@
 FAR = pl.BlockSpec(memory_space=pltpu.HBM)
 
 
-def kernel_call(body, name, scalars, near, far, outs, scratch, flops, limit, out_specs=None):
+def kernel_call(body, name, scalars, near, far, outs, scratch, flops, limit, out_specs=None, pin=False, last=(), kept=0):
     shapes = [jax.ShapeDtypeStruct(shape, dtype) for shape, dtype in outs]
+    out_specs = out_specs or [VMEM] * len(shapes)
+    pinned = [pltpu.HBM(s.shape, s.dtype) if spec is FAR else s for s, spec in zip(shapes, out_specs)]
+    if pin:
+        far = [pltpu.with_memory_space_constraint(a, pltpu.HBM) for a in far]
     moved = sum(a.size * a.dtype.itemsize for a in (*near, *far)) + sum(s.size * s.dtype.itemsize for s in shapes)
-    buffers = [pltpu.VMEM(a.shape, a.dtype) for a in far]
+    buffers = [pltpu.VMEM(a.shape, a.dtype) for a in far[: len(far) - kept]]
     if far:
         buffers.append(pltpu.SemaphoreType.DMA((len(far),)))
     return pl.pallas_call(
         body,
         name=name,
-        out_shape=shapes,
+        out_shape=pinned,
         in_specs=[SMEM] * len(scalars) + [VMEM] * len(near) + [FAR] * len(far),
-        out_specs=out_specs or [VMEM] * len(shapes),
-        scratch_shapes=[*scratch, *buffers],
+        out_specs=out_specs,
+        scratch_shapes=[*scratch, *buffers, *last],
         compiler_params=pltpu.CompilerParams(vmem_limit_bytes=limit * MIB),
         cost_estimate=pl.CostEstimate(flops=flops, bytes_accessed=moved, transcendentals=0),
     )(*scalars, *near, *far)
@@ -603,9 +658,10 @@
     swap = [(index, index ^ 1) for index in range(owners)]
     place = lax.axis_index("lat").astype(jnp.int32).reshape(1)
 
-    def gather(message):
+    def gather(message, *later):
         first = lax.all_to_all(message, "lat", 0, 0, tiled=True, axis_index_groups=groups)
-        return first, lax.ppermute(first, "lat", swap)
+        first, *later = lax.optimization_barrier((first, *later))
+        return first, lax.ppermute(first, "lat", swap), *later
 
     send = enc_sender.reshape(1, edges)
     receive = enc_receiver.reshape(1, edges)
@@ -617,76 +673,144 @@
         [grid_latent, enc_proj, mesh_latent, send, receive, enc_feat, enc_feat_w.T, serve_rows[0].T],
         [((chips, parts * (slots + 8) + 8, 128), BF), ((edges, width), BF), ((slots, width), BF)],
         [
-            pltpu.VMEM((grid_rows, width), BF),
-            pltpu.VMEM((edges, grid_rows), BF),
+            pltpu.VMEM((grid_rows + 128, width), BF),
+            pltpu.VMEM((edges, grid_rows + 128), BF),
             pltpu.VMEM((edges, width), BF),
             pltpu.SemaphoreType.DMA((edges // math.gcd(edges, 512),)),
         ],
         2 * edges * grid_rows * width,
-        60,
+        28,
         [VMEM, FAR, VMEM],
-    )
-    first, second = gather(message)
+        pin=True,
+        last=[pltpu.SemaphoreType.DMA((grid_rows // math.gcd(grid_rows, 256),))],
+    )
+    term_rows = stack_rows(feats)
+    first, second, served = gather(message, served)
+    pick, pick_turned, near_node, near_dec, near_feat_w, near_cotangent = kernel_call(
+        decoder_picks,
+        "decoder_picks",
+        [],
+        [served],
+        [dec_sender, dec_feat, node_proj, dec_proj, dec_feat_w.T, grid_cotangent],
+        [
+            ((slots + term_rows, 3 * grid_rows), BF),
+            ((3 * grid_rows, 128), BF),
+            ((width, width), BF),
+            ((width, width), BF),
+            ((feats, width), F32),
+            ((grid_rows, width), BF),
+        ],
+        [],
+        2000 * MIB,
+        16,
+        pin=True,
+        kept=4,
+    )
     message, keys, same, agg_slope, dec_grad = kernel_call(
         lambda *refs: decoder_kernel(cap, mesh_rows, *refs),
         "decoder",
         [place],
-        [first, second, served],
-        [node_proj, dec_proj, dec_sender, dec_feat, dec_feat_w.T, grid_cotangent],
+        [first, second, served, pick, pick_turned, near_node, near_dec, near_feat_w, near_cotangent],
+        [],
         [
             ((chips, parts * slots + slots * share // 128, 128), BF),
             ((2, span), F32),
             ((2, slots, span), BF),
             ((slots, width), F32),
-            ((8, width), F32),
+            ((2 * feats, width), F32),
         ],
         [],
         24 * grid_rows * 128 * width,
         20,
     )
-    first_back, second_back = gather(message)
-    term_rows = -(-6 * feats // 16) * 16
+    first_back, second_back, pick_count = gather(message, enc_count)
+    to_edge, latent_turned, dec_turned, node_turned, near_send, near_feat, near_slope = kernel_call(
+        encoder_picks,
+        "encoder_picks",
+        [pick_count],
+        [],
+        [receive, grid_latent, dec_proj, node_proj, send, enc_feat, slope],
+        [
+            ((edges, 128), BF),
+            ((width, grid_rows), BF),
+            ((width, width), BF),
+            ((width, width), BF),
+            ((1, edges), jnp.int32),
+            ((feats, edges), F32),
+            ((edges, width), BF),
+        ],
+        [],
+        2000 * MIB,
+        16,
+        pin=True,
+        kept=3,
+    )
     dpx, keep, give = kernel_call(
         backward_kernel,
         "backward",
-        [place, enc_count],
-        [first_back, second_back, same, agg_slope, dec_grad],
-        [node_proj, dec_proj, send, receive, enc_feat, grid_latent, slope],
+        [place],
+        [
+            first_back,
+            second_back,
+            same,
+            agg_slope,
+            dec_grad,
+            to_edge,
+            latent_turned,
+            dec_turned,
+            node_turned,
+            near_send,
+            near_feat,
+            near_slope,
+        ],
+        [],
         [((grid_rows, width), BF), ((chips, parts * block + 8, 128), F32), ((chips, parts * block + 8, 128), BF)],
         [
-            pltpu.VMEM((grid_rows + term_rows, edges), BF),
             pltpu.VMEM((edges, width), BF),
             pltpu.VMEM((width, width), F32),
+            pltpu.VMEM((grid_rows, width), BF),
+            pltpu.SemaphoreType.DMA((grid_rows // math.gcd(grid_rows, 256),)),
         ],
         2 * edges * grid_rows * width,
         24,
+        [FAR, VMEM, VMEM],
     )
     given = lax.ppermute(give, "lat", swap)
+    (pair,) = kernel_call(pair_kernel, "pair", [], [keep, given], [], [(give.shape, BF)], [], keep.size, 8)
+    pair, keys, dpx = lax.optimization_barrier((pair, keys, dpx))
+    arrived = lax.all_to_all(pair, "lat", 0, 0, tiled=True, axis_index_groups=groups)
     (grid_grad,) = kernel_call(
         grid_kernel,
         "grid",
         [],
-        [dpx],
-        [enc_proj, grid_cotangent],
+        [],
+        [dpx, enc_proj, grid_cotangent],
         [((grid_rows, width), BF)],
         [],
         2 * grid_rows * width * width,
         16,
     )
-    given, grid_grad = lax.optimization_barrier((given, grid_grad))
-    (pair,) = kernel_call(pair_kernel, "pair", [], [keep, given], [], [(give.shape, BF)], [], keep.size, 8)
-    pair, keys = lax.optimization_barrier((pair, keys))
-    arrived = lax.all_to_all(pair, "lat", 0, 0, tiled=True, axis_index_groups=groups)
+    both, turn, own = kernel_call(
+        lambda *refs: act_kernel(cap, mesh_rows, *refs),
+        "acts",
+        [place],
+        [first, second, keys],
+        [node_proj],
+        [((2 * span, 256), F32), ((2 * span, 2 * span), BF), ((mesh_rows, 2 * span), BF)],
+        [],
+        2 * (2 * span) * (2 * span) * width,
+        20,
+    )
     mesh_grad, dec_proj_grad, node_proj_grad = kernel_call(
-        lambda *refs: weight_kernel(cap, mesh_rows, *refs),
+        weight_kernel,
         "weights",
         [place],
-        [first, second, first_back, second_back, keys],
-        [node_proj, dec_proj],
+        [first_back, second_back, both, turn, own, dec_turned],
+        [],
         [((mesh_rows, width), BF), ((block, width), F32), ((block, width), F32)],
         [],
-        2 * (2 * span) * (2 * span) * width,
-        24,
+        8 * (2 * span) * 256 * width,
+        20,
     )
     enc_proj_grad, enc_feat_grad, dec_feat_grad = kernel_call(
         lambda *refs: final_kernel(feats, *refs),

time: 88.2 us -> 82.9 us (0.940)
  waiting for transfers between devices: 5.93 us -> 1.55 us
    ppermute x2, waiting for transfers between devices: 4.03 us -> 0.37 us  [gather(): return (first, lax.ppermute(first, 'lat', swap), *later)]
    all_to_all x1, waiting for transfers between devices: 1.9 us -> 0.01 us  [gather_plan(): lax.all_to_all(pair, 'lat', 0, 0, tiled=True, axis_index_groups=groups)]
    ppermute x1, waiting for transfers between devices: 0.01 us -> 1.19 us  [gather_plan(): given = lax.ppermute(give, 'lat', swap)]
    unnamed x34 -> x16, local copies, waits for them, and re-layouts: 2.98 us -> 2.29 us
    pallas_call x7 -> x10, Pallas kernels: 29.9 us -> 29.4 us  [kernel_call(): pl.pallas_call(body, name=name, out_shape=pinned, in_specs=[SMEM] * len(s...]
  transfers between devices with their start and end apart: 4 -> 4, of which waited for: 3 -> 2; matrix products, arithmetic and copies ran while one was open for 0% -> 0% of each run, Pallas kernels for 9% -> 15%
where the time goes in v3:
time: 82.9 us; the launch traced here: 82.4 us
  blocking collectives  43.6 us (53%)
  Pallas kernels  29.4 us (35%)
  starting transfers between devices  4.18 us (5%)
  local copies, waits for them, and re-layouts  2.29 us (3%)
  waiting for transfers between devices  1.55 us (2%)
  between operations  1.44 us (2%)
    all_to_all x2, blocking collectives, gather(): lax.all_to_all(message, 'lat', 0, 0, tiled=True, axis_index_groups=groups)  43.6 us
    pallas_call x10, Pallas kernels, kernel_call(): pl.pallas_call(body, name=name, out_shape=pinned, in_specs=[SMEM] * len(s...  29.4 us
    all_to_all x1, starting transfers between devices, gather_plan(): lax.all_to_all(pair, 'lat', 0, 0, tiled=True, axis_index_groups=groups)  3.6 us
    unnamed x16, local copies, waits for them, and re-layouts  2.29 us
  transfers between devices with their start and end apart: 4, of which 2 were waited for; matrix products, arithmetic and copies ran while one was open for 0% of the time, Pallas kernels for 15%

profile of v3, /device:TPU:0, one launch (start us, length us, event | category | flops | bytes accessed | tf_op | source)
XLA Modules:
  0.0 82.4 jit_solution(8307055114350210061)
XLA Ops:
  1.3 7.1 %encoder.1 = (bf16[8,296,128]{2,1,0:T(8,128)(2,1)S(1)}, bf16[2048,512]{1,0:T(8,128)(2,1)}, bf16[64,512]{1,0:T(8,128)(2,1)S(1)}) custom-call(s32[1]{0:T(128)S(6)} %copy.22.refs_0_.count, bf16[1024,512]{1,0:T(8,128)(2,1)} %latent_any.1, bf16[512,512]{1,0:T(8,128)(2,1)} %weight_any.1, bf16[320,512]{1,0:T(8,128)(2,1)} %refs_3_.1, s32[1,2048]{1,0:T(1,128)} %bitcast.12, ...), custom_call_target="tpu_custom_call" | custom-call | flops 2147483648 | bytes 4727040 | tf_op jit(solution)/shard_map/encoder/pallas_call | solution.py:616
  8.3 23.9 %all_to_all.15.refs_1_ = bf16[8,296,128]{2,1,0:T(8,128)(2,1)S(1)} all-to-all(bf16[8,296,128]{2,1,0:T(8,128)(2,1)S(1)} %get-tuple-element.47), channel_id=1, replica_groups={{0,2,4,6,8,10,12,14},{1,3,5,7,9,11,13,15},{16,18,20,22,24,26,28,30},{17..., dimensions={0} | all-to-all | bytes 1212416 | tf_op jit(solution)/shard_map/all_to_all | solution.py:662
  32.2 0.0 collective-permute-start
  32.2 1.7 %decoder_picks.1 = (bf16[96,3072]{1,0:T(8,128)(2,1)S(1)}, bf16[3072,128]{1,0:T(8,128)(2,1)S(1)}, bf16[512,512]{1,0:T(8,128)(2,1)S(1)}, bf16[512,512]{1,0:T(8,128...) custom-call(bf16[64,512]{1,0:T(8,128)(2,1)S(1)} %get-tuple-element.50.after.refs_3_, s32[3,1024]{1,0:T(4,128)} %send_any.1, ...), custom_call_target="tpu_custom_call" | custom-call | flops 2097152000 | bytes 5713920 | tf_op jit(solution)/shard_map/decoder_picks/pallas_call | solution.py:616
  33.9 0.4 collective-permute-done.refs_2_
  34.3 0.0 copy-start.5
  34.3 3.8 %decoder.1 = (bf16[8,288,128]{2,1,0:T(8,128)(2,1)S(1)}, f32[2,512]{1,0:T(2,128)S(1)}, bf16[2,64,512]{2,1,0:T(8,128)(2,1)S(1)}, f32[64,512]{1,0:T(8,128)S(1)}, f32[8,512]{1,0:T(8,128)S(1)}) custom-call(s32[1]{0:T(128)} %bitcast.refs_0_.place, bf16[8,296,128]{2,1,0:T(8,128)(2,1)S(1)} %all_to_all.15.refs_1_, ...), custom_call_target="tpu_custom_call" | custom-call | flops 1610612736 | bytes 5632000 | tf_op jit(solution)/shard_map/decoder/pallas_call | solution.py:616
  38.1 0.0 copy-done.5
  38.1 19.7 %all_to_all.16.first = bf16[8,288,128]{2,1,0:T(8,128)(2,1)S(1)} all-to-all(bf16[8,288,128]{2,1,0:T(8,128)(2,1)S(1)} %get-tuple-element.57), channel_id=1, replica_groups={{0,2,4,6,8,10,12,14},{1,3,5,7,9,11,13,15},{16,18,20,22,24,26,28,30},{17..., dimensions={0} | all-to-all | bytes 1179648 | tf_op jit(solution)/shard_map/all_to_all | solution.py:662
  57.8 0.0 collective-permute-start.1
  57.8 2.3 %encoder_picks.1 = (bf16[2048,128]{1,0:T(8,128)(2,1)S(1)}, bf16[512,1024]{1,0:T(8,128)(2,1)S(1)}, bf16[512,512]{1,0:T(8,128)(2,1)S(1)}, bf16[512,512]{1,0:T(8,12...) custom-call(s32[1]{0:T(128)S(6)} %copy.22.refs_0_.count, ...), custom_call_target="tpu_custom_call" | custom-call | flops 2097152000 | bytes 9003008 | tf_op jit(solution)/shard_map/encoder_picks/pallas_call | solution.py:616
  60.1 0.0 copy-start.3
  60.1 0.0 collective-permute-done.1.second
  60.2 5.1 %backward.1 = (bf16[1024,512]{1,0:T(8,128)(2,1)}, f32[8,136,128]{2,1,0:T(8,128)S(1)}, bf16[8,136,128]{2,1,0:T(8,128)(2,1)S(1)}) custom-call(s32[1]{0:T(128)} %bitcast.refs_0_.place, bf16[8,288,128]{2,1,0:T(8,128)(2,1)S(1)} %all_to_all.16.first, bf16[8,288,128]{2,1,0:T(8,128)(2,1)S(1)} %collective-permute-done.1.second, ...), custom_call_target="tpu_custom_call" | custom-call | flops 2147483648 | bytes 8101888 | tf_op jit(solution)/shard_map/backward/pallas_call | solution.py:616
  65.3 0.0 copy-done.3
  65.3 0.0 copy-start
  65.3 0.6 collective-permute-start.2
  65.9 1.2 %collective-permute-done.2.given = bf16[8,136,128]{2,1,0:T(8,128)(2,1)S(1)} collective-permute-done((bf16[8,136,128]{2,1,0:T(8,128)(2,1)S(1)}, bf16[8,136,128]{2,1,0:T(8,128)(2,1)S(1)}, u32[]{:S(2)}, u32[]{:S(2)}) %collective-permute-start.2) | collective-permute-done | bytes 278560 | tf_op jit(solution)/shard_map/ppermute | solution.py:778
  67.1 0.8 pair.1
  67.9 3.6 %all-to-all-start.2 = ((bf16[8,136,128]{2,1,0:T(8,128)(2,1)}), bf16[8,136,128]{2,1,0:T(8,128)(2,1)S(1)}, u32[]{:S(2)}, u32[]{:S(2)}) async-start(bf16[8,136,128]{2,1,0:T(8,128)(2,1)} %pair.1), calls=%async_computation.2 | async-start | bytes 557056 | tf_op jit(solution)/shard_map/all_to_all | solution.py:781
  71.5 0.0 copy-done
  71.5 0.0 copy-start.1
  71.5 1.2 %copy-done.1 = bf16[1024,512]{1,0:T(8,128)(2,1)S(1)} copy-done((bf16[1024,512]{1,0:T(8,128)(2,1)S(1)}, bf16[1024,512]{1,0:T(8,128)(2,1)}, u32[]{:S(2)}) %copy-start.1) | copy-done | bytes 1048600
  72.7 0.0 copy-start.2
  72.7 1.0 %copy-done.2 = bf16[512,512]{1,0:T(8,128)(2,1)S(1)} copy-done((bf16[512,512]{1,0:T(8,128)(2,1)S(1)}, bf16[512,512]{1,0:T(8,128)(2,1)}, u32[]{:S(2)}) %copy-start.2) | copy-done | bytes 524312
  73.7 0.0 copy-start.6
  73.7 0.0 copy-start.7
  73.7 1.9 %grid.1 = bf16[1024,512]{1,0:T(8,128)(2,1)} custom-call(bf16[1024,512]{1,0:T(8,128)(2,1)S(1)} %copy-done.1, bf16[512,512]{1,0:T(8,128)(2,1)S(1)} %copy-done.2, bf16[1024,512]{1,0:T(8,128)(2,1)S(1)} %copy-done), custom_call_target="tpu_custom_call" | custom-call | flops 536870912 | bytes 3670016 | tf_op jit(solution)/shard_map/grid/pallas_call | solution.py:616
  75.7 0.0 copy-done.6
  75.7 0.0 copy-done.7
  75.7 0.0 copy-start.4
  75.7 3.1 %acts.1 = (f32[1024,256]{1,0:T(8,128)S(1)}, bf16[1024,1024]{1,0:T(8,128)(2,1)S(1)}, bf16[320,1024]{1,0:T(8,128)(2,1)S(1)}) custom-call(s32[1]{0:T(128)} %bitcast.refs_0_.place, bf16[8,296,128]{2,1,0:T(8,128)(2,1)S(1)} %all_to_all.15.refs_1_, bf16[8,296,128]{2,1,0:T(8,128)(2,1)S(1)} %copy-done.6, f32[2,512]{1,0:T(2,128)S(1)} %get-tuple-element.76.refs_3_, ...), custom_call_target="tpu_custom_call" | custom-call | flops 1073741824 | bytes 5541888 | tf_op jit(solution)/shard_map/acts/pallas_call | solution.py:616
  78.9 0.0 copy-done.4
  78.9 2.9 %weights.1 = (bf16[320,512]{1,0:T(8,128)(2,1)}, f32[32,512]{1,0:T(8,128)}, f32[32,512]{1,0:T(8,128)}) custom-call(s32[1]{0:T(128)} %bitcast.refs_0_.place, bf16[8,288,128]{2,1,0:T(8,128)(2,1)S(1)} %all_to_all.16.first, bf16[8,288,128]{2,1,0:T(8,128)(2,1)S(1)} %collective-permute-done.1.second, f32[1024,256]{1,0:T(8,128)S(1)} %get-tuple-element.77.both, ...), custom_call_target="tpu_custom_call" | custom-call | flops 1073741824 | bytes 5963776 | tf_op jit(solution)/shard_map/weights/pallas_call | solution.py:616
  81.8 0.0 all-to-all-done.2.refs_0_
  81.8 0.7 final.1
Async XLA Ops:
  32.2 2.0 %collective-permute-start = (bf16[8,296,128]{2,1,0:T(8,128)(2,1)S(1)}, bf16[8,296,128]{2,1,0:T(8,128)(2,1)S(1)}, u32[]{:S(2)}, u32[]{:S(2)}) collective-permute-start(bf16[8,296,128]{2,1,0:T(8,128)(2,1)S(1)} %all_to_all.15.refs_1_), channel_id=1, source_target_pairs={{0,1},{1,0},{2,3},{3,2},{4,5},{5,4},{6,7},{7,6},{8,9},{9,8},{10,11... | collective-permute-start | bytes 1818632 | tf_op jit(solution)/shard_map/ppermute | solution.py:664
  34.3 3.8 %copy-start.5 = (bf16[8,296,128]{2,1,0:T(8,128)(2,1)}, bf16[8,296,128]{2,1,0:T(8,128)(2,1)S(1)}, u32[]{:S(2)}) copy-start(bf16[8,296,128]{2,1,0:T(8,128)(2,1)S(1)} %collective-permute-done.refs_2_) | copy-start | bytes 1818628
  57.8 2.4 %collective-permute-start.1 = (bf16[8,288,128]{2,1,0:T(8,128)(2,1)S(1)}, bf16[8,288,128]{2,1,0:T(8,128)(2,1)S(1)}, u32[]{:S(2)}, u32[]{:S(2)}) collective-permute-start(bf16[8,288,128]{2,1,0:T(8,128)(2,1)S(1)} %all_to_all.16.first), channel_id=1, source_target_pairs={{0,1},{1,0},{2,3},{3,2},{4,5},{5,4},{6,7},{7,6},{8,9},{9,8},{10,11... | collective-permute-start | bytes 1769480 | tf_op jit(solution)/shard_map/ppermute | solution.py:664
  60.1 5.2 %copy-start.3 = (bf16[512,512]{1,0:T(8,128)(2,1)}, bf16[512,512]{1,0:T(8,128)(2,1)S(1)}, u32[]{:S(2)}) copy-start(bf16[512,512]{1,0:T(8,128)(2,1)S(1)} %get-tuple-element.66.dec_turned) | copy-start | bytes 1572868
  65.3 6.2 %copy-start = (bf16[1024,512]{1,0:T(8,128)(2,1)S(1)}, bf16[1024,512]{1,0:T(8,128)(2,1)}, u32[]{:S(2)}) copy-start(bf16[1024,512]{1,0:T(8,128)(2,1)} %cot_any.3) | copy-start | bytes 3145732
  65.3 1.8 %collective-permute-start.2 = (bf16[8,136,128]{2,1,0:T(8,128)(2,1)S(1)}, bf16[8,136,128]{2,1,0:T(8,128)(2,1)S(1)}, u32[]{:S(2)}, u32[]{:S(2)}) collective-permute-start(bf16[8,136,128]{2,1,0:T(8,128)(2,1)S(1)} %get-tuple-element.72), channel_id=1, source_target_pairs={{0,1},{1,0},{2,3},{3,2},{4,5},{5,4},{6,7},{7,6},{8,9},{9,8},{10,11... | collective-permute-start | bytes 835592 | tf_op jit(solution)/shard_map/ppermute | solution.py:778
  67.9 13.9 %all-to-all-start.2 = ((bf16[8,136,128]{2,1,0:T(8,128)(2,1)}), bf16[8,136,128]{2,1,0:T(8,128)(2,1)S(1)}, u32[]{:S(2)}, u32[]{:S(2)}) async-start(bf16[8,136,128]{2,1,0:T(8,128)(2,1)} %pair.1), calls=%async_computation.2 | async-start | bytes 557056 | tf_op jit(solution)/shard_map/all_to_all | solution.py:781
  71.5 1.2 %copy-start.1 = (bf16[1024,512]{1,0:T(8,128)(2,1)S(1)}, bf16[1024,512]{1,0:T(8,128)(2,1)}, u32[]{:S(2)}) copy-start(bf16[1024,512]{1,0:T(8,128)(2,1)} %get-tuple-element.75.dpx_any) | copy-start | bytes 3145732
  72.7 1.0 %copy-start.2 = (bf16[512,512]{1,0:T(8,128)(2,1)S(1)}, bf16[512,512]{1,0:T(8,128)(2,1)}, u32[]{:S(2)}) copy-start(bf16[512,512]{1,0:T(8,128)(2,1)} %weight_any.1) | copy-start | bytes 1572868
  73.7 1.9 %copy-start.6 = (bf16[8,296,128]{2,1,0:T(8,128)(2,1)S(1)}, bf16[8,296,128]{2,1,0:T(8,128)(2,1)}, u32[]{:S(2)}) copy-start(bf16[8,296,128]{2,1,0:T(8,128)(2,1)} %copy-done.5) | copy-start | bytes 1818628
  73.7 1.9 %copy-start.7 = (bf16[512,512]{1,0:T(8,128)(2,1)S(1)}, bf16[512,512]{1,0:T(8,128)(2,1)}, u32[]{:S(2)}) copy-start(bf16[512,512]{1,0:T(8,128)(2,1)} %refs_4_.1) | copy-start | bytes 1572868
  75.7 3.2 %copy-start.4 = (bf16[512,512]{1,0:T(8,128)(2,1)S(1)}, bf16[512,512]{1,0:T(8,128)(2,1)}, u32[]{:S(2)}) copy-start(bf16[512,512]{1,0:T(8,128)(2,1)} %copy-done.3) | copy-start | bytes 1572868

commit v4 on v3

--- a/solution.py
+++ b/solution.py
@@ -231,7 +231,7 @@
 
 def encoder_kernel(
     cap, count, latent_any, weight_any, mesh_any, send_any, receive_any, feat_any, feat_w_any, serve_any,
-    message, slope_far, served_out, px, picks, slope, slope_sems,
+    message, slope_far, served_out, own_out, px, picks, silus, slope, slope_sems,
     latent, weight, mesh, send, receive, feat, feat_w, serve, sems, latent_sems,
 ):
     sources = (send_any, feat_any, weight_any, feat_w_any, receive_any, mesh_any, serve_any)
@@ -266,7 +266,6 @@
         copy.wait()
     terms = stack_terms(0.5 * feat_w[...], WEIGHT_ORDER)
     px[grid_rows:, :] = jnp.concatenate([terms, jnp.zeros((128 - terms.shape[0], width), F32)], 0).astype(BF)
-    total = jnp.zeros((slots, width), F32)
     stores = []
     for start in range(0, edges, block):
         part = slice(start, start + block)
@@ -279,10 +278,9 @@
         out = pltpu.make_async_copy(slope.at[part, :], slope_far.at[part, :], slope_sems.at[len(stores)])
         out.start()
         stores.append(out)
-        live = iota((1, block), 1) + start < count[0]
-        slot = jnp.where(live, receive[:, part], -1)
-        to_slot = hot(iota((slots, block), 0) == slot)
-        total = total + mm(to_slot, silu.astype(BF))
+        silus[part, :] = silu.astype(BF)
+    live = iota((1, edges), 1) < count[0]
+    total = mm(hot(iota((slots, edges), 0) == jnp.where(live, receive[...], -1)), silus[...])
     copies[5].wait()
     copies[6].wait()
     owners = slots // cap
@@ -301,6 +299,7 @@
     wide = mm(digits[0].astype(BF), hot(lane == back)) + mm(digits[1].astype(BF), hot(lane == back + slots))
     id_rows = jnp.where(iota((8, 128), 0) == 0, wide, 0.0)
     half = total.astype(BF)
+    own_out[...] = (total - half.astype(F32)).astype(BF)
     for chip in range(chips):
         write_slots(message, chip, half)
         rows = served[2 * cap * chip : 2 * cap * (chip + 1)]
@@ -383,11 +382,11 @@
 
 
 def decoder_picks(
-    after, send_any, feat_any, node_any, dec_any, feat_w_any, cot_any,
-    pick, pick_turned, node_w, dec_w, feat_w, cotangent, send, feat, sems,
+    after, send_any, feat_any, node_any, dec_any, feat_w_any,
+    pick, pick_turned, node_w, dec_w, feat_w, send, feat, sems,
 ):
-    sources = (send_any, feat_any, node_any, dec_any, feat_w_any, cot_any)
-    copies = fetch(sources, (send, feat, node_w, dec_w, feat_w, cotangent), sems)
+    sources = (send_any, feat_any, node_any, dec_any, feat_w_any)
+    copies = fetch(sources, (send, feat, node_w, dec_w, feat_w), sems)
     slots = after.shape[0]
     grid_rows = send.shape[1]
     copies[0].wait()
@@ -407,11 +406,11 @@
 
 
 def encoder_picks(
-    count, receive_any, latent_any, dec_any, node_any, send_any, feat_any, slope_any,
-    to_edge, latent_turned, dec_turned, node_turned, send, feat, slope, receive, latent, dec_w, node_w, sems,
+    count, latent, receive_any, dec_any, node_any, send_any, feat_any,
+    to_edge, latent_turned, dec_turned, node_turned, send, feat, receive, dec_w, node_w, sems,
 ):
-    sources = (receive_any, dec_any, node_any, latent_any, send_any, feat_any, slope_any)
-    copies = fetch(sources, (receive, dec_w, node_w, latent, send, feat, slope), sems)
+    sources = (receive_any, dec_any, node_any, send_any, feat_any)
+    copies = fetch(sources, (receive, dec_w, node_w, send, feat), sems)
     edges = receive.shape[1]
     copies[0].wait()
     block = math.gcd(edges, 512)
@@ -420,18 +419,18 @@
         live = iota((1, block), 1) + start < count[0]
         slot = jnp.where(live, receive[:, part], -1)
         to_edge[part, :] = jnp.where(iota((128, block), 0) == slot, 1.0, 0.0).T.astype(BF)
-    for copy in copies[1:4]:
+    for copy in copies[1:3]:
         copy.wait()
     dec_turned[...] = dec_w[...].T
     node_turned[...] = node_w[...].T
     latent_turned[...] = latent[...].T
-    for copy in copies[4:]:
+    for copy in copies[3:]:
         copy.wait()
 
 
 def decoder_kernel(
-    cap, mesh_rows, place, first, second, extra, pick, pick_turned, node_w, dec_w, feat_w, cotangent,
-    message, keys_out, same_out, slope_out, grad_out,
+    cap, mesh_rows, place, first, second, extra, rest, pick, pick_turned, node_w, dec_w, feat_w, cotangent,
+    message, keys_out, same_out, slope_out, grad_out, mine_out, rest_out,
 ):
     slots, width = extra.shape
     keys, same, latent = slot_matches(first, second, place[0], cap, mesh_rows, width)
@@ -440,6 +439,11 @@
         keys_out[piece : piece + 1, :] = keys[piece]
         same_out[piece] = same[piece]
         agg = agg + mm(same[piece], slot_rows(ref, slots, width))
+    shape = (same[0].shape[1], slots)
+    chosen = hot(iota(shape, 0) == slots * lax.div(place[0], 2) + iota(shape, 1))
+    mine = mm(same[0], chosen).astype(BF)
+    mine_out[...] = mine
+    agg = agg + mm(mine, rest[...])
     silu, double = halves(0.5 * agg)
     slope_out[...] = 0.25 * double
     hmesh = (latent + mm(silu.astype(BF), node_w[...])).astype(BF)
@@ -459,6 +463,7 @@
             total = total + mm(pick[:, part], (cot * double).astype(BF))
     total = 0.5 * total
     half = total[:slots].astype(BF)
+    rest_out[...] = (total[:slots] - half.astype(F32)).astype(BF)
     grad_out[...] = feature_grad(total[slots:], feat_w.shape[0])
     chips = message.shape[0]
     share = width // chips
@@ -471,8 +476,8 @@
 
 
 def backward_kernel(
-    place, first, second, same, agg_slope, dec_grad, to_edge, latent_turned, dec_turned, node_turned,
-    send, feat, slope, dpx_far, keep, give, grads, part, dpx, dpx_sems,
+    place, first, second, same, mine, rest, agg_slope, dec_grad, to_edge, latent_turned, dec_turned, node_turned,
+    send, feat, slope, dpx_far, dpx, give, sums_out, grads, dpx_sems,
 ):
     slots = same.shape[1]
     edges, width = grads.shape
@@ -480,6 +485,7 @@
     feats = feat.shape[0]
     core = lax.rem(place[0], 2)
     dproj = mm(same[0], slot_rows(first, slots, width)) + mm(same[1], slot_rows(second, slots, width))
+    dproj = dproj + mm(mine[...], rest[...])
     high = dproj.astype(BF)
     low = (dproj - high.astype(F32)).astype(BF)
     dhmesh = mm(jnp.concatenate([high, low], 0), dec_turned[...])
@@ -501,30 +507,33 @@
         stores.append(out)
     enc_grad = feature_grad(mm(stack_terms(feat[...], FEAT_ORDER).astype(BF), grads[...]), feats)
     sums = jnp.where(iota(enc_grad.shape, 0) < feats, enc_grad, pltpu.roll(dec_grad[...], feats, 0))
-    part[...] = mm(latent_turned[...], dpx[...])
-    rows = width // (2 * keep.shape[0])
-    blank = jnp.zeros((8, 128 - rows), F32)
-    for chip in range(keep.shape[0]):
-        pair = [sums[:, base : base + rows] for base in (2 * chip * rows, (2 * chip + 1) * rows)]
-        for out, side in ((keep, core), (give, 1 - core)):
-            block = part[pl.ds((2 * chip + side) * rows, rows), :]
-            small = jnp.where(side == 0, pair[0], pair[1])
-            pieces = [block[:, base : base + 128] for base in range(0, width, 128)]
-            whole = jnp.concatenate([*pieces, jnp.concatenate([small, blank], 1)], 0)
-            out[chip] = whole.astype(out.dtype)
+    sums_out[...] = sums
+    write_shares(give, 1 - core, latent_turned, dpx, sums)
     for out in stores:
         out.wait()
 
 
+def write_shares(out, side, latent_turned, dpx, sums):
+    chips = out.shape[0]
+    width = dpx.shape[1]
+    rows = width // (2 * chips)
+    left = [latent_turned[pl.ds((2 * chip + side) * rows, rows), :] for chip in range(chips)]
+    product = mm(jnp.concatenate(left, 0), dpx[...])
+    blank = jnp.zeros((8, 128 - rows), F32)
+    for chip in range(chips):
+        block = product[chip * rows : (chip + 1) * rows]
+        pair = [sums[:, base : base + rows] for base in (2 * chip * rows, (2 * chip + 1) * rows)]
+        small = jnp.concatenate([jnp.where(side == 0, pair[0], pair[1]), blank], 1)
+        pieces = [block[:, base : base + 128] for base in range(0, width, 128)]
+        out[chip] = jnp.concatenate([*pieces, small], 0).astype(out.dtype)
+
+
+def keep_kernel(place, latent_turned, dpx, sums, keep):
+    write_shares(keep, lax.rem(place[0], 2), latent_turned, dpx, sums[...])
+
+
 def pair_kernel(keep, given, out):
     out[...] = (keep[...] + given[...].astype(F32)).astype(BF)
-
-
-def grid_kernel(dpx_any, weight_any, cot_any, out, dpx, weight, cotangent, sems):
-    copies = fetch((dpx_any, weight_any, cot_any), (dpx, weight, cotangent), sems)
-    for copy in copies:
-        copy.wait()
-    out[...] = (cotangent[...].astype(F32) + mm(dpx[...], weight[...], NT)).astype(BF)
 
 
 def final_kernel(feats, arrived, out, enc_out, dec_out):
@@ -537,8 +546,16 @@
     dec_out[...] = total[base + feats : base + 2 * feats, :rows]
 
 
-def act_kernel(cap, mesh_rows, place, first, second, keys, node_any, both_out, turn_out, own_out, node_w, sems):
-    copies = fetch((node_any,), (node_w,), sems)
+def beside_kernel(
+    cap, mesh_rows, place, keys, node_any, first_any, second_any, first_back_any, second_back_any, dec_any, dpx_any,
+    weight_any, cot_any, mesh_out, dec_out, node_out, grid_out,
+    node_w, first, second, first_back, second_back, dec_w, dpx, weight, cotangent, sems,
+):
+    sources = (
+        first_any, second_any, node_any, first_back_any, second_back_any, dec_any, dpx_any, weight_any, cot_any,
+    )
+    targets = (first, second, node_w, first_back, second_back, dec_w, dpx, weight, cotangent)
+    copies = fetch(sources, targets, sems)
     width = node_w.shape[0]
     chips = first.shape[0]
     owners = 2 * chips
@@ -547,55 +564,48 @@
     me = place[0]
     core = lax.rem(me, 2)
     block = width // owners
-    forward = jnp.concatenate([slot_rows(ref, slots, width) for ref in (first, second)], 0)
     key = jnp.concatenate([keys[0:1, :], keys[1:2, :]], 1)
     down = jnp.broadcast_to(key, (128, 2 * span)).T
     same = jnp.concatenate([hot(down == key[:, base : base + 128]) for base in range(0, 2 * span, 128)], 1)
-    agg = mm(same, forward)
-    act = halves(0.5 * agg)[0].astype(BF)
+    for copy in copies[:3]:
+        copy.wait()
+    forward = jnp.concatenate([slot_rows(ref, slots, width) for ref in (first, second)], 0)
+    act = halves(0.5 * mm(same, forward))[0].astype(BF)
     shape = (width, 128)
     mine = hot((iota(shape, 0) == block * me + iota(shape, 1)) & (iota(shape, 1) < block))
-    copies[0].wait()
     node_cols = mm(node_w[...], mine).astype(BF)
-    both_out[...] = mm(act, jnp.concatenate([node_cols, mine], 1))
+    both = mm(act, jnp.concatenate([node_cols, mine], 1))
     step = slots * 2 * block // 128
     pieces = [gathered_slots(piece, chips, core, cap, (span, 1), 0) for piece in range(2)]
     band, owner, turn = [jnp.concatenate([a, b], 0) for a, b in zip(*pieces)]
     source = jnp.where(lax.rem(owner, 2) == core, 0, chips) + lax.div(owner, 2)
     number = cap * band + turn
     at = lax.div(number, step) * (owners * step) + source * step + lax.rem(number, step)
-    turn_out[...] = hot(iota((2 * span, 2 * span), 1) == at)
-    own = (me * mesh_rows + iota((own_out.shape[0], 2 * span), 0)).astype(F32)
-    own_out[...] = hot(own == key)
-
-
-def weight_kernel(place, first, second, both, turn, own, dec_turned, mesh_out, dec_out, node_out):
-    width = dec_turned.shape[0]
-    chips = first.shape[0]
-    slots = turn.shape[0] // (2 * chips)
-    block = dec_out.shape[0]
-    core = lax.rem(place[0], 2)
-    back = jnp.concatenate([slot_rows(ref, slots, width) for ref in (first, second)], 0)
+    for copy in copies[3:]:
+        copy.wait()
+    back = jnp.concatenate([slot_rows(ref, slots, width) for ref in (first_back, second_back)], 0)
     tail = slots * (width // 128)
-    columns = jnp.concatenate([ref[chip, tail:, :] for ref in (first, second) for chip in range(chips)], 0)
+    columns = [ref[chip, tail:, :] for ref in (first_back, second_back) for chip in range(chips)]
+    columns = jnp.concatenate(columns, 0)
     shape = (128, 128)
     folded = []
     for base in range(0, 128, 2 * block):
         fold = hot((iota(shape, 0) == base + block * core + iota(shape, 1)) & (iota(shape, 1) < block))
         folded.append(mm(columns, fold).astype(BF))
-    latent = mm(turn[...], jnp.concatenate(folded, 0))
+    latent = mm(hot(iota((2 * span, 2 * span), 1) == at), jnp.concatenate(folded, 0))
     hmesh = (both[:, :128] + latent).astype(BF)
     left = jnp.concatenate([hmesh, both[:, 128:].astype(BF)], 1)
     sums = mm(left, back, TN)
     dec_out[...] = sums[:block]
-    lead = sums[128 : 128 + block]
-    high = lead.astype(BF)
-    low = (lead - high.astype(F32)).astype(BF)
-    node_out[...] = mm(high, dec_turned[...]) + mm(low, dec_turned[...])
-    dproj = mm(own[...], back)
+    own = (me * mesh_rows + iota((mesh_out.shape[0], 2 * span), 0)).astype(F32)
+    dproj = jnp.concatenate([mm(hot(own == key), back), sums[128 : 128 + block]], 0)
     high = dproj.astype(BF)
     low = (dproj - high.astype(F32)).astype(BF)
-    mesh_out[...] = (mm(high, dec_turned[...]) + mm(low, dec_turned[...])).astype(BF)
+    turned = mm(high, dec_w[...], NT) + mm(low, dec_w[...], NT)
+    mesh = mesh_out.shape[0]
+    mesh_out[...] = turned[:mesh].astype(BF)
+    node_out[...] = turned[mesh:]
+    grid_out[...] = (cotangent[...].astype(F32) + mm(dpx[...], weight[...], NT)).astype(BF)
 
 
 SMEM = pl.BlockSpec(memory_space=pltpu.SMEM)
@@ -665,52 +675,57 @@
 
     send = enc_sender.reshape(1, edges)
     receive = enc_receiver.reshape(1, edges)
-    message, slope, served = kernel_call(
+    message, slope, served, rest = kernel_call(
         lambda *refs: encoder_kernel(cap, *refs),
         "encoder",
         [enc_count],
         [],
         [grid_latent, enc_proj, mesh_latent, send, receive, enc_feat, enc_feat_w.T, serve_rows[0].T],
-        [((chips, parts * (slots + 8) + 8, 128), BF), ((edges, width), BF), ((slots, width), BF)],
+        [
+            ((chips, parts * (slots + 8) + 8, 128), BF),
+            ((edges, width), BF),
+            ((slots, width), BF),
+            ((slots, width), BF),
+        ],
         [
             pltpu.VMEM((grid_rows + 128, width), BF),
-            pltpu.VMEM((edges, grid_rows + 128), BF),
+            pltpu.VMEM((edges, grid_rows), BF),
+            pltpu.VMEM((edges, width), BF),
             pltpu.VMEM((edges, width), BF),
             pltpu.SemaphoreType.DMA((edges // math.gcd(edges, 512),)),
         ],
         2 * edges * grid_rows * width,
         28,
-        [VMEM, FAR, VMEM],
+        [VMEM, FAR, VMEM, VMEM],
         pin=True,
         last=[pltpu.SemaphoreType.DMA((grid_rows // math.gcd(grid_rows, 256),))],
     )
     term_rows = stack_rows(feats)
     first, second, served = gather(message, served)
-    pick, pick_turned, near_node, near_dec, near_feat_w, near_cotangent = kernel_call(
+    pick, pick_turned, near_node, near_dec, near_feat_w = kernel_call(
         decoder_picks,
         "decoder_picks",
         [],
         [served],
-        [dec_sender, dec_feat, node_proj, dec_proj, dec_feat_w.T, grid_cotangent],
+        [dec_sender, dec_feat, node_proj, dec_proj, dec_feat_w.T],
         [
             ((slots + term_rows, 3 * grid_rows), BF),
             ((3 * grid_rows, 128), BF),
             ((width, width), BF),
             ((width, width), BF),
             ((feats, width), F32),
-            ((grid_rows, width), BF),
         ],
         [],
         2000 * MIB,
         16,
         pin=True,
-        kept=4,
-    )
-    message, keys, same, agg_slope, dec_grad = kernel_call(
+        kept=3,
+    )
+    message, keys, same, agg_slope, dec_grad, mine, rest = kernel_call(
         lambda *refs: decoder_kernel(cap, mesh_rows, *refs),
         "decoder",
         [place],
-        [first, second, served, pick, pick_turned, near_node, near_dec, near_feat_w, near_cotangent],
+        [first, second, served, rest, pick, pick_turned, near_node, near_dec, near_feat_w, grid_cotangent],
         [],
         [
             ((chips, parts * slots + slots * share // 128, 128), BF),
@@ -718,18 +733,20 @@
             ((2, slots, span), BF),
             ((slots, width), F32),
             ((2 * feats, width), F32),
+            ((slots, slots), BF),
+            ((slots, width), BF),
         ],
         [],
         24 * grid_rows * 128 * width,
         20,
     )
     first_back, second_back, pick_count = gather(message, enc_count)
-    to_edge, latent_turned, dec_turned, node_turned, near_send, near_feat, near_slope = kernel_call(
+    to_edge, latent_turned, dec_turned, node_turned, near_send, near_feat = kernel_call(
         encoder_picks,
         "encoder_picks",
         [pick_count],
-        [],
-        [receive, grid_latent, dec_proj, node_proj, send, enc_feat, slope],
+        [grid_latent],
+        [receive, dec_proj, node_proj, send, enc_feat],
         [
             ((edges, 128), BF),
             ((width, grid_rows), BF),
@@ -737,15 +754,14 @@
             ((width, width), BF),
             ((1, edges), jnp.int32),
             ((feats, edges), F32),
-            ((edges, width), BF),
         ],
         [],
         2000 * MIB,
         16,
         pin=True,
-        kept=3,
-    )
-    dpx, keep, give = kernel_call(
+        kept=2,
+    )
+    dpx_far, dpx, give, sums = kernel_call(
         backward_kernel,
         "backward",
         [place],
@@ -753,6 +769,8 @@
             first_back,
             second_back,
             same,
+            mine,
+            rest,
             agg_slope,
             dec_grad,
             to_edge,
@@ -761,56 +779,64 @@
             node_turned,
             near_send,
             near_feat,
-            near_slope,
+            slope,
         ],
         [],
-        [((grid_rows, width), BF), ((chips, parts * block + 8, 128), F32), ((chips, parts * block + 8, 128), BF)],
+        [
+            ((grid_rows, width), BF),
+            ((grid_rows, width), BF),
+            ((chips, parts * block + 8, 128), BF),
+            ((2 * feats, width), F32),
+        ],
         [
             pltpu.VMEM((edges, width), BF),
-            pltpu.VMEM((width, width), F32),
-            pltpu.VMEM((grid_rows, width), BF),
             pltpu.SemaphoreType.DMA((grid_rows // math.gcd(grid_rows, 256),)),
         ],
         2 * edges * grid_rows * width,
         24,
-        [FAR, VMEM, VMEM],
+        [FAR, VMEM, VMEM, VMEM],
+    )
+    (keep,) = kernel_call(
+        keep_kernel,
+        "keep",
+        [place],
+        [latent_turned, dpx, sums],
+        [],
+        [((chips, parts * block + 8, 128), F32)],
+        [],
+        grid_rows * width * width,
+        16,
     )
     given = lax.ppermute(give, "lat", swap)
     (pair,) = kernel_call(pair_kernel, "pair", [], [keep, given], [], [(give.shape, BF)], [], keep.size, 8)
-    pair, keys, dpx = lax.optimization_barrier((pair, keys, dpx))
+    pair, keys, dpx_far = lax.optimization_barrier((pair, keys, dpx_far))
     arrived = lax.all_to_all(pair, "lat", 0, 0, tiled=True, axis_index_groups=groups)
-    (grid_grad,) = kernel_call(
-        grid_kernel,
-        "grid",
-        [],
-        [],
-        [dpx, enc_proj, grid_cotangent],
-        [((grid_rows, width), BF)],
-        [],
-        2 * grid_rows * width * width,
-        16,
-    )
-    both, turn, own = kernel_call(
-        lambda *refs: act_kernel(cap, mesh_rows, *refs),
-        "acts",
+    mesh_grad, dec_proj_grad, node_proj_grad, grid_grad = kernel_call(
+        lambda *refs: beside_kernel(cap, mesh_rows, *refs),
+        "beside",
         [place],
-        [first, second, keys],
-        [node_proj],
-        [((2 * span, 256), F32), ((2 * span, 2 * span), BF), ((mesh_rows, 2 * span), BF)],
+        [keys],
+        [
+            node_proj,
+            first,
+            second,
+            first_back,
+            second_back,
+            dec_proj,
+            dpx_far,
+            enc_proj,
+            grid_cotangent,
+        ],
+        [
+            ((mesh_rows, width), BF),
+            ((block, width), F32),
+            ((block, width), F32),
+            ((grid_rows, width), BF),
+        ],
         [],
         2 * (2 * span) * (2 * span) * width,
-        20,
-    )
-    mesh_grad, dec_proj_grad, node_proj_grad = kernel_call(
-        weight_kernel,
-        "weights",
-        [place],
-        [first_back, second_back, both, turn, own, dec_turned],
-        [],
-        [((mesh_rows, width), BF), ((block, width), F32), ((block, width), F32)],
-        [],
-        8 * (2 * span) * 256 * width,
-        20,
+        30,
+        pin=True,
     )
     enc_proj_grad, enc_feat_grad, dec_feat_grad = kernel_call(
         lambda *refs: final_kernel(feats, *refs),

time: 82.9 us -> 81.5 us (0.983)
  local copies, waits for them, and re-layouts: 2.29 us -> 0.03 us
  waiting for transfers between devices: 1.55 us -> 2.53 us
    unnamed x16 -> x14, local copies, waits for them, and re-layouts: 2.29 us -> 0.03 us
    all_to_all x1, waiting for transfers between devices: 0.01 us -> 1.16 us  [gather_plan(): lax.all_to_all(pair, 'lat', 0, 0, tiled=True, axis_index_groups=groups)]
    pallas_call x10 -> x9, Pallas kernels: 29.4 us -> 29.7 us  [kernel_call(): pl.pallas_call(body, name=name, out_shape=pinned, in_specs=[SMEM] * len(s...]
  transfers between devices with their start and end apart: 4 -> 4, of which waited for: 2 -> 3; matrix products, arithmetic and copies ran while one was open for 0% -> 0% of each run, Pallas kernels for 15% -> 16%
where the time goes in v4:
time: 81.5 us; the launch traced here: 81.1 us
  blocking collectives  43.5 us (53%)
  Pallas kernels  29.7 us (36%)
  starting transfers between devices  3.91 us (5%)
  waiting for transfers between devices  2.53 us (3%)
  between operations  1.41 us (2%)
    all_to_all x2, blocking collectives, gather(): lax.all_to_all(message, 'lat', 0, 0, tiled=True, axis_index_groups=groups)  43.5 us
    pallas_call x9, Pallas kernels, kernel_call(): pl.pallas_call(body, name=name, out_shape=pinned, in_specs=[SMEM] * len(s...  29.7 us
    all_to_all x1, starting transfers between devices, gather_plan(): lax.all_to_all(pair, 'lat', 0, 0, tiled=True, axis_index_groups=groups)  3.6 us
  transfers between devices with their start and end apart: 4, of which 3 were waited for; matrix products, arithmetic and copies ran while one was open for 0% of the time, Pallas kernels for 16%

profile of v4, /device:TPU:0, one launch (start us, length us, event | category | flops | bytes accessed | tf_op | source)
XLA Modules:
  0.0 81.1 jit_solution(15910275953227229099)
XLA Ops:
  1.3 6.9 %encoder.1 = (bf16[8,296,128]{2,1,0:T(8,128)(2,1)S(1)}, bf16[2048,512]{1,0:T(8,128)(2,1)}, bf16[64,512]{1,0:T(8,128)(2,1)S(1)}, bf16[64,512]{1,0:T(8,128)(2,1)S(1)}) custom-call(s32[1]{0:T(128)S(6)} %copy.22.refs_0_.count, bf16[1024,512]{1,0:T(8,128)(2,1)} %latent.1, bf16[512,512]{1,0:T(8,128)(2,1)} %refs_9_.1, bf16[320,512]{1,0:T(8,128)(2,1)} %refs_3_.1, ...), custom_call_target="tpu_custom_call" | custom-call | flops 2147483648 | bytes 4792576 | tf_op jit(solution)/shard_map/encoder/pallas_call | solution.py:626
  8.2 23.9 %all_to_all.15.refs_1_.refs_3_ = bf16[8,296,128]{2,1,0:T(8,128)(2,1)S(1)} all-to-all(bf16[8,296,128]{2,1,0:T(8,128)(2,1)S(1)} %get-tuple-element.47), channel_id=1, replica_groups={{0,2,4,6,8,10,12,14},{1,3,5,7,9,11,13,15},{16,18,20,22,24,26,28,30},{17..., dimensions={0} | all-to-all | bytes 1212416 | tf_op jit(solution)/shard_map/all_to_all | solution.py:672
  32.0 0.0 copy-start
  32.1 0.0 collective-permute-start
  32.1 0.0 copy-start.2
  32.1 1.5 %decoder_picks.1 = (bf16[96,3072]{1,0:T(8,128)(2,1)S(1)}, bf16[3072,128]{1,0:T(8,128)(2,1)S(1)}, bf16[512,512]{1,0:T(8,128)(2,1)S(1)}, bf16[512,512]{1,0:T(8,128)(2,1)S(1)}, f32[4,512]{1,0:T(4,128)S(1)}) custom-call(bf16[64,512]{1,0:T(8,128)(2,1)S(1)} %get-tuple-element.50.after.refs_3_, s32[3,1024]{1,0:T(4,128)} %send_any.1, f32[3,4,1024]{2,1,0:T(4,128)} %feat_any.2, ...), custom_call_target="tpu_custom_call" | custom-call | flops 2097152000 | bytes 3616768 | tf_op jit(solution)/shard_map/decoder_picks/pallas_call | solution.py:626
  33.6 0.5 collective-permute-done.refs_2_.refs_4_
  34.1 0.0 copy-start.3
  34.1 0.0 copy-done
  34.1 0.0 copy-done.2
  34.1 0.0 copy-start.5
  34.1 4.0 %decoder.1 = (bf16[8,288,128]{2,1,0:T(8,128)(2,1)S(1)}, f32[2,512]{1,0:T(2,128)S(1)}, bf16[2,64,512]{2,1,0:T(8,128)(2,1)S(1)}, f32[64,512]{1,0:T(8,128)S(1)}, f3...) custom-call(s32[1]{0:T(128)} %bitcast.refs_0_.place, ...), custom_call_target="tpu_custom_call" | custom-call | flops 1610612736 | bytes 5771264 | tf_op jit(solution)/shard_map/decoder/pallas_call | solution.py:626
  38.1 0.0 copy-done.3
  38.1 19.6 %all_to_all.16.first.refs_5_ = bf16[8,288,128]{2,1,0:T(8,128)(2,1)S(1)} all-to-all(bf16[8,288,128]{2,1,0:T(8,128)(2,1)S(1)} %get-tuple-element.57), channel_id=1, replica_groups={{0,2,4,6,8,10,12,14},{1,3,5,7,9,11,13,15},{16,18,20,22,24,26,28,30},{17..., dimensions={0} | all-to-all | bytes 1179648 | tf_op jit(solution)/shard_map/all_to_all | solution.py:672
  57.7 0.0 copy-start.1
  57.7 0.0 copy-start.6
  57.7 0.0 collective-permute-start.1
  57.7 0.0 copy-done.5
  57.7 2.1 %encoder_picks.1 = (bf16[2048,128]{1,0:T(8,128)(2,1)S(1)}, bf16[512,1024]{1,0:T(8,128)(2,1)S(1)}, bf16[512,512]{1,0:T(8,128)(2,1)S(1)}, bf16[512,512]{1,0:T(8,12...) custom-call(s32[1]{0:T(128)S(6)} %copy.22.refs_0_.count, bf16[1024,512]{1,0:T(8,128)(2,1)S(1)} %copy-done.5, ...), custom_call_target="tpu_custom_call" | custom-call | flops 2097152000 | bytes 4808704 | tf_op jit(solution)/shard_map/encoder_picks/pallas_call | solution.py:626
  59.9 0.0 collective-permute-done.1.second.refs_6_
  59.9 0.0 copy-start.4
  59.9 0.0 copy-done.1
  59.9 0.0 copy-done.6
  59.9 4.7 %backward.1 = (bf16[1024,512]{1,0:T(8,128)(2,1)}, bf16[1024,512]{1,0:T(8,128)(2,1)S(1)}, bf16[8,136,128]{2,1,0:T(8,128)(2,1)S(1)}, f32[8,512]{1,0:T(8,128)S(1)}) custom-call(s32[1]{0:T(128)} %bitcast.refs_0_.place, bf16[8,288,128]{2,1,0:T(8,128)(2,1)S(1)} %all_to_all.16.first.refs_5_, bf16[8,288,128]{2,1,0:T(8,128)(2,1)S(1)} %collective-permute-done.1.second.refs_6_, ...), custom_call_target="tpu_custom_call" | custom-call | flops 2147483648 | bytes 8683520 | tf_op jit(solution)/shard_map/backward/pallas_call | solution.py:626
  64.6 0.0 copy-done.4
  64.6 0.3 collective-permute-start.2
  64.9 0.4 keep.1
  65.4 0.9 %collective-permute-done.2.given = bf16[8,136,128]{2,1,0:T(8,128)(2,1)S(1)} collective-permute-done((bf16[8,136,128]{2,1,0:T(8,128)(2,1)S(1)}, bf16[8,136,128]{2,1,0:T(8,128)(2,1)S(1)}, u32[]{:S(2)}, u32[]{:S(2)}) %collective-permute-start.2) | collective-permute-done | bytes 278560 | tf_op jit(solution)/shard_map/ppermute | solution.py:810
  66.3 0.8 pair.1
  67.0 3.6 %all-to-all-start.2 = ((bf16[8,136,128]{2,1,0:T(8,128)(2,1)}), bf16[8,136,128]{2,1,0:T(8,128)(2,1)S(1)}, u32[]{:S(2)}, u32[]{:S(2)}) async-start(bf16[8,136,128]{2,1,0:T(8,128)(2,1)} %pair.1), calls=%async_computation.2 | async-start | bytes 557056 | tf_op jit(solution)/shard_map/all_to_all | solution.py:813
  70.6 8.7 %beside.1 = (bf16[320,512]{1,0:T(8,128)(2,1)}, f32[32,512]{1,0:T(8,128)}, f32[32,512]{1,0:T(8,128)}, bf16[1024,512]{1,0:T(8,128)(2,1)}) custom-call(s32[1]{0:T(128)} %bitcast.refs_0_.place, f32[2,512]{1,0:T(2,128)S(1)} %get-tuple-element.77.refs_1_, bf16[512,512]{1,0:T(8,128)(2,1)} %refs_2_.3, bf16[8,296,128]{2,1,0:T(8,128)(2,1)} %copy-done, ...), custom_call_target="tpu_custom_call" | custom-call | flops 1073741824 | bytes 7573504 | tf_op jit(solution)/shard_map/beside/pallas_call | solution.py:626
  79.3 1.2 %all-to-all-done.2.refs_0_ = bf16[8,136,128]{2,1,0:T(8,128)(2,1)S(1)} async-done(((bf16[8,136,128]{2,1,0:T(8,128)(2,1)}), bf16[8,136,128]{2,1,0:T(8,128)(2,1)S(1)}, u32[]{:S(2)}, u32[]{:S(2)}) %all-to-all-start.2) | async-done | bytes 278560 | tf_op jit(solution)/shard_map/all_to_all | solution.py:813
  80.5 0.7 final.1
Async XLA Ops:
  32.0 2.0 %copy-start = (bf16[8,296,128]{2,1,0:T(8,128)(2,1)}, bf16[8,296,128]{2,1,0:T(8,128)(2,1)S(1)}, u32[]{:S(2)}) copy-start(bf16[8,296,128]{2,1,0:T(8,128)(2,1)S(1)} %all_to_all.15.refs_1_.refs_3_) | copy-start | bytes 1818628
  32.1 2.0 %collective-permute-start = (bf16[8,296,128]{2,1,0:T(8,128)(2,1)S(1)}, bf16[8,296,128]{2,1,0:T(8,128)(2,1)S(1)}, u32[]{:S(2)}, u32[]{:S(2)}) collective-permute-start(bf16[8,296,128]{2,1,0:T(8,128)(2,1)S(1)} %all_to_all.15.refs_1_.refs_3_), channel_id=1, source_target_pairs={{0,1},{1,0},{2,3},{3,2},{4,5},{5,4},{6,7},{7,6},{8,9},{9,8},{10,11... | collective-permute-start | bytes 1818632 | tf_op jit(solution)/shard_map/ppermute | solution.py:674
  32.1 2.0 %copy-start.2 = (bf16[1024,512]{1,0:T(8,128)(2,1)S(1)}, bf16[1024,512]{1,0:T(8,128)(2,1)}, u32[]{:S(2)}) copy-start(bf16[1024,512]{1,0:T(8,128)(2,1)} %refs_10_.3) | copy-start | bytes 3145732
  34.1 4.0 %copy-start.3 = (bf16[8,296,128]{2,1,0:T(8,128)(2,1)}, bf16[8,296,128]{2,1,0:T(8,128)(2,1)S(1)}, u32[]{:S(2)}) copy-start(bf16[8,296,128]{2,1,0:T(8,128)(2,1)S(1)} %collective-permute-done.refs_2_.refs_4_) | copy-start | bytes 1818628
  34.1 23.6 %copy-start.5 = (bf16[1024,512]{1,0:T(8,128)(2,1)S(1)}, bf16[1024,512]{1,0:T(8,128)(2,1)}, u32[]{:S(2)}) copy-start(bf16[1024,512]{1,0:T(8,128)(2,1)} %latent.1) | copy-start | bytes 3145732
  57.7 2.2 %copy-start.1 = (bf16[8,288,128]{2,1,0:T(8,128)(2,1)}, bf16[8,288,128]{2,1,0:T(8,128)(2,1)S(1)}, u32[]{:S(2)}) copy-start(bf16[8,288,128]{2,1,0:T(8,128)(2,1)S(1)} %all_to_all.16.first.refs_5_) | copy-start | bytes 1769476
  57.7 2.2 %copy-start.6 = (bf16[2048,512]{1,0:T(8,128)(2,1)S(1)}, bf16[2048,512]{1,0:T(8,128)(2,1)}, u32[]{:S(2)}) copy-start(bf16[2048,512]{1,0:T(8,128)(2,1)} %get-tuple-element.71.slope) | copy-start | bytes 6291460
  57.7 2.2 %collective-permute-start.1 = (bf16[8,288,128]{2,1,0:T(8,128)(2,1)S(1)}, bf16[8,288,128]{2,1,0:T(8,128)(2,1)S(1)}, u32[]{:S(2)}, u32[]{:S(2)}) collective-permute-start(bf16[8,288,128]{2,1,0:T(8,128)(2,1)S(1)} %all_to_all.16.first.refs_5_), channel_id=1, source_target_pairs={{0,1},{1,0},{2,3},{3,2},{4,5},{5,4},{6,7},{7,6},{8,9},{9,8},{10,11... | collective-permute-start | bytes 1769480 | tf_op jit(solution)/shard_map/ppermute | solution.py:674
  59.9 4.7 %copy-start.4 = (bf16[8,288,128]{2,1,0:T(8,128)(2,1)}, bf16[8,288,128]{2,1,0:T(8,128)(2,1)S(1)}, u32[]{:S(2)}) copy-start(bf16[8,288,128]{2,1,0:T(8,128)(2,1)S(1)} %collective-permute-done.1.second.refs_6_) | copy-start | bytes 1769476
  64.6 1.6 %collective-permute-start.2 = (bf16[8,136,128]{2,1,0:T(8,128)(2,1)S(1)}, bf16[8,136,128]{2,1,0:T(8,128)(2,1)S(1)}, u32[]{:S(2)}, u32[]{:S(2)}) collective-permute-start(bf16[8,136,128]{2,1,0:T(8,128)(2,1)S(1)} %get-tuple-element.74), channel_id=1, source_target_pairs={{0,1},{1,0},{2,3},{3,2},{4,5},{5,4},{6,7},{7,6},{8,9},{9,8},{10,11... | collective-permute-start | bytes 835592 | tf_op jit(solution)/shard_map/ppermute | solution.py:810
  67.0 13.4 %all-to-all-start.2 = ((bf16[8,136,128]{2,1,0:T(8,128)(2,1)}), bf16[8,136,128]{2,1,0:T(8,128)(2,1)S(1)}, u32[]{:S(2)}, u32[]{:S(2)}) async-start(bf16[8,136,128]{2,1,0:T(8,128)(2,1)} %pair.1), calls=%async_computation.2 | async-start | bytes 557056 | tf_op jit(solution)/shard_map/all_to_all | solution.py:813

commit v5 on v4

--- a/solution.py
+++ b/solution.py
@@ -248,16 +248,12 @@
     block = math.gcd(edges, 512)
     copies[0].wait()
     copies[1].wait()
-
-    def build(start):
+    for start in range(0, edges, block):
         part = slice(start, start + block)
         ids = jnp.broadcast_to(send[:, part].astype(F32), (128, block)).T
         for base in range(0, grid_rows, 128):
             lane = (iota((block, 128), 1) + base).astype(F32)
             picks[part, base : base + 128] = hot(ids == lane)
-
-    for start in range(0, edges // 2, block):
-        build(start)
     copies[2].wait()
     for cut, chunk in zip(cuts, chunks):
         chunk.wait()
@@ -269,8 +265,6 @@
     stores = []
     for start in range(0, edges, block):
         part = slice(start, start + block)
-        if start >= edges // 2:
-            build(start)
         pre = mm(picks[part, :grid_rows], px[:grid_rows, :])
         pre = pre + mm(stack_terms(feat[:, part], FEAT_ORDER).astype(BF), px[grid_rows : grid_rows + 32, :], TN)
         silu, double = halves(pre)
@@ -453,7 +447,7 @@
     terms = jnp.concatenate([stack_terms(0.5 * feat_w[...], WEIGHT_ORDER), blank], 0).astype(BF)
     table = jnp.concatenate([(0.5 * proj.astype(F32)).astype(BF), terms], 0)
     grid_rows = cotangent.shape[0]
-    block = math.gcd(grid_rows, 512)
+    block = math.gcd(grid_rows, 1024)
     total = jnp.zeros((rows, width), F32)
     for start in range(0, grid_rows, block):
         cot = cotangent[start : start + block, :].astype(F32)
@@ -492,20 +486,25 @@
     mesh_grad = (dhmesh[:slots] + dhmesh[slots:]).astype(BF)
     dagg = mm(mesh_grad, node_turned[...]) * agg_slope[...]
     dagg = jnp.concatenate([dagg, jnp.zeros((128 - slots, width), F32)], 0).astype(BF)
-    block = math.gcd(edges, 512)
+    block = math.gcd(edges, 1024)
     for start in range(0, edges, block):
         cut = slice(start, start + block)
         grads[cut, :] = (mm(to_edge[cut, :], dagg) * slope[cut, :].astype(F32)).astype(BF)
-    step = math.gcd(grid_rows, 256)
+    step = math.gcd(grid_rows, 512)
     stores = []
+    terms = stack_terms(feat[...], FEAT_ORDER).astype(BF)
     for start in range(0, grid_rows, step):
         cut = slice(start, start + step)
-        from_row = hot(iota((step, edges), 0) + start == send[...])
-        dpx[cut, :] = mm(from_row, grads[...]).astype(BF)
+        left = hot(iota((step, edges), 0) + start == send[...])
+        if start == 0:
+            left = jnp.concatenate([left, terms], 0)
+        product = mm(left, grads[...])
+        if start == 0:
+            enc_grad = feature_grad(product[step:], feats)
+        dpx[cut, :] = product[:step].astype(BF)
         out = pltpu.make_async_copy(dpx.at[cut, :], dpx_far.at[cut, :], dpx_sems.at[len(stores)])
         out.start()
         stores.append(out)
-    enc_grad = feature_grad(mm(stack_terms(feat[...], FEAT_ORDER).astype(BF), grads[...]), feats)
     sums = jnp.where(iota(enc_grad.shape, 0) < feats, enc_grad, pltpu.roll(dec_grad[...], feats, 0))
     sums_out[...] = sums
     write_shares(give, 1 - core, latent_turned, dpx, sums)

time: 81.5 us -> 80.6 us (0.989)
  no operation moved by 1% of the time
where the time goes in v5:
time: 80.6 us; the launch traced here: 80.3 us
  blocking collectives  43.6 us (54%)
  Pallas kernels  29 us (36%)
  starting transfers between devices  3.92 us (5%)
  waiting for transfers between devices  2.34 us (3%)
  between operations  1.41 us (2%)
    all_to_all x2, blocking collectives, gather(): lax.all_to_all(message, 'lat', 0, 0, tiled=True, axis_index_groups=groups)  43.6 us
    pallas_call x9, Pallas kernels, kernel_call(): pl.pallas_call(body, name=name, out_shape=pinned, in_specs=[SMEM] * len(s...  29 us
    all_to_all x1, starting transfers between devices, gather_plan(): lax.all_to_all(pair, 'lat', 0, 0, tiled=True, axis_index_groups=groups)  3.6 us
  transfers between devices with their start and end apart: 4, of which 3 were waited for; matrix products, arithmetic and copies ran while one was open for 0% of the time, Pallas kernels for 16%

profile of v5, /device:TPU:0, one launch (start us, length us, event | category | flops | bytes accessed | tf_op | source)
XLA Modules:
  0.0 80.3 jit_solution(4197278845708912012)
XLA Ops:
  1.3 6.7 %encoder.1 = (bf16[8,296,128]{2,1,0:T(8,128)(2,1)S(1)}, bf16[2048,512]{1,0:T(8,128)(2,1)}, bf16[64,512]{1,0:T(8,128)(2,1)S(1)}, bf16[64,512]{1,0:T(8,128)(2,1)S(1)}) custom-call(s32[1]{0:T(128)S(6)} %copy.22.refs_0_.count, bf16[1024,512]{1,0:T(8,128)(2,1)} %latent.1, bf16[512,512]{1,0:T(8,128)(2,1)} %refs_9_.1, bf16[320,512]{1,0:T(8,128)(2,1)} %refs_3_.1, ...), custom_call_target="tpu_custom_call" | custom-call | flops 2147483648 | bytes 4792576 | tf_op jit(solution)/shard_map/encoder/pallas_call | solution.py:625
  8.0 23.9 %all_to_all.15.refs_1_.refs_3_ = bf16[8,296,128]{2,1,0:T(8,128)(2,1)S(1)} all-to-all(bf16[8,296,128]{2,1,0:T(8,128)(2,1)S(1)} %get-tuple-element.47), channel_id=1, replica_groups={{0,2,4,6,8,10,12,14},{1,3,5,7,9,11,13,15},{16,18,20,22,24,26,28,30},{17..., dimensions={0} | all-to-all | bytes 1212416 | tf_op jit(solution)/shard_map/all_to_all | solution.py:671
  31.9 0.0 copy-start
  31.9 0.0 collective-permute-start
  31.9 0.0 copy-start.2
  31.9 1.5 %decoder_picks.1 = (bf16[96,3072]{1,0:T(8,128)(2,1)S(1)}, bf16[3072,128]{1,0:T(8,128)(2,1)S(1)}, bf16[512,512]{1,0:T(8,128)(2,1)S(1)}, bf16[512,512]{1,0:T(8,128)(2,1)S(1)}, f32[4,512]{1,0:T(4,128)S(1)}) custom-call(bf16[64,512]{1,0:T(8,128)(2,1)S(1)} %get-tuple-element.50.after.refs_3_, s32[3,1024]{1,0:T(4,128)} %send_any.1, f32[3,4,1024]{2,1,0:T(4,128)} %feat_any.2, ...), custom_call_target="tpu_custom_call" | custom-call | flops 2097152000 | bytes 3616768 | tf_op jit(solution)/shard_map/decoder_picks/pallas_call | solution.py:625
  33.5 0.5 collective-permute-done.refs_2_.refs_4_
  34.0 0.0 copy-start.3
  34.0 0.0 copy-done
  34.0 0.0 copy-done.2
  34.0 0.0 copy-start.5
  34.0 3.6 %decoder.1 = (bf16[8,288,128]{2,1,0:T(8,128)(2,1)S(1)}, f32[2,512]{1,0:T(2,128)S(1)}, bf16[2,64,512]{2,1,0:T(8,128)(2,1)S(1)}, f32[64,512]{1,0:T(8,128)S(1)}, f3...) custom-call(s32[1]{0:T(128)} %bitcast.refs_0_.place, ...), custom_call_target="tpu_custom_call" | custom-call | flops 1610612736 | bytes 5771264 | tf_op jit(solution)/shard_map/decoder/pallas_call | solution.py:625
  37.5 0.0 copy-done.3
  37.6 19.6 %all_to_all.16.first.refs_5_ = bf16[8,288,128]{2,1,0:T(8,128)(2,1)S(1)} all-to-all(bf16[8,288,128]{2,1,0:T(8,128)(2,1)S(1)} %get-tuple-element.57), channel_id=1, replica_groups={{0,2,4,6,8,10,12,14},{1,3,5,7,9,11,13,15},{16,18,20,22,24,26,28,30},{17..., dimensions={0} | all-to-all | bytes 1179648 | tf_op jit(solution)/shard_map/all_to_all | solution.py:671
  57.2 0.0 copy-start.1
  57.2 0.0 copy-start.6
  57.2 0.0 collective-permute-start.1
  57.2 0.0 copy-done.5
  57.2 2.1 %encoder_picks.1 = (bf16[2048,128]{1,0:T(8,128)(2,1)S(1)}, bf16[512,1024]{1,0:T(8,128)(2,1)S(1)}, bf16[512,512]{1,0:T(8,128)(2,1)S(1)}, bf16[512,512]{1,0:T(8,12...) custom-call(s32[1]{0:T(128)S(6)} %copy.22.refs_0_.count, bf16[1024,512]{1,0:T(8,128)(2,1)S(1)} %copy-done.5, ...), custom_call_target="tpu_custom_call" | custom-call | flops 2097152000 | bytes 4808704 | tf_op jit(solution)/shard_map/encoder_picks/pallas_call | solution.py:625
  59.4 0.0 collective-permute-done.1.second.refs_6_
  59.4 0.0 copy-start.4
  59.4 0.0 copy-done.1
  59.4 0.0 copy-done.6
  59.4 4.5 %backward.1 = (bf16[1024,512]{1,0:T(8,128)(2,1)}, bf16[1024,512]{1,0:T(8,128)(2,1)S(1)}, bf16[8,136,128]{2,1,0:T(8,128)(2,1)S(1)}, f32[8,512]{1,0:T(8,128)S(1)}) custom-call(s32[1]{0:T(128)} %bitcast.refs_0_.place, bf16[8,288,128]{2,1,0:T(8,128)(2,1)S(1)} %all_to_all.16.first.refs_5_, bf16[8,288,128]{2,1,0:T(8,128)(2,1)S(1)} %collective-permute-done.1.second.refs_6_, ...), custom_call_target="tpu_custom_call" | custom-call | flops 2147483648 | bytes 8683520 | tf_op jit(solution)/shard_map/backward/pallas_call | solution.py:625
  63.9 0.0 copy-done.4
  63.9 0.3 collective-permute-start.2
  64.2 0.4 keep.1
  64.7 0.9 %collective-permute-done.2.given = bf16[8,136,128]{2,1,0:T(8,128)(2,1)S(1)} collective-permute-done((bf16[8,136,128]{2,1,0:T(8,128)(2,1)S(1)}, bf16[8,136,128]{2,1,0:T(8,128)(2,1)S(1)}, u32[]{:S(2)}, u32[]{:S(2)}) %collective-permute-start.2) | collective-permute-done | bytes 278560 | tf_op jit(solution)/shard_map/ppermute | solution.py:809
  65.5 0.8 pair.1
  66.3 3.6 %all-to-all-start.2 = ((bf16[8,136,128]{2,1,0:T(8,128)(2,1)}), bf16[8,136,128]{2,1,0:T(8,128)(2,1)S(1)}, u32[]{:S(2)}, u32[]{:S(2)}) async-start(bf16[8,136,128]{2,1,0:T(8,128)(2,1)} %pair.1), calls=%async_computation.2 | async-start | bytes 557056 | tf_op jit(solution)/shard_map/all_to_all | solution.py:812
  69.9 8.7 %beside.1 = (bf16[320,512]{1,0:T(8,128)(2,1)}, f32[32,512]{1,0:T(8,128)}, f32[32,512]{1,0:T(8,128)}, bf16[1024,512]{1,0:T(8,128)(2,1)}) custom-call(s32[1]{0:T(128)} %bitcast.refs_0_.place, f32[2,512]{1,0:T(2,128)S(1)} %get-tuple-element.77.refs_1_, bf16[512,512]{1,0:T(8,128)(2,1)} %refs_2_.3, bf16[8,296,128]{2,1,0:T(8,128)(2,1)} %copy-done, ...), custom_call_target="tpu_custom_call" | custom-call | flops 1073741824 | bytes 7573504 | tf_op jit(solution)/shard_map/beside/pallas_call | solution.py:625
  78.6 1.0 %all-to-all-done.2.refs_0_ = bf16[8,136,128]{2,1,0:T(8,128)(2,1)S(1)} async-done(((bf16[8,136,128]{2,1,0:T(8,128)(2,1)}), bf16[8,136,128]{2,1,0:T(8,128)(2,1)S(1)}, u32[]{:S(2)}, u32[]{:S(2)}) %all-to-all-start.2) | async-done | bytes 278560 | tf_op jit(solution)/shard_map/all_to_all | solution.py:812
  79.6 0.7 final.1
Async XLA Ops:
  31.9 2.0 %copy-start = (bf16[8,296,128]{2,1,0:T(8,128)(2,1)}, bf16[8,296,128]{2,1,0:T(8,128)(2,1)S(1)}, u32[]{:S(2)}) copy-start(bf16[8,296,128]{2,1,0:T(8,128)(2,1)S(1)} %all_to_all.15.refs_1_.refs_3_) | copy-start | bytes 1818628
  31.9 2.0 %collective-permute-start = (bf16[8,296,128]{2,1,0:T(8,128)(2,1)S(1)}, bf16[8,296,128]{2,1,0:T(8,128)(2,1)S(1)}, u32[]{:S(2)}, u32[]{:S(2)}) collective-permute-start(bf16[8,296,128]{2,1,0:T(8,128)(2,1)S(1)} %all_to_all.15.refs_1_.refs_3_), channel_id=1, source_target_pairs={{0,1},{1,0},{2,3},{3,2},{4,5},{5,4},{6,7},{7,6},{8,9},{9,8},{10,11... | collective-permute-start | bytes 1818632 | tf_op jit(solution)/shard_map/ppermute | solution.py:673
  31.9 2.0 %copy-start.2 = (bf16[1024,512]{1,0:T(8,128)(2,1)S(1)}, bf16[1024,512]{1,0:T(8,128)(2,1)}, u32[]{:S(2)}) copy-start(bf16[1024,512]{1,0:T(8,128)(2,1)} %refs_10_.3) | copy-start | bytes 3145732
  34.0 3.6 %copy-start.3 = (bf16[8,296,128]{2,1,0:T(8,128)(2,1)}, bf16[8,296,128]{2,1,0:T(8,128)(2,1)S(1)}, u32[]{:S(2)}) copy-start(bf16[8,296,128]{2,1,0:T(8,128)(2,1)S(1)} %collective-permute-done.refs_2_.refs_4_) | copy-start | bytes 1818628
  34.0 23.3 %copy-start.5 = (bf16[1024,512]{1,0:T(8,128)(2,1)S(1)}, bf16[1024,512]{1,0:T(8,128)(2,1)}, u32[]{:S(2)}) copy-start(bf16[1024,512]{1,0:T(8,128)(2,1)} %latent.1) | copy-start | bytes 3145732
  57.2 2.2 %copy-start.1 = (bf16[8,288,128]{2,1,0:T(8,128)(2,1)}, bf16[8,288,128]{2,1,0:T(8,128)(2,1)S(1)}, u32[]{:S(2)}) copy-start(bf16[8,288,128]{2,1,0:T(8,128)(2,1)S(1)} %all_to_all.16.first.refs_5_) | copy-start | bytes 1769476
  57.2 2.2 %copy-start.6 = (bf16[2048,512]{1,0:T(8,128)(2,1)S(1)}, bf16[2048,512]{1,0:T(8,128)(2,1)}, u32[]{:S(2)}) copy-start(bf16[2048,512]{1,0:T(8,128)(2,1)} %get-tuple-element.71.slope) | copy-start | bytes 6291460
  57.2 2.2 %collective-permute-start.1 = (bf16[8,288,128]{2,1,0:T(8,128)(2,1)S(1)}, bf16[8,288,128]{2,1,0:T(8,128)(2,1)S(1)}, u32[]{:S(2)}, u32[]{:S(2)}) collective-permute-start(bf16[8,288,128]{2,1,0:T(8,128)(2,1)S(1)} %all_to_all.16.first.refs_5_), channel_id=1, source_target_pairs={{0,1},{1,0},{2,3},{3,2},{4,5},{5,4},{6,7},{7,6},{8,9},{9,8},{10,11... | collective-permute-start | bytes 1769480 | tf_op jit(solution)/shard_map/ppermute | solution.py:673
  59.4 4.5 %copy-start.4 = (bf16[8,288,128]{2,1,0:T(8,128)(2,1)}, bf16[8,288,128]{2,1,0:T(8,128)(2,1)S(1)}, u32[]{:S(2)}) copy-start(bf16[8,288,128]{2,1,0:T(8,128)(2,1)S(1)} %collective-permute-done.1.second.refs_6_) | copy-start | bytes 1769476
  63.9 1.6 %collective-permute-start.2 = (bf16[8,136,128]{2,1,0:T(8,128)(2,1)S(1)}, bf16[8,136,128]{2,1,0:T(8,128)(2,1)S(1)}, u32[]{:S(2)}, u32[]{:S(2)}) collective-permute-start(bf16[8,136,128]{2,1,0:T(8,128)(2,1)S(1)} %get-tuple-element.74), channel_id=1, source_target_pairs={{0,1},{1,0},{2,3},{3,2},{4,5},{5,4},{6,7},{7,6},{8,9},{9,8},{10,11... | collective-permute-start | bytes 835592 | tf_op jit(solution)/shard_map/ppermute | solution.py:809
  66.3 13.3 %all-to-all-start.2 = ((bf16[8,136,128]{2,1,0:T(8,128)(2,1)}), bf16[8,136,128]{2,1,0:T(8,128)(2,1)S(1)}, u32[]{:S(2)}, u32[]{:S(2)}) async-start(bf16[8,136,128]{2,1,0:T(8,128)(2,1)} %pair.1), calls=%async_computation.2 | async-start | bytes 557056 | tf_op jit(solution)/shard_map/all_to_all | solution.py:812

commit v6 on v5

--- a/solution.py
+++ b/solution.py
@@ -288,19 +288,55 @@
     id_row = (digits[0] * 256.0 + digits[1]).astype(jnp.int32)
     served = mm(hot(iota((mesh.shape[0], slots), 0) == id_row), mesh[...], TN)
     served_out[...] = served.astype(BF)
+    code = scale_codes(jnp.max(jnp.abs(total), 1, keepdims=True))
+    fixed = to_fixed(total * scale_values(code, -1))
+    own_out[...] = (total - fixed.astype(F32) * scale_values(code, 1)).astype(BF)
+    half = fixed.astype(jnp.int16)
+    latents = to_fixed(served * (1.0 / LATENT_STEP))
+    code_row = jnp.broadcast_to(code.astype(F32), (slots, 128)).T[:1, :]
     lane = iota((slots, 128), 1)
     back = iota((slots, 128), 0)
-    wide = mm(digits[0].astype(BF), hot(lane == back)) + mm(digits[1].astype(BF), hot(lane == back + slots))
-    id_rows = jnp.where(iota((8, 128), 0) == 0, wide, 0.0)
-    half = total.astype(BF)
-    own_out[...] = (total - half.astype(F32)).astype(BF)
+    wide = 256.0 * mm(digits[0].astype(BF), hot(lane == back)) + mm(digits[1].astype(BF), hot(lane == back))
+    wide = wide + mm(code_row.astype(BF), hot(lane == back + slots))
+    id_rows = jnp.where(iota((8, 128), 0) == 0, wide, 0.0).astype(jnp.int32)
     for chip in range(chips):
         write_slots(message, chip, half)
-        rows = served[2 * cap * chip : 2 * cap * (chip + 1)]
+        rows = latents[2 * cap * chip : 2 * cap * (chip + 1)]
         tail = [rows[:, base : base + 128] for base in range(0, width, 128)]
-        message[chip, slots * (width // 128) :, :] = jnp.concatenate([*tail, id_rows], 0).astype(BF)
+        message[chip, slots * (width // 128) :, :] = jnp.concatenate([*tail, id_rows], 0).astype(jnp.int16)
     for out in stores:
         out.wait()
+
+
+POWERS = range(-40, 24)
+LATENT_STEP = 6.0 / 32000.0
+
+
+def scale_codes(peak):
+    code = jnp.zeros(peak.shape, jnp.int32)
+    for power in POWERS[:-1]:
+        code = code + jnp.where(peak > 32000.0 * 2.0**power, 1, 0)
+    return code
+
+
+def scale_values(code, sign):
+    value = jnp.zeros(code.shape, F32)
+    for index, power in enumerate(POWERS):
+        value = jnp.where(code == index, 2.0 ** (sign * power), value)
+    return value
+
+
+def to_fixed(value):
+    return jnp.floor(value + 0.5).astype(jnp.int32)
+
+
+def fixed_rows(ref, slots, width):
+    parts = [
+        jnp.concatenate([ref[chip, base : base + slots, :].astype(jnp.int32) for chip in range(ref.shape[0])], 0)
+        for base in range(0, slots * (width // 128), slots)
+    ]
+    value = jnp.concatenate(parts, 1)
+    return lax.shift_right_arithmetic(value, 8).astype(F32).astype(BF), (value & 255).astype(F32).astype(BF)
 
 
 def write_slots(message, chip, value):
@@ -338,41 +374,53 @@
     span = chips * slots
     parts = width // 128
     core = lax.rem(me, 2)
-    table = jnp.zeros((owners, 128), F32)
+    tables = [jnp.zeros((owners, 128), F32)] * 2
     latent = jnp.zeros((slots, width), F32)
     for piece, ref in enumerate((first, second)):
         ids, rows = [], []
         for chip in range(chips):
-            tail = ref[chip, slots * parts :, :].astype(F32)
+            tail = ref[chip, slots * parts :, :].astype(jnp.int32)
             ids.append(tail[8 * parts :])
             rows.append(jnp.concatenate([tail[8 * part : 8 * part + 8] for part in range(parts)], 1))
-        ids = jnp.concatenate(ids, 0).astype(BF)
-        rows = jnp.concatenate(rows, 0).astype(BF)
+        ids = jnp.concatenate(ids, 0)
+        rows = jnp.concatenate(rows, 0)
         shape = (owners, 8 * chips)
-        table = table + mm(hot(iota(shape, 1) == (iota(shape, 0) - piece * chips) * 8), ids)
+        take = hot(iota(shape, 1) == (iota(shape, 0) - piece * chips) * 8)
+        for index, digit in enumerate((lax.shift_right_arithmetic(ids, 8), ids & 255)):
+            tables[index] = tables[index] + mm(take, digit.astype(F32).astype(BF))
         shape = (slots, 8 * chips)
         window = iota(shape, 0)
         owner = lax.div(window, cap)
         held = lax.rem(owner, 2) == (core if piece == 0 else 1 - core)
         at = lax.div(owner, 2) * 8 + cap * core + lax.rem(window, cap)
-        latent = latent + mm(hot(held & (iota(shape, 1) == at)), rows)
-    digits = table.astype(BF)
-    shape = (slots, owners)
-    mine = mm(hot(holder_of(shape, 1, chips, core) == lax.div(iota(shape, 0), cap)), digits)
+        pick = hot(held & (iota(shape, 1) == at))
+        high = lax.shift_right_arithmetic(rows, 8).astype(F32).astype(BF)
+        latent = latent + 256.0 * mm(pick, high) + mm(pick, (rows & 255).astype(F32).astype(BF))
+    latent = (latent * LATENT_STEP).astype(BF).astype(F32)
+    digits = jnp.concatenate(tables, 0).astype(BF)
+    shape = (slots, 2 * owners)
+    half = lax.rem(iota(shape, 1), owners)
+    holder = jnp.where(half < chips, 2 * half + core, 2 * (half - chips) + 1 - core)
+    wanted = jnp.where(holder == lax.div(iota(shape, 0), cap), 1.0, 0.0)
+    mine = mm((wanted * jnp.where(iota(shape, 1) < owners, 256.0, 1.0)).astype(BF), digits)
     lane = iota((slots, 128), 1) - cap * me - lax.rem(iota((slots, 128), 0), cap)
-    scaled = jnp.where(lane == 0, 256.0 * mine, jnp.where(lane == slots, mine, 0.0))
-    own_key = jnp.sum(scaled, 1, keepdims=True)
+    own_key = jnp.sum(jnp.where(lane == 0, mine, 0.0), 1, keepdims=True)
     own_key = own_key + (lax.div(iota((slots, 1), 0), cap) * mesh_rows).astype(F32)
-    keys, same = [], []
+    keys, same, scales = [], [], []
     for piece in range(2):
         band, owner, place = gathered_slots(piece, chips, core, cap, (1, span), 1)
-        at = iota((128, span), 0) - cap * band - place
-        weight = jnp.where(at == 0, 256.0, jnp.where(at == slots, 1.0, 0.0)).astype(BF)
-        value = jnp.where(holder_of((owners, 1), 0, chips, core) == owner, mm(digits, weight), 0.0)
+        spread = mm(digits, hot(iota((128, span), 0) == cap * band + place))
+        value = 256.0 * spread[:owners] + spread[owners:]
+        value = jnp.where(holder_of((owners, 1), 0, chips, core) == owner, value, 0.0)
         key = jnp.sum(value, 0, keepdims=True) + (owner * mesh_rows).astype(F32)
         keys.append(key)
         same.append(hot(key == own_key))
-    return keys, same, latent
+        index = iota((1, span), 1)
+        spread = mm(digits[owners:], hot(iota((128, span), 0) == slots + lax.rem(index, slots)))
+        source = iota((owners, 1), 0) - piece * chips == lax.div(index, slots)
+        code = jnp.sum(jnp.where(source, spread, 0.0), 0, keepdims=True)
+        scales.append(scale_values(code.astype(jnp.int32), 1))
+    return keys, same, scales, latent
 
 
 def decoder_picks(
@@ -401,7 +449,7 @@
 
 def encoder_picks(
     count, latent, receive_any, dec_any, node_any, send_any, feat_any,
-    to_edge, latent_turned, dec_turned, node_turned, send, feat, receive, dec_w, node_w, sems,
+    to_edge, latent_turned, chain, send, feat, receive, dec_w, node_w, sems,
 ):
     sources = (receive_any, dec_any, node_any, send_any, feat_any)
     copies = fetch(sources, (receive, dec_w, node_w, send, feat), sems)
@@ -415,8 +463,7 @@
         to_edge[part, :] = jnp.where(iota((128, block), 0) == slot, 1.0, 0.0).T.astype(BF)
     for copy in copies[1:3]:
         copy.wait()
-    dec_turned[...] = dec_w[...].T
-    node_turned[...] = node_w[...].T
+    chain[...] = mm(node_w[...], dec_w[...]).T.astype(BF)
     latent_turned[...] = latent[...].T
     for copy in copies[3:]:
         copy.wait()
@@ -427,12 +474,15 @@
     message, keys_out, same_out, slope_out, grad_out, mine_out, rest_out,
 ):
     slots, width = extra.shape
-    keys, same, latent = slot_matches(first, second, place[0], cap, mesh_rows, width)
+    keys, same, scales, latent = slot_matches(first, second, place[0], cap, mesh_rows, width)
     agg = jnp.zeros((slots, width), F32)
     for piece, ref in enumerate((first, second)):
         keys_out[piece : piece + 1, :] = keys[piece]
         same_out[piece] = same[piece]
-        agg = agg + mm(same[piece], slot_rows(ref, slots, width))
+        keys_out[2 + piece : 3 + piece, :] = scales[piece]
+        weight = (same[piece].astype(F32) * scales[piece]).astype(BF)
+        high, low = fixed_rows(ref, slots, width)
+        agg = agg + 256.0 * mm(weight, high) + mm(weight, low)
     shape = (same[0].shape[1], slots)
     chosen = hot(iota(shape, 0) == slots * lax.div(place[0], 2) + iota(shape, 1))
     mine = mm(same[0], chosen).astype(BF)
@@ -470,7 +520,7 @@
 
 
 def backward_kernel(
-    place, first, second, same, mine, rest, agg_slope, dec_grad, to_edge, latent_turned, dec_turned, node_turned,
+    place, first, second, same, mine, rest, agg_slope, dec_grad, to_edge, latent_turned, chain,
     send, feat, slope, dpx_far, dpx, give, sums_out, grads, dpx_sems,
 ):
     slots = same.shape[1]
@@ -482,9 +532,8 @@
     dproj = dproj + mm(mine[...], rest[...])
     high = dproj.astype(BF)
     low = (dproj - high.astype(F32)).astype(BF)
-    dhmesh = mm(jnp.concatenate([high, low], 0), dec_turned[...])
-    mesh_grad = (dhmesh[:slots] + dhmesh[slots:]).astype(BF)
-    dagg = mm(mesh_grad, node_turned[...]) * agg_slope[...]
+    dact = mm(jnp.concatenate([high, low], 0), chain[...])
+    dagg = (dact[:slots] + dact[slots:]) * agg_slope[...]
     dagg = jnp.concatenate([dagg, jnp.zeros((128 - slots, width), F32)], 0).astype(BF)
     block = math.gcd(edges, 1024)
     for start in range(0, edges, block):
@@ -565,11 +614,17 @@
     block = width // owners
     key = jnp.concatenate([keys[0:1, :], keys[1:2, :]], 1)
     down = jnp.broadcast_to(key, (128, 2 * span)).T
-    same = jnp.concatenate([hot(down == key[:, base : base + 128]) for base in range(0, 2 * span, 128)], 1)
+    scale = jnp.concatenate([keys[2:3, :], keys[3:4, :]], 1)
+    same = [
+        jnp.where(down == key[:, base : base + 128], scale[:, base : base + 128], 0.0).astype(BF)
+        for base in range(0, 2 * span, 128)
+    ]
+    same = jnp.concatenate(same, 1)
     for copy in copies[:3]:
         copy.wait()
-    forward = jnp.concatenate([slot_rows(ref, slots, width) for ref in (first, second)], 0)
-    act = halves(0.5 * mm(same, forward))[0].astype(BF)
+    fixed = [fixed_rows(ref, slots, width) for ref in (first, second)]
+    high, low = [jnp.concatenate([a, b], 0) for a, b in zip(*fixed)]
+    act = halves(0.5 * (256.0 * mm(same, high) + mm(same, low)))[0].astype(BF)
     shape = (width, 128)
     mine = hot((iota(shape, 0) == block * me + iota(shape, 1)) & (iota(shape, 1) < block))
     node_cols = mm(node_w[...], mine).astype(BF)
@@ -681,7 +736,7 @@
         [],
         [grid_latent, enc_proj, mesh_latent, send, receive, enc_feat, enc_feat_w.T, serve_rows[0].T],
         [
-            ((chips, parts * (slots + 8) + 8, 128), BF),
+            ((chips, parts * (slots + 8) + 8, 128), jnp.int16),
             ((edges, width), BF),
             ((slots, width), BF),
             ((slots, width), BF),
@@ -728,7 +783,7 @@
         [],
         [
             ((chips, parts * slots + slots * share // 128, 128), BF),
-            ((2, span), F32),
+            ((4, span), F32),
             ((2, slots, span), BF),
             ((slots, width), F32),
             ((2 * feats, width), F32),
@@ -740,7 +795,7 @@
         20,
     )
     first_back, second_back, pick_count = gather(message, enc_count)
-    to_edge, latent_turned, dec_turned, node_turned, near_send, near_feat = kernel_call(
+    to_edge, latent_turned, chain, near_send, near_feat = kernel_call(
         encoder_picks,
         "encoder_picks",
         [pick_count],
@@ -749,7 +804,6 @@
         [
             ((edges, 128), BF),
             ((width, grid_rows), BF),
-            ((width, width), BF),
             ((width, width), BF),
             ((1, edges), jnp.int32),
             ((feats, edges), F32),
@@ -774,8 +828,7 @@
             dec_grad,
             to_edge,
             latent_turned,
-            dec_turned,
-            node_turned,
+            chain,
             near_send,
             near_feat,
             slope,
@@ -872,7 +925,7 @@
         and width % (8 * owners) == 0
         and 128 % (width // chips) == 0
         and owners * cap * (width // chips) % 2048 == 0
-        and mesh_latent.shape[0] <= 65536
+        and mesh_latent.shape[0] <= 32768
         and mesh_latent.shape[0] * owners < 1 << 24
         and args[0].shape[0] % 128 == 0
         and args[3].shape[0] % 128 == 0

time: 80.6 us -> 81.3 us (level)
  Pallas kernels: 29 us -> 30.8 us
  waiting for transfers between devices: 2.34 us -> 1.38 us
    pallas_call x9, Pallas kernels: 29 us -> 30.8 us  [kernel_call(): pl.pallas_call(body, name=name, out_shape=pinned, in_specs=[SMEM] * len(s...]
    all_to_all x1, waiting for transfers between devices: 0.99 us -> 0.01 us  [gather_plan(): lax.all_to_all(pair, 'lat', 0, 0, tiled=True, axis_index_groups=groups)]
  transfers between devices with their start and end apart: 4 -> 4, of which waited for: 3 -> 2; matrix products, arithmetic and copies ran while one was open for 0% -> 0% of each run, Pallas kernels for 16% -> 17%
where the time goes in v6:
time: 81.3 us; the launch traced here: 80.9 us
  blocking collectives  43.6 us (54%)
  Pallas kernels  30.8 us (38%)
  starting transfers between devices  3.71 us (5%)
  between operations  1.41 us (2%)
  waiting for transfers between devices  1.38 us (2%)
    all_to_all x2, blocking collectives, gather(): lax.all_to_all(message, 'lat', 0, 0, tiled=True, axis_index_groups=groups)  43.6 us
    pallas_call x9, Pallas kernels, kernel_call(): pl.pallas_call(body, name=name, out_shape=pinned, in_specs=[SMEM] * len(s...  30.8 us
    all_to_all x1, starting transfers between devices, gather_plan(): lax.all_to_all(pair, 'lat', 0, 0, tiled=True, axis_index_groups=groups)  3.42 us
  transfers between devices with their start and end apart: 4, of which 2 were waited for; matrix products, arithmetic and copies ran while one was open for 0% of the time, Pallas kernels for 17%

profile of v6, /device:TPU:0, one launch (start us, length us, event | category | flops | bytes accessed | tf_op | source)
XLA Modules:
  0.0 80.9 jit_solution(18048133700956570406)
XLA Ops:
  1.3 7.0 %encoder.1 = (s16[8,296,128]{2,1,0:T(8,128)(2,1)S(1)}, bf16[2048,512]{1,0:T(8,128)(2,1)}, bf16[64,512]{1,0:T(8,128)(2,1)S(1)}, bf16[64,512]{1,0:T(8,128)(2,1)S(1)}) custom-call(s32[1]{0:T(128)S(6)} %copy.22.refs_0_.count, bf16[1024,512]{1,0:T(8,128)(2,1)} %latent.1, bf16[512,512]{1,0:T(8,128)(2,1)} %refs_9_.1, bf16[320,512]{1,0:T(8,128)(2,1)} %refs_3_.1, ...), custom_call_target="tpu_custom_call" | custom-call | flops 2147483648 | bytes 4792576 | tf_op jit(solution)/shard_map/encoder/pallas_call | solution.py:680
  8.2 23.9 %all_to_all.15.refs_1_.refs_3_ = s16[8,296,128]{2,1,0:T(8,128)(2,1)S(1)} all-to-all(s16[8,296,128]{2,1,0:T(8,128)(2,1)S(1)} %get-tuple-element.46), channel_id=1, replica_groups={{0,2,4,6,8,10,12,14},{1,3,5,7,9,11,13,15},{16,18,20,22,24,26,28,30},{17..., dimensions={0} | all-to-all | bytes 1212416 | tf_op jit(solution)/shard_map/all_to_all | solution.py:726
  32.2 0.0 copy-start
  32.2 0.0 collective-permute-start
  32.2 0.0 copy-start.2
  32.2 1.5 %decoder_picks.1 = (bf16[96,3072]{1,0:T(8,128)(2,1)S(1)}, bf16[3072,128]{1,0:T(8,128)(2,1)S(1)}, bf16[512,512]{1,0:T(8,128)(2,1)S(1)}, bf16[512,512]{1,0:T(8,128)(2,1)S(1)}, f32[4,512]{1,0:T(4,128)S(1)}) custom-call(bf16[64,512]{1,0:T(8,128)(2,1)S(1)} %get-tuple-element.49.after.refs_3_, s32[3,1024]{1,0:T(4,128)} %send_any.1, f32[3,4,1024]{2,1,0:T(4,128)} %feat_any.2, ...), custom_call_target="tpu_custom_call" | custom-call | flops 2097152000 | bytes 3616768 | tf_op jit(solution)/shard_map/decoder_picks/pallas_call | solution.py:680
  33.7 0.5 collective-permute-done.refs_2_.refs_4_
  34.2 0.0 copy-start.3
  34.2 0.0 copy-done
  34.2 0.0 copy-done.2
  34.2 0.0 copy-start.5
  34.2 4.2 %decoder.1 = (bf16[8,288,128]{2,1,0:T(8,128)(2,1)S(1)}, f32[4,512]{1,0:T(4,128)S(1)}, bf16[2,64,512]{2,1,0:T(8,128)(2,1)S(1)}, f32[64,512]{1,0:T(8,128)S(1)}, f3...) custom-call(s32[1]{0:T(128)} %bitcast.refs_0_.place, ...), custom_call_target="tpu_custom_call" | custom-call | flops 1610612736 | bytes 5775360 | tf_op jit(solution)/shard_map/decoder/pallas_call | solution.py:680
  38.4 0.0 copy-done.3
  38.4 19.6 %all_to_all.16.first.refs_5_ = bf16[8,288,128]{2,1,0:T(8,128)(2,1)S(1)} all-to-all(bf16[8,288,128]{2,1,0:T(8,128)(2,1)S(1)} %get-tuple-element.56), channel_id=1, replica_groups={{0,2,4,6,8,10,12,14},{1,3,5,7,9,11,13,15},{16,18,20,22,24,26,28,30},{17..., dimensions={0} | all-to-all | bytes 1179648 | tf_op jit(solution)/shard_map/all_to_all | solution.py:726
  58.0 0.0 copy-start.1
  58.0 0.0 copy-start.6
  58.0 0.0 collective-permute-start.1
  58.0 0.0 copy-done.5
  58.1 2.1 %encoder_picks.1 = (bf16[2048,128]{1,0:T(8,128)(2,1)S(1)}, bf16[512,1024]{1,0:T(8,128)(2,1)S(1)}, bf16[512,512]{1,0:T(8,128)(2,1)S(1)}, s32[1,2048]{1,0:T(1,128)S(1)}, f32[4,2048]{1,0:T(4,128)S(1)}) custom-call(s32[1]{0:T(128)S(6)} %copy.22.refs_0_.count, bf16[1024,512]{1,0:T(8,128)(2,1)S(1)} %copy-done.5, s32[1,2048]{1,0:T(1,128)} %bitcast.15, ...), custom_call_target="tpu_custom_call" | custom-call | flops 2097152000 | bytes 4284416 | tf_op jit(solution)/shard_map/encoder_picks/pallas_call | solution.py:680
  60.1 0.0 collective-permute-done.1.second.refs_6_
  60.2 0.0 copy-start.4
  60.2 0.0 copy-done.1
  60.2 0.0 copy-done.6
  60.2 4.3 %backward.1 = (bf16[1024,512]{1,0:T(8,128)(2,1)}, bf16[1024,512]{1,0:T(8,128)(2,1)S(1)}, bf16[8,136,128]{2,1,0:T(8,128)(2,1)S(1)}, f32[8,512]{1,0:T(8,128)S(1)}) custom-call(s32[1]{0:T(128)} %bitcast.refs_0_.place, bf16[8,288,128]{2,1,0:T(8,128)(2,1)S(1)} %all_to_all.16.first.refs_5_, bf16[8,288,128]{2,1,0:T(8,128)(2,1)S(1)} %collective-permute-done.1.second.refs_6_, ...), custom_call_target="tpu_custom_call" | custom-call | flops 2147483648 | bytes 8159232 | tf_op jit(solution)/shard_map/backward/pallas_call | solution.py:680
  64.6 0.0 copy-done.4
  64.6 0.3 collective-permute-start.2
  64.9 0.4 keep.1
  65.3 0.9 %collective-permute-done.2.given = bf16[8,136,128]{2,1,0:T(8,128)(2,1)S(1)} collective-permute-done((bf16[8,136,128]{2,1,0:T(8,128)(2,1)S(1)}, bf16[8,136,128]{2,1,0:T(8,128)(2,1)S(1)}, u32[]{:S(2)}, u32[]{:S(2)}) %collective-permute-start.2) | collective-permute-done | bytes 278560 | tf_op jit(solution)/shard_map/ppermute | solution.py:862
  66.2 0.8 pair.1
  67.0 3.4 %all-to-all-start.2 = ((bf16[8,136,128]{2,1,0:T(8,128)(2,1)}), bf16[8,136,128]{2,1,0:T(8,128)(2,1)S(1)}, u32[]{:S(2)}, u32[]{:S(2)}) async-start(bf16[8,136,128]{2,1,0:T(8,128)(2,1)} %pair.1), calls=%async_computation.2 | async-start | bytes 557056 | tf_op jit(solution)/shard_map/all_to_all | solution.py:865
  70.4 9.8 %beside.1 = (bf16[320,512]{1,0:T(8,128)(2,1)}, f32[32,512]{1,0:T(8,128)}, f32[32,512]{1,0:T(8,128)}, bf16[1024,512]{1,0:T(8,128)(2,1)}) custom-call(s32[1]{0:T(128)} %bitcast.refs_0_.place, f32[4,512]{1,0:T(4,128)S(1)} %get-tuple-element.75.refs_1_, bf16[512,512]{1,0:T(8,128)(2,1)} %refs_2_.3, s16[8,296,128]{2,1,0:T(8,128)(2,1)} %copy-done, ...), custom_call_target="tpu_custom_call" | custom-call | flops 1073741824 | bytes 7577600 | tf_op jit(solution)/shard_map/beside/pallas_call | solution.py:680
  80.2 0.0 all-to-all-done.2.refs_0_
  80.2 0.7 final.1
Async XLA Ops:
  32.2 2.0 %copy-start = (s16[8,296,128]{2,1,0:T(8,128)(2,1)}, s16[8,296,128]{2,1,0:T(8,128)(2,1)S(1)}, u32[]{:S(2)}) copy-start(s16[8,296,128]{2,1,0:T(8,128)(2,1)S(1)} %all_to_all.15.refs_1_.refs_3_) | copy-start | bytes 1818628
  32.2 2.0 %collective-permute-start = (s16[8,296,128]{2,1,0:T(8,128)(2,1)S(1)}, s16[8,296,128]{2,1,0:T(8,128)(2,1)S(1)}, u32[]{:S(2)}, u32[]{:S(2)}) collective-permute-start(s16[8,296,128]{2,1,0:T(8,128)(2,1)S(1)} %all_to_all.15.refs_1_.refs_3_), channel_id=1, source_target_pairs={{0,1},{1,0},{2,3},{3,2},{4,5},{5,4},{6,7},{7,6},{8,9},{9,8},{10,11... | collective-permute-start | bytes 1818632 | tf_op jit(solution)/shard_map/ppermute | solution.py:728
  32.2 2.0 %copy-start.2 = (bf16[1024,512]{1,0:T(8,128)(2,1)S(1)}, bf16[1024,512]{1,0:T(8,128)(2,1)}, u32[]{:S(2)}) copy-start(bf16[1024,512]{1,0:T(8,128)(2,1)} %refs_10_.3) | copy-start | bytes 3145732
  34.2 4.2 %copy-start.3 = (s16[8,296,128]{2,1,0:T(8,128)(2,1)}, s16[8,296,128]{2,1,0:T(8,128)(2,1)S(1)}, u32[]{:S(2)}) copy-start(s16[8,296,128]{2,1,0:T(8,128)(2,1)S(1)} %collective-permute-done.refs_2_.refs_4_) | copy-start | bytes 1818628
  34.2 23.9 %copy-start.5 = (bf16[1024,512]{1,0:T(8,128)(2,1)S(1)}, bf16[1024,512]{1,0:T(8,128)(2,1)}, u32[]{:S(2)}) copy-start(bf16[1024,512]{1,0:T(8,128)(2,1)} %latent.1) | copy-start | bytes 3145732
  58.0 2.1 %copy-start.1 = (bf16[8,288,128]{2,1,0:T(8,128)(2,1)}, bf16[8,288,128]{2,1,0:T(8,128)(2,1)S(1)}, u32[]{:S(2)}) copy-start(bf16[8,288,128]{2,1,0:T(8,128)(2,1)S(1)} %all_to_all.16.first.refs_5_) | copy-start | bytes 1769476
  58.0 2.2 %copy-start.6 = (bf16[2048,512]{1,0:T(8,128)(2,1)S(1)}, bf16[2048,512]{1,0:T(8,128)(2,1)}, u32[]{:S(2)}) copy-start(bf16[2048,512]{1,0:T(8,128)(2,1)} %get-tuple-element.69.slope) | copy-start | bytes 6291460
  58.0 2.1 %collective-permute-start.1 = (bf16[8,288,128]{2,1,0:T(8,128)(2,1)S(1)}, bf16[8,288,128]{2,1,0:T(8,128)(2,1)S(1)}, u32[]{:S(2)}, u32[]{:S(2)}) collective-permute-start(bf16[8,288,128]{2,1,0:T(8,128)(2,1)S(1)} %all_to_all.16.first.refs_5_), channel_id=1, source_target_pairs={{0,1},{1,0},{2,3},{3,2},{4,5},{5,4},{6,7},{7,6},{8,9},{9,8},{10,11... | collective-permute-start | bytes 1769480 | tf_op jit(solution)/shard_map/ppermute | solution.py:728
  60.2 4.4 %copy-start.4 = (bf16[8,288,128]{2,1,0:T(8,128)(2,1)}, bf16[8,288,128]{2,1,0:T(8,128)(2,1)S(1)}, u32[]{:S(2)}) copy-start(bf16[8,288,128]{2,1,0:T(8,128)(2,1)S(1)} %collective-permute-done.1.second.refs_6_) | copy-start | bytes 1769476
  64.6 1.6 %collective-permute-start.2 = (bf16[8,136,128]{2,1,0:T(8,128)(2,1)S(1)}, bf16[8,136,128]{2,1,0:T(8,128)(2,1)S(1)}, u32[]{:S(2)}, u32[]{:S(2)}) collective-permute-start(bf16[8,136,128]{2,1,0:T(8,128)(2,1)S(1)} %get-tuple-element.72), channel_id=1, source_target_pairs={{0,1},{1,0},{2,3},{3,2},{4,5},{5,4},{6,7},{7,6},{8,9},{9,8},{10,11... | collective-permute-start | bytes 835592 | tf_op jit(solution)/shard_map/ppermute | solution.py:862
  67.0 13.3 %all-to-all-start.2 = ((bf16[8,136,128]{2,1,0:T(8,128)(2,1)}), bf16[8,136,128]{2,1,0:T(8,128)(2,1)S(1)}, u32[]{:S(2)}, u32[]{:S(2)}) async-start(bf16[8,136,128]{2,1,0:T(8,128)(2,1)} %pair.1), calls=%async_computation.2 | async-start | bytes 557056 | tf_op jit(solution)/shard_map/all_to_all | solution.py:865

commit v7 on v6

--- a/solution.py
+++ b/solution.py
@@ -288,9 +288,9 @@
     id_row = (digits[0] * 256.0 + digits[1]).astype(jnp.int32)
     served = mm(hot(iota((mesh.shape[0], slots), 0) == id_row), mesh[...], TN)
     served_out[...] = served.astype(BF)
-    code = scale_codes(jnp.max(jnp.abs(total), 1, keepdims=True))
-    fixed = to_fixed(total * scale_values(code, -1))
-    own_out[...] = (total - fixed.astype(F32) * scale_values(code, 1)).astype(BF)
+    code, scale, inverse = scale_codes(jnp.max(jnp.abs(total), 1, keepdims=True))
+    fixed = to_fixed(total * inverse)
+    own_out[...] = (total - fixed.astype(F32) * scale).astype(BF)
     half = fixed.astype(jnp.int16)
     latents = to_fixed(served * (1.0 / LATENT_STEP))
     code_row = jnp.broadcast_to(code.astype(F32), (slots, 128)).T[:1, :]
@@ -308,21 +308,26 @@
         out.wait()
 
 
-POWERS = range(-40, 24)
+LEAST_POWER = -40
 LATENT_STEP = 6.0 / 32000.0
 
 
 def scale_codes(peak):
     code = jnp.zeros(peak.shape, jnp.int32)
-    for power in POWERS[:-1]:
-        code = code + jnp.where(peak > 32000.0 * 2.0**power, 1, 0)
-    return code
-
-
-def scale_values(code, sign):
-    value = jnp.zeros(code.shape, F32)
-    for index, power in enumerate(POWERS):
-        value = jnp.where(code == index, 2.0 ** (sign * power), value)
+    scale = jnp.full(peak.shape, 2.0**LEAST_POWER, F32)
+    inverse = jnp.full(peak.shape, 2.0**-LEAST_POWER, F32)
+    for bit in (32, 16, 8, 4, 2, 1):
+        more = peak > 32000.0 * (scale * 2.0 ** (bit - 1))
+        code = code + jnp.where(more, bit, 0)
+        scale = scale * jnp.where(more, 2.0**bit, 1.0)
+        inverse = inverse * jnp.where(more, 2.0**-bit, 1.0)
+    return code, scale, inverse
+
+
+def scale_values(code):
+    value = jnp.full(code.shape, 2.0**LEAST_POWER, F32)
+    for bit in range(6):
+        value = value * jnp.where((lax.shift_right_logical(code, bit) & 1) == 1, 2.0 ** (1 << bit), 1.0)
     return value
 
 
@@ -419,7 +424,7 @@
         spread = mm(digits[owners:], hot(iota((128, span), 0) == slots + lax.rem(index, slots)))
         source = iota((owners, 1), 0) - piece * chips == lax.div(index, slots)
         code = jnp.sum(jnp.where(source, spread, 0.0), 0, keepdims=True)
-        scales.append(scale_values(code.astype(jnp.int32), 1))
+        scales.append(scale_values(code.astype(jnp.int32)))
     return keys, same, scales, latent
 
 
@@ -622,9 +627,8 @@
     same = jnp.concatenate(same, 1)
     for copy in copies[:3]:
         copy.wait()
-    fixed = [fixed_rows(ref, slots, width) for ref in (first, second)]
-    high, low = [jnp.concatenate([a, b], 0) for a, b in zip(*fixed)]
-    act = halves(0.5 * (256.0 * mm(same, high) + mm(same, low)))[0].astype(BF)
+    forward = jnp.concatenate([slot_rows(ref, slots, width) for ref in (first, second)], 0)
+    act = halves(0.5 * mm(same, forward.astype(F32).astype(BF)))[0].astype(BF)
     shape = (width, 128)
     mine = hot((iota(shape, 0) == block * me + iota(shape, 1)) & (iota(shape, 1) < block))
     node_cols = mm(node_w[...], mine).astype(BF)

time: 81.3 us -> 80.9 us (level)
  Pallas kernels: 30.8 us -> 29.4 us
  waiting for transfers between devices: 1.38 us -> 2.45 us
    pallas_call x9, Pallas kernels: 30.8 us -> 29.4 us  [kernel_call(): pl.pallas_call(body, name=name, out_shape=pinned, in_specs=[SMEM] * len(s...]
    all_to_all x1, waiting for transfers between devices: 0.01 us -> 1.08 us  [gather_plan(): lax.all_to_all(pair, 'lat', 0, 0, tiled=True, axis_index_groups=groups)]
  transfers between devices with their start and end apart: 4 -> 4, of which waited for: 2 -> 3; matrix products, arithmetic and copies ran while one was open for 0% -> 0% of each run, Pallas kernels for 17% -> 16%
where the time goes in v7:
time: 80.9 us; the launch traced here: 80.5 us
  blocking collectives  43.6 us (54%)
  Pallas kernels  29.4 us (36%)
  starting transfers between devices  3.72 us (5%)
  waiting for transfers between devices  2.45 us (3%)
  between operations  1.4 us (2%)
    all_to_all x2, blocking collectives, gather(): lax.all_to_all(message, 'lat', 0, 0, tiled=True, axis_index_groups=groups)  43.6 us
    pallas_call x9, Pallas kernels, kernel_call(): pl.pallas_call(body, name=name, out_shape=pinned, in_specs=[SMEM] * len(s...  29.4 us
    all_to_all x1, starting transfers between devices, gather_plan(): lax.all_to_all(pair, 'lat', 0, 0, tiled=True, axis_index_groups=groups)  3.42 us
  transfers between devices with their start and end apart: 4, of which 3 were waited for; matrix products, arithmetic and copies ran while one was open for 0% of the time, Pallas kernels for 16%

profile of v7, /device:TPU:0, one launch (start us, length us, event | category | flops | bytes accessed | tf_op | source)
XLA Modules:
  0.0 80.5 jit_solution(12308262082497531273)
XLA Ops:
  1.3 6.7 %encoder.1 = (s16[8,296,128]{2,1,0:T(8,128)(2,1)S(1)}, bf16[2048,512]{1,0:T(8,128)(2,1)}, bf16[64,512]{1,0:T(8,128)(2,1)S(1)}, bf16[64,512]{1,0:T(8,128)(2,1)S(1)}) custom-call(s32[1]{0:T(128)S(6)} %copy.22.refs_0_.count, bf16[1024,512]{1,0:T(8,128)(2,1)} %latent.1, bf16[512,512]{1,0:T(8,128)(2,1)} %refs_9_.1, bf16[320,512]{1,0:T(8,128)(2,1)} %refs_3_.1, ...), custom_call_target="tpu_custom_call" | custom-call | flops 2147483648 | bytes 4792576 | tf_op jit(solution)/shard_map/encoder/pallas_call | solution.py:684
  8.0 23.9 %all_to_all.15.refs_1_.refs_3_ = s16[8,296,128]{2,1,0:T(8,128)(2,1)S(1)} all-to-all(s16[8,296,128]{2,1,0:T(8,128)(2,1)S(1)} %get-tuple-element.46), channel_id=1, replica_groups={{0,2,4,6,8,10,12,14},{1,3,5,7,9,11,13,15},{16,18,20,22,24,26,28,30},{17..., dimensions={0} | all-to-all | bytes 1212416 | tf_op jit(solution)/shard_map/all_to_all | solution.py:730
  31.9 0.0 copy-start
  31.9 0.0 collective-permute-start
  31.9 0.0 copy-start.2
  31.9 1.5 %decoder_picks.1 = (bf16[96,3072]{1,0:T(8,128)(2,1)S(1)}, bf16[3072,128]{1,0:T(8,128)(2,1)S(1)}, bf16[512,512]{1,0:T(8,128)(2,1)S(1)}, bf16[512,512]{1,0:T(8,128)(2,1)S(1)}, f32[4,512]{1,0:T(4,128)S(1)}) custom-call(bf16[64,512]{1,0:T(8,128)(2,1)S(1)} %get-tuple-element.49.after.refs_3_, s32[3,1024]{1,0:T(4,128)} %send_any.1, f32[3,4,1024]{2,1,0:T(4,128)} %feat_any.2, ...), custom_call_target="tpu_custom_call" | custom-call | flops 2097152000 | bytes 3616768 | tf_op jit(solution)/shard_map/decoder_picks/pallas_call | solution.py:684
  33.5 0.5 collective-permute-done.refs_2_.refs_4_
  34.0 0.0 copy-start.3
  34.0 0.0 copy-done
  34.0 0.0 copy-done.2
  34.0 0.0 copy-start.5
  34.0 4.1 %decoder.1 = (bf16[8,288,128]{2,1,0:T(8,128)(2,1)S(1)}, f32[4,512]{1,0:T(4,128)S(1)}, bf16[2,64,512]{2,1,0:T(8,128)(2,1)S(1)}, f32[64,512]{1,0:T(8,128)S(1)}, f3...) custom-call(s32[1]{0:T(128)} %bitcast.refs_0_.place, ...), custom_call_target="tpu_custom_call" | custom-call | flops 1610612736 | bytes 5775360 | tf_op jit(solution)/shard_map/decoder/pallas_call | solution.py:684
  38.1 0.0 copy-done.3
  38.1 19.6 %all_to_all.16.first.refs_5_ = bf16[8,288,128]{2,1,0:T(8,128)(2,1)S(1)} all-to-all(bf16[8,288,128]{2,1,0:T(8,128)(2,1)S(1)} %get-tuple-element.56), channel_id=1, replica_groups={{0,2,4,6,8,10,12,14},{1,3,5,7,9,11,13,15},{16,18,20,22,24,26,28,30},{17..., dimensions={0} | all-to-all | bytes 1179648 | tf_op jit(solution)/shard_map/all_to_all | solution.py:730
  57.7 0.0 copy-start.1
  57.7 0.0 copy-start.6
  57.7 0.0 collective-permute-start.1
  57.7 0.0 copy-done.5
  57.7 2.1 %encoder_picks.1 = (bf16[2048,128]{1,0:T(8,128)(2,1)S(1)}, bf16[512,1024]{1,0:T(8,128)(2,1)S(1)}, bf16[512,512]{1,0:T(8,128)(2,1)S(1)}, s32[1,2048]{1,0:T(1,128)S(1)}, f32[4,2048]{1,0:T(4,128)S(1)}) custom-call(s32[1]{0:T(128)S(6)} %copy.22.refs_0_.count, bf16[1024,512]{1,0:T(8,128)(2,1)S(1)} %copy-done.5, s32[1,2048]{1,0:T(1,128)} %bitcast.15, ...), custom_call_target="tpu_custom_call" | custom-call | flops 2097152000 | bytes 4284416 | tf_op jit(solution)/shard_map/encoder_picks/pallas_call | solution.py:684
  59.8 0.0 collective-permute-done.1.second.refs_6_
  59.8 0.0 copy-start.4
  59.8 0.0 copy-done.1
  59.8 0.0 copy-done.6
  59.9 4.3 %backward.1 = (bf16[1024,512]{1,0:T(8,128)(2,1)}, bf16[1024,512]{1,0:T(8,128)(2,1)S(1)}, bf16[8,136,128]{2,1,0:T(8,128)(2,1)S(1)}, f32[8,512]{1,0:T(8,128)S(1)}) custom-call(s32[1]{0:T(128)} %bitcast.refs_0_.place, bf16[8,288,128]{2,1,0:T(8,128)(2,1)S(1)} %all_to_all.16.first.refs_5_, bf16[8,288,128]{2,1,0:T(8,128)(2,1)S(1)} %collective-permute-done.1.second.refs_6_, ...), custom_call_target="tpu_custom_call" | custom-call | flops 2147483648 | bytes 8159232 | tf_op jit(solution)/shard_map/backward/pallas_call | solution.py:684
  64.2 0.0 copy-done.4
  64.2 0.3 collective-permute-start.2
  64.5 0.4 keep.1
  65.0 0.9 %collective-permute-done.2.given = bf16[8,136,128]{2,1,0:T(8,128)(2,1)S(1)} collective-permute-done((bf16[8,136,128]{2,1,0:T(8,128)(2,1)S(1)}, bf16[8,136,128]{2,1,0:T(8,128)(2,1)S(1)}, u32[]{:S(2)}, u32[]{:S(2)}) %collective-permute-start.2) | collective-permute-done | bytes 278560 | tf_op jit(solution)/shard_map/ppermute | solution.py:866
  65.9 0.8 pair.1
  66.6 3.4 %all-to-all-start.2 = ((bf16[8,136,128]{2,1,0:T(8,128)(2,1)}), bf16[8,136,128]{2,1,0:T(8,128)(2,1)S(1)}, u32[]{:S(2)}, u32[]{:S(2)}) async-start(bf16[8,136,128]{2,1,0:T(8,128)(2,1)} %pair.1), calls=%async_computation.2 | async-start | bytes 557056 | tf_op jit(solution)/shard_map/all_to_all | solution.py:869
  70.1 8.7 %beside.1 = (bf16[320,512]{1,0:T(8,128)(2,1)}, f32[32,512]{1,0:T(8,128)}, f32[32,512]{1,0:T(8,128)}, bf16[1024,512]{1,0:T(8,128)(2,1)}) custom-call(s32[1]{0:T(128)} %bitcast.refs_0_.place, f32[4,512]{1,0:T(4,128)S(1)} %get-tuple-element.75.refs_1_, bf16[512,512]{1,0:T(8,128)(2,1)} %refs_2_.3, s16[8,296,128]{2,1,0:T(8,128)(2,1)} %copy-done, ...), custom_call_target="tpu_custom_call" | custom-call | flops 1073741824 | bytes 7577600 | tf_op jit(solution)/shard_map/beside/pallas_call | solution.py:684
  78.8 1.1 %all-to-all-done.2.refs_0_ = bf16[8,136,128]{2,1,0:T(8,128)(2,1)S(1)} async-done(((bf16[8,136,128]{2,1,0:T(8,128)(2,1)}), bf16[8,136,128]{2,1,0:T(8,128)(2,1)S(1)}, u32[]{:S(2)}, u32[]{:S(2)}) %all-to-all-start.2) | async-done | bytes 278560 | tf_op jit(solution)/shard_map/all_to_all | solution.py:869
  79.9 0.7 final.1
Async XLA Ops:
  31.9 2.0 %copy-start = (s16[8,296,128]{2,1,0:T(8,128)(2,1)}, s16[8,296,128]{2,1,0:T(8,128)(2,1)S(1)}, u32[]{:S(2)}) copy-start(s16[8,296,128]{2,1,0:T(8,128)(2,1)S(1)} %all_to_all.15.refs_1_.refs_3_) | copy-start | bytes 1818628
  31.9 2.0 %collective-permute-start = (s16[8,296,128]{2,1,0:T(8,128)(2,1)S(1)}, s16[8,296,128]{2,1,0:T(8,128)(2,1)S(1)}, u32[]{:S(2)}, u32[]{:S(2)}) collective-permute-start(s16[8,296,128]{2,1,0:T(8,128)(2,1)S(1)} %all_to_all.15.refs_1_.refs_3_), channel_id=1, source_target_pairs={{0,1},{1,0},{2,3},{3,2},{4,5},{5,4},{6,7},{7,6},{8,9},{9,8},{10,11... | collective-permute-start | bytes 1818632 | tf_op jit(solution)/shard_map/ppermute | solution.py:732
  31.9 2.0 %copy-start.2 = (bf16[1024,512]{1,0:T(8,128)(2,1)S(1)}, bf16[1024,512]{1,0:T(8,128)(2,1)}, u32[]{:S(2)}) copy-start(bf16[1024,512]{1,0:T(8,128)(2,1)} %refs_10_.3) | copy-start | bytes 3145732
  34.0 4.1 %copy-start.3 = (s16[8,296,128]{2,1,0:T(8,128)(2,1)}, s16[8,296,128]{2,1,0:T(8,128)(2,1)S(1)}, u32[]{:S(2)}) copy-start(s16[8,296,128]{2,1,0:T(8,128)(2,1)S(1)} %collective-permute-done.refs_2_.refs_4_) | copy-start | bytes 1818628
  34.0 23.8 %copy-start.5 = (bf16[1024,512]{1,0:T(8,128)(2,1)S(1)}, bf16[1024,512]{1,0:T(8,128)(2,1)}, u32[]{:S(2)}) copy-start(bf16[1024,512]{1,0:T(8,128)(2,1)} %latent.1) | copy-start | bytes 3145732
  57.7 2.1 %copy-start.1 = (bf16[8,288,128]{2,1,0:T(8,128)(2,1)}, bf16[8,288,128]{2,1,0:T(8,128)(2,1)S(1)}, u32[]{:S(2)}) copy-start(bf16[8,288,128]{2,1,0:T(8,128)(2,1)S(1)} %all_to_all.16.first.refs_5_) | copy-start | bytes 1769476
  57.7 2.2 %copy-start.6 = (bf16[2048,512]{1,0:T(8,128)(2,1)S(1)}, bf16[2048,512]{1,0:T(8,128)(2,1)}, u32[]{:S(2)}) copy-start(bf16[2048,512]{1,0:T(8,128)(2,1)} %get-tuple-element.69.slope) | copy-start | bytes 6291460
  57.7 2.1 %collective-permute-start.1 = (bf16[8,288,128]{2,1,0:T(8,128)(2,1)S(1)}, bf16[8,288,128]{2,1,0:T(8,128)(2,1)S(1)}, u32[]{:S(2)}, u32[]{:S(2)}) collective-permute-start(bf16[8,288,128]{2,1,0:T(8,128)(2,1)S(1)} %all_to_all.16.first.refs_5_), channel_id=1, source_target_pairs={{0,1},{1,0},{2,3},{3,2},{4,5},{5,4},{6,7},{7,6},{8,9},{9,8},{10,11... | collective-permute-start | bytes 1769480 | tf_op jit(solution)/shard_map/ppermute | solution.py:732
  59.8 4.4 %copy-start.4 = (bf16[8,288,128]{2,1,0:T(8,128)(2,1)}, bf16[8,288,128]{2,1,0:T(8,128)(2,1)S(1)}, u32[]{:S(2)}) copy-start(bf16[8,288,128]{2,1,0:T(8,128)(2,1)S(1)} %collective-permute-done.1.second.refs_6_) | copy-start | bytes 1769476
  64.2 1.6 %collective-permute-start.2 = (bf16[8,136,128]{2,1,0:T(8,128)(2,1)S(1)}, bf16[8,136,128]{2,1,0:T(8,128)(2,1)S(1)}, u32[]{:S(2)}, u32[]{:S(2)}) collective-permute-start(bf16[8,136,128]{2,1,0:T(8,128)(2,1)S(1)} %get-tuple-element.72), channel_id=1, source_target_pairs={{0,1},{1,0},{2,3},{3,2},{4,5},{5,4},{6,7},{7,6},{8,9},{9,8},{10,11... | collective-permute-start | bytes 835592 | tf_op jit(solution)/shard_map/ppermute | solution.py:866
  66.6 13.2 %all-to-all-start.2 = ((bf16[8,136,128]{2,1,0:T(8,128)(2,1)}), bf16[8,136,128]{2,1,0:T(8,128)(2,1)S(1)}, u32[]{:S(2)}, u32[]{:S(2)}) async-start(bf16[8,136,128]{2,1,0:T(8,128)(2,1)} %pair.1), calls=%async_computation.2 | async-start | bytes 557056 | tf_op jit(solution)/shard_map/all_to_all | solution.py:869

commit v8 on v7

--- a/solution.py
+++ b/solution.py
@@ -480,19 +480,19 @@
 ):
     slots, width = extra.shape
     keys, same, scales, latent = slot_matches(first, second, place[0], cap, mesh_rows, width)
-    agg = jnp.zeros((slots, width), F32)
+    weights, values = [], []
     for piece, ref in enumerate((first, second)):
         keys_out[piece : piece + 1, :] = keys[piece]
         same_out[piece] = same[piece]
         keys_out[2 + piece : 3 + piece, :] = scales[piece]
-        weight = (same[piece].astype(F32) * scales[piece]).astype(BF)
-        high, low = fixed_rows(ref, slots, width)
-        agg = agg + 256.0 * mm(weight, high) + mm(weight, low)
+        weight = same[piece].astype(F32) * scales[piece]
+        weights += [(256.0 * weight).astype(BF), weight.astype(BF)]
+        values += fixed_rows(ref, slots, width)
     shape = (same[0].shape[1], slots)
     chosen = hot(iota(shape, 0) == slots * lax.div(place[0], 2) + iota(shape, 1))
     mine = mm(same[0], chosen).astype(BF)
     mine_out[...] = mine
-    agg = agg + mm(mine, rest[...])
+    agg = mm(jnp.concatenate([*weights, mine], 1), jnp.concatenate([*values, rest[...]], 0))
     silu, double = halves(0.5 * agg)
     slope_out[...] = 0.25 * double
     hmesh = (latent + mm(silu.astype(BF), node_w[...])).astype(BF)

time: 80.9 us -> 80.8 us (level)
  no operation moved by 1% of the time
where the time goes in v8:
time: 80.8 us; the launch traced here: 80.4 us
  blocking collectives  43.5 us (54%)
  Pallas kernels  29.3 us (36%)
  starting transfers between devices  3.71 us (5%)
  waiting for transfers between devices  2.45 us (3%)
  between operations  1.4 us (2%)
    all_to_all x2, blocking collectives, gather(): lax.all_to_all(message, 'lat', 0, 0, tiled=True, axis_index_groups=groups)  43.5 us
    pallas_call x9, Pallas kernels, kernel_call(): pl.pallas_call(body, name=name, out_shape=pinned, in_specs=[SMEM] * len(s...  29.3 us
    all_to_all x1, starting transfers between devices, gather_plan(): lax.all_to_all(pair, 'lat', 0, 0, tiled=True, axis_index_groups=groups)  3.42 us
  transfers between devices with their start and end apart: 4, of which 3 were waited for; matrix products, arithmetic and copies ran while one was open for 0% of the time, Pallas kernels for 16%

profile of v8, /device:TPU:0, one launch (start us, length us, event | category | flops | bytes accessed | tf_op | source)
XLA Modules:
  0.0 80.4 jit_solution(11760686732092556522)
XLA Ops:
  1.3 6.7 %encoder.1 = (s16[8,296,128]{2,1,0:T(8,128)(2,1)S(1)}, bf16[2048,512]{1,0:T(8,128)(2,1)}, bf16[64,512]{1,0:T(8,128)(2,1)S(1)}, bf16[64,512]{1,0:T(8,128)(2,1)S(1)}) custom-call(s32[1]{0:T(128)S(6)} %copy.22.refs_0_.count, bf16[1024,512]{1,0:T(8,128)(2,1)} %latent.1, bf16[512,512]{1,0:T(8,128)(2,1)} %refs_9_.1, bf16[320,512]{1,0:T(8,128)(2,1)} %refs_3_.1, ...), custom_call_target="tpu_custom_call" | custom-call | flops 2147483648 | bytes 4792576 | tf_op jit(solution)/shard_map/encoder/pallas_call | solution.py:684
  8.0 23.9 %all_to_all.15.refs_1_.refs_3_ = s16[8,296,128]{2,1,0:T(8,128)(2,1)S(1)} all-to-all(s16[8,296,128]{2,1,0:T(8,128)(2,1)S(1)} %get-tuple-element.46), channel_id=1, replica_groups={{0,2,4,6,8,10,12,14},{1,3,5,7,9,11,13,15},{16,18,20,22,24,26,28,30},{17..., dimensions={0} | all-to-all | bytes 1212416 | tf_op jit(solution)/shard_map/all_to_all | solution.py:730
  31.9 0.0 copy-start
  31.9 0.0 collective-permute-start
  31.9 0.0 copy-start.2
  31.9 1.5 %decoder_picks.1 = (bf16[96,3072]{1,0:T(8,128)(2,1)S(1)}, bf16[3072,128]{1,0:T(8,128)(2,1)S(1)}, bf16[512,512]{1,0:T(8,128)(2,1)S(1)}, bf16[512,512]{1,0:T(8,128)(2,1)S(1)}, f32[4,512]{1,0:T(4,128)S(1)}) custom-call(bf16[64,512]{1,0:T(8,128)(2,1)S(1)} %get-tuple-element.49.after.refs_3_, s32[3,1024]{1,0:T(4,128)} %send_any.1, f32[3,4,1024]{2,1,0:T(4,128)} %feat_any.2, ...), custom_call_target="tpu_custom_call" | custom-call | flops 2097152000 | bytes 3616768 | tf_op jit(solution)/shard_map/decoder_picks/pallas_call | solution.py:684
  33.5 0.5 collective-permute-done.refs_2_.refs_4_
  34.0 0.0 copy-start.3
  34.0 0.0 copy-done
  34.0 0.0 copy-done.2
  34.0 0.0 copy-start.5
  34.0 4.0 %decoder.1 = (bf16[8,288,128]{2,1,0:T(8,128)(2,1)S(1)}, f32[4,512]{1,0:T(4,128)S(1)}, bf16[2,64,512]{2,1,0:T(8,128)(2,1)S(1)}, f32[64,512]{1,0:T(8,128)S(1)}, f3...) custom-call(s32[1]{0:T(128)} %bitcast.refs_0_.place, ...), custom_call_target="tpu_custom_call" | custom-call | flops 1610612736 | bytes 5775360 | tf_op jit(solution)/shard_map/decoder/pallas_call | solution.py:684
  38.0 0.0 copy-done.3
  38.0 19.6 %all_to_all.16.first.refs_5_ = bf16[8,288,128]{2,1,0:T(8,128)(2,1)S(1)} all-to-all(bf16[8,288,128]{2,1,0:T(8,128)(2,1)S(1)} %get-tuple-element.56), channel_id=1, replica_groups={{0,2,4,6,8,10,12,14},{1,3,5,7,9,11,13,15},{16,18,20,22,24,26,28,30},{17..., dimensions={0} | all-to-all | bytes 1179648 | tf_op jit(solution)/shard_map/all_to_all | solution.py:730
  57.6 0.0 copy-start.1
  57.6 0.0 copy-start.6
  57.6 0.0 collective-permute-start.1
  57.6 0.0 copy-done.5
  57.6 2.1 %encoder_picks.1 = (bf16[2048,128]{1,0:T(8,128)(2,1)S(1)}, bf16[512,1024]{1,0:T(8,128)(2,1)S(1)}, bf16[512,512]{1,0:T(8,128)(2,1)S(1)}, s32[1,2048]{1,0:T(1,128)S(1)}, f32[4,2048]{1,0:T(4,128)S(1)}) custom-call(s32[1]{0:T(128)S(6)} %copy.22.refs_0_.count, bf16[1024,512]{1,0:T(8,128)(2,1)S(1)} %copy-done.5, s32[1,2048]{1,0:T(1,128)} %bitcast.15, ...), custom_call_target="tpu_custom_call" | custom-call | flops 2097152000 | bytes 4284416 | tf_op jit(solution)/shard_map/encoder_picks/pallas_call | solution.py:684
  59.7 0.0 collective-permute-done.1.second.refs_6_
  59.7 0.0 copy-start.4
  59.7 0.0 copy-done.1
  59.8 0.0 copy-done.6
  59.8 4.3 %backward.1 = (bf16[1024,512]{1,0:T(8,128)(2,1)}, bf16[1024,512]{1,0:T(8,128)(2,1)S(1)}, bf16[8,136,128]{2,1,0:T(8,128)(2,1)S(1)}, f32[8,512]{1,0:T(8,128)S(1)}) custom-call(s32[1]{0:T(128)} %bitcast.refs_0_.place, bf16[8,288,128]{2,1,0:T(8,128)(2,1)S(1)} %all_to_all.16.first.refs_5_, bf16[8,288,128]{2,1,0:T(8,128)(2,1)S(1)} %collective-permute-done.1.second.refs_6_, ...), custom_call_target="tpu_custom_call" | custom-call | flops 2147483648 | bytes 8159232 | tf_op jit(solution)/shard_map/backward/pallas_call | solution.py:684
  64.1 0.0 copy-done.4
  64.1 0.3 collective-permute-start.2
  64.4 0.4 keep.1
  64.9 0.9 %collective-permute-done.2.given = bf16[8,136,128]{2,1,0:T(8,128)(2,1)S(1)} collective-permute-done((bf16[8,136,128]{2,1,0:T(8,128)(2,1)S(1)}, bf16[8,136,128]{2,1,0:T(8,128)(2,1)S(1)}, u32[]{:S(2)}, u32[]{:S(2)}) %collective-permute-start.2) | collective-permute-done | bytes 278560 | tf_op jit(solution)/shard_map/ppermute | solution.py:866
  65.8 0.8 pair.1
  66.5 3.4 %all-to-all-start.2 = ((bf16[8,136,128]{2,1,0:T(8,128)(2,1)}), bf16[8,136,128]{2,1,0:T(8,128)(2,1)S(1)}, u32[]{:S(2)}, u32[]{:S(2)}) async-start(bf16[8,136,128]{2,1,0:T(8,128)(2,1)} %pair.1), calls=%async_computation.2 | async-start | bytes 557056 | tf_op jit(solution)/shard_map/all_to_all | solution.py:869
  70.0 8.7 %beside.1 = (bf16[320,512]{1,0:T(8,128)(2,1)}, f32[32,512]{1,0:T(8,128)}, f32[32,512]{1,0:T(8,128)}, bf16[1024,512]{1,0:T(8,128)(2,1)}) custom-call(s32[1]{0:T(128)} %bitcast.refs_0_.place, f32[4,512]{1,0:T(4,128)S(1)} %get-tuple-element.75.refs_1_, bf16[512,512]{1,0:T(8,128)(2,1)} %refs_2_.3, s16[8,296,128]{2,1,0:T(8,128)(2,1)} %copy-done, ...), custom_call_target="tpu_custom_call" | custom-call | flops 1073741824 | bytes 7577600 | tf_op jit(solution)/shard_map/beside/pallas_call | solution.py:684
  78.7 1.1 %all-to-all-done.2.refs_0_ = bf16[8,136,128]{2,1,0:T(8,128)(2,1)S(1)} async-done(((bf16[8,136,128]{2,1,0:T(8,128)(2,1)}), bf16[8,136,128]{2,1,0:T(8,128)(2,1)S(1)}, u32[]{:S(2)}, u32[]{:S(2)}) %all-to-all-start.2) | async-done | bytes 278560 | tf_op jit(solution)/shard_map/all_to_all | solution.py:869
  79.8 0.7 final.1
Async XLA Ops:
  31.9 2.0 %copy-start = (s16[8,296,128]{2,1,0:T(8,128)(2,1)}, s16[8,296,128]{2,1,0:T(8,128)(2,1)S(1)}, u32[]{:S(2)}) copy-start(s16[8,296,128]{2,1,0:T(8,128)(2,1)S(1)} %all_to_all.15.refs_1_.refs_3_) | copy-start | bytes 1818628
  31.9 2.0 %collective-permute-start = (s16[8,296,128]{2,1,0:T(8,128)(2,1)S(1)}, s16[8,296,128]{2,1,0:T(8,128)(2,1)S(1)}, u32[]{:S(2)}, u32[]{:S(2)}) collective-permute-start(s16[8,296,128]{2,1,0:T(8,128)(2,1)S(1)} %all_to_all.15.refs_1_.refs_3_), channel_id=1, source_target_pairs={{0,1},{1,0},{2,3},{3,2},{4,5},{5,4},{6,7},{7,6},{8,9},{9,8},{10,11... | collective-permute-start | bytes 1818632 | tf_op jit(solution)/shard_map/ppermute | solution.py:732
  31.9 2.0 %copy-start.2 = (bf16[1024,512]{1,0:T(8,128)(2,1)S(1)}, bf16[1024,512]{1,0:T(8,128)(2,1)}, u32[]{:S(2)}) copy-start(bf16[1024,512]{1,0:T(8,128)(2,1)} %refs_10_.3) | copy-start | bytes 3145732
  34.0 4.0 %copy-start.3 = (s16[8,296,128]{2,1,0:T(8,128)(2,1)}, s16[8,296,128]{2,1,0:T(8,128)(2,1)S(1)}, u32[]{:S(2)}) copy-start(s16[8,296,128]{2,1,0:T(8,128)(2,1)S(1)} %collective-permute-done.refs_2_.refs_4_) | copy-start | bytes 1818628
  34.0 23.7 %copy-start.5 = (bf16[1024,512]{1,0:T(8,128)(2,1)S(1)}, bf16[1024,512]{1,0:T(8,128)(2,1)}, u32[]{:S(2)}) copy-start(bf16[1024,512]{1,0:T(8,128)(2,1)} %latent.1) | copy-start | bytes 3145732
  57.6 2.1 %copy-start.1 = (bf16[8,288,128]{2,1,0:T(8,128)(2,1)}, bf16[8,288,128]{2,1,0:T(8,128)(2,1)S(1)}, u32[]{:S(2)}) copy-start(bf16[8,288,128]{2,1,0:T(8,128)(2,1)S(1)} %all_to_all.16.first.refs_5_) | copy-start | bytes 1769476
  57.6 2.2 %copy-start.6 = (bf16[2048,512]{1,0:T(8,128)(2,1)S(1)}, bf16[2048,512]{1,0:T(8,128)(2,1)}, u32[]{:S(2)}) copy-start(bf16[2048,512]{1,0:T(8,128)(2,1)} %get-tuple-element.69.slope) | copy-start | bytes 6291460
  57.6 2.1 %collective-permute-start.1 = (bf16[8,288,128]{2,1,0:T(8,128)(2,1)S(1)}, bf16[8,288,128]{2,1,0:T(8,128)(2,1)S(1)}, u32[]{:S(2)}, u32[]{:S(2)}) collective-permute-start(bf16[8,288,128]{2,1,0:T(8,128)(2,1)S(1)} %all_to_all.16.first.refs_5_), channel_id=1, source_target_pairs={{0,1},{1,0},{2,3},{3,2},{4,5},{5,4},{6,7},{7,6},{8,9},{9,8},{10,11... | collective-permute-start | bytes 1769480 | tf_op jit(solution)/shard_map/ppermute | solution.py:732
  59.7 4.4 %copy-start.4 = (bf16[8,288,128]{2,1,0:T(8,128)(2,1)}, bf16[8,288,128]{2,1,0:T(8,128)(2,1)S(1)}, u32[]{:S(2)}) copy-start(bf16[8,288,128]{2,1,0:T(8,128)(2,1)S(1)} %collective-permute-done.1.second.refs_6_) | copy-start | bytes 1769476
  64.1 1.6 %collective-permute-start.2 = (bf16[8,136,128]{2,1,0:T(8,128)(2,1)S(1)}, bf16[8,136,128]{2,1,0:T(8,128)(2,1)S(1)}, u32[]{:S(2)}, u32[]{:S(2)}) collective-permute-start(bf16[8,136,128]{2,1,0:T(8,128)(2,1)S(1)} %get-tuple-element.72), channel_id=1, source_target_pairs={{0,1},{1,0},{2,3},{3,2},{4,5},{5,4},{6,7},{7,6},{8,9},{9,8},{10,11... | collective-permute-start | bytes 835592 | tf_op jit(solution)/shard_map/ppermute | solution.py:866
  66.5 13.2 %all-to-all-start.2 = ((bf16[8,136,128]{2,1,0:T(8,128)(2,1)}), bf16[8,136,128]{2,1,0:T(8,128)(2,1)S(1)}, u32[]{:S(2)}, u32[]{:S(2)}) async-start(bf16[8,136,128]{2,1,0:T(8,128)(2,1)} %pair.1), calls=%async_computation.2 | async-start | bytes 557056 | tf_op jit(solution)/shard_map/all_to_all | solution.py:869
